TPU v7x, 128 devices: a whole 4x4x4 slice. The times are simulated.
128 devices in a mesh: chan: 8 (over z, core), tile: 16 (over x, y).
Axes of the slice: x: 4, y: 4, z: 4, core: 2. Of those that a mesh axis runs over, the one named last changes fastest.
Arguments:
- voltages: bfloat16 [2, 1024, 65536], P(None, 'tile', 'chan'), may hold values from -20 to 20
- flags: int32 [1024], replicated, may hold values 0 or 1
Outputs:
- visibilities: bfloat16 [2, 256, 1024, 1024], P(None, 'chan', 'tile')
- gains: float32 [2, 256, 1024], P(None, 'chan', 'tile')
All inputs are finite; a program needn't handle non-finite values.
Results may differ from a plain program's by a relative error of at most 0.0069.
Values may be sent and summed in bfloat16 or wider, within the bound.
No kernel may reach another device: no remote copies, remote signals or barrier semaphores. Data moves between devices by JAX's collectives and lax.ppermute only.
A program may use at most 192 MiB of HBM per device.

v0:
```python
import math

import jax
import jax.numpy as jnp
from jax import lax
from jax.sharding import PartitionSpec as P

NCH = 256
TAPS = 16
ITERS = 3


def shifted(value, axis, steps):
    count = lax.axis_size(axis)
    first, last = (max(0, -steps), min(count, count - steps))
    return lax.ppermute(value, axis, [(source, source + steps) for source in range(first, last)])


def taps_table(taps, channels):
    length = taps * channels
    index = jnp.arange(length, dtype=jnp.float32)
    centre = (length - 1) / 2.0
    shaped = jnp.sinc((index - centre) / channels)
    window = 0.5 - 0.5 * jnp.cos(2.0 * math.pi * (index + 0.5) / length)
    values = shaped * window
    values = values * jnp.sqrt(channels / jnp.sum(values * values))
    return values.reshape(taps, channels)


def dft_table(channels):
    index = jnp.arange(channels, dtype=jnp.int32)
    product = index[:, None] * index[None, :] % channels
    angle = 2.0 * math.pi / channels * product.astype(jnp.float32)
    scale = 1.0 / math.sqrt(channels)
    cosine = jnp.cos(angle) * scale
    sine = jnp.sin(angle) * scale
    upper = jnp.stack([cosine, -sine], axis=1)
    lower = jnp.stack([sine, cosine], axis=1)
    return jnp.concatenate([upper, lower], axis=0).astype(jnp.bfloat16)


def rows_times(matrix, vector):
    return jnp.einsum(
        "cpq,cq->cp",
        matrix,
        vector,
        precision=lax.Precision.HIGHEST,
        preferred_element_type=jnp.float32,
    )


def body(voltages, flags):
    row_count = voltages.shape[1]
    frame_count = voltages.shape[2] // NCH
    frames = voltages.reshape(2, row_count, frame_count, NCH)
    history = shifted(frames[:, :, frame_count - (TAPS - 1) :, :], "chan", 1)
    extended = jnp.concatenate([history, frames], axis=2)
    coefficients = taps_table(TAPS, NCH)
    filtered = coefficients[0] * extended[:, :, 0:frame_count, :]
    for step in range(1, TAPS):
        filtered = filtered + coefficients[step] * extended[:, :, step : step + frame_count, :]
    filtered = filtered.astype(jnp.bfloat16)
    joined = jnp.concatenate([filtered[0], filtered[1]], axis=-1)
    spectra = jnp.einsum(
        "imj,jrk->kirm", joined, dft_table(NCH), preferred_element_type=jnp.float32
    ).astype(jnp.bfloat16)
    turned = lax.all_to_all(spectra, "chan", split_axis=0, concat_axis=3, tiled=True)
    chan_count = turned.shape[0]
    samples = turned.shape[3]
    own_series = turned.reshape(chan_count, row_count, 2 * samples)
    rotated = jnp.concatenate([own_series[..., samples:], -own_series[..., :samples]], axis=-1)
    row_pair = jnp.stack([own_series, rotated], axis=0)
    inverse = 1.0 / samples
    position = lax.axis_index("tile")
    sums = (
        jnp.einsum(
            "rcit,cjt->rcij",
            row_pair,
            lax.all_gather(own_series, "tile", axis=1, tiled=True),
            preferred_element_type=jnp.float32,
        )
        * inverse
    )
    visibilities = sums.astype(jnp.bfloat16)
    keep = (1 - flags).astype(jnp.float32)
    input_count = keep.shape[0]
    row_start = position * row_count
    keep_own = lax.dynamic_slice_in_dim(keep, row_start, row_count, 0)
    square = lax.dynamic_slice_in_dim(sums, row_start, row_count, 3)
    diagonal = jnp.diagonal(square, axis1=2, axis2=3)
    gains_full = jnp.stack(
        [
            jnp.broadcast_to(keep, (chan_count, input_count)),
            jnp.zeros((chan_count, input_count), jnp.float32),
        ]
    )
    gains_own = jnp.stack(
        [
            jnp.broadcast_to(keep_own, (chan_count, row_count)),
            jnp.zeros((chan_count, row_count), jnp.float32),
        ]
    )
    for step in range(ITERS):
        total = jnp.sum(gains_full * gains_full, axis=(0, 2))
        num_real = (
            rows_times(sums[0], gains_full[0])
            - rows_times(sums[1], gains_full[1])
            - (diagonal[0] * gains_own[0] - diagonal[1] * gains_own[1])
        )
        num_imag = (
            rows_times(sums[0], gains_full[1])
            + rows_times(sums[1], gains_full[0])
            - (diagonal[0] * gains_own[1] + diagonal[1] * gains_own[0])
        )
        denominator = total[:, None] - (gains_own[0] * gains_own[0] + gains_own[1] * gains_own[1])
        updated = jnp.stack([num_real, num_imag]) * keep_own / denominator
        if step % 2 == 1:
            updated = 0.5 * (updated + gains_own)
        gains_own = updated
        if step + 1 < ITERS:
            gains_full = lax.all_gather(gains_own, "tile", axis=2, tiled=True)
    return (visibilities, gains_own)


def solution(mesh):
    in_specs = (P(None, "tile", "chan"), P())
    out_specs = (P(None, "chan", "tile", None), P(None, "chan", "tile"))
    return jax.shard_map(body, mesh=mesh, in_specs=in_specs, out_specs=out_specs, check_vma=False)
```

profile of v0, /device:TPU:6, one launch (start us, length us, event | category | flops | bytes accessed | tf_op | source)
XLA Modules:
  0.0 443.0 jit_solution(18212678889593385601)
XLA Ops:
  7.2 2.0 copy.114
  9.3 2.7 collective-permute-start
  12.0 0.7 multiply_reduce_fusion.3
  13.5 1.0 fusion.43
  14.5 1.1 negate_convert_fusion
  15.7 1.3 constant_dynamic-update-slice_fusion.1
  17.3 8.5 %add_convert_fusion = bf16[2,64,32,256]{3,1,2,0:T(8,128)(2,1)S(1)} fusion(bf16[2,64,47,256]{3,1,2,0:T(8,128)(2,1)S(1)} %constant_dynamic-update-slice_fusion, f32[256]{0:T(256)S(1)} %get-tuple-element.41, f32[256]{0:T(256)S(1)} %get-tuple-element.42, f32[256]{0:T(256)S(1)} %get-tuple-element.43, f32[256]{0:T(256)S(1)} %get-tuple-element.44, ...), kind=kLoop, calls=%fused_computation.35 | loop fusion | flops 50331648 | bytes 35667968 | tf_op jit(solution)/shard_map/convert_element_type | solution.py:62
  26.0 1.3 convert_bitcast_fusion
  27.3 6.6 %copy.38 = bf16[256,64,2,32]{1,3,2,0:T(8,128)(2,1)} copy(bf16[256,64,2,32]{0,1,3,2:T(8,128)(2,1)S(1)} %convert_bitcast_fusion) | data formatting | bytes 4194304 | tf_op jit(solution)/shard_map/convert_element_type | solution.py:66
  34.0 6.4 %reshape.213 = bf16[8,2,65536]{2,1,0:T(2,128)(2,1)S(1)} reshape(bf16[256,2,32,64]{3,2,1,0:T(8,128)(2,1)} %bitcast.198) | data formatting | bytes 4194304
  40.3 42.1 %all_to_all.15 = bf16[8,2,65536]{2,1,0:T(2,128)(2,1)} all-to-all(bf16[8,2,65536]{2,1,0:T(2,128)(2,1)S(1)} %reshape.213), channel_id=1, replica_groups=mesh['chan'=8,'tile'=16] {'chan'}, dimensions={0} | all-to-all | bytes 4194304 | tf_op jit(solution)/shard_map/all_to_all | solution.py:67
  82.4 7.4 %reshape.214 = bf16[256,2,32,64]{3,2,1,0:T(8,128)(2,1)} reshape(bf16[8,2,65536]{2,1,0:T(2,128)(2,1)} %all_to_all.15) | data formatting | bytes 4194304
  89.8 5.3 %copy.39 = bf16[32,64,2,8,32]{1,4,3,2,0:T(8,128)(2,1)} copy(bf16[32,64,2,8,32]{1,4,2,0,3:T(8,128)(2,1)} %bitcast.199) | data formatting | bytes 4194304 | tf_op jit(solution)/shard_map/all_to_all | solution.py:67
  95.1 4.8 %copy.40 = bf16[32,64,512]{2,1,0:T(8,128)(2,1)} copy(bf16[32,64,512]{1,2,0:T(8,128)(2,1)} %bitcast.193) | data formatting | bytes 4194304 | tf_op jit(solution)/shard_map/reshape | solution.py:70
  100.2 4.9 %copy.44 = bf16[1,32,64,512]{3,2,0,1:T(8,128)(2,1)} copy(bf16[1,32,64,512]{2,3,1,0:T(8,128)(2,1)} %bitcast.194) | data formatting | bytes 4194304 | tf_op jit(solution)/shard_map/stack;reshape | solution.py:72
  105.3 1.5 maximum_bitcast_fusion.2
  106.9 189.5 %all-gather.2.cloned.1.call-done = bf16[32,1024,512]{2,1,0:T(8,128)(2,1)} async-done(((bf16[32,64,512]{2,1,0:T(8,128)(2,1)}), bf16[32,1024,512]{2,1,0:T(8,128)(2,1)}) %all-gather.2.cloned.1.call-update) | async-done | bytes 33554448 | tf_op jit(solution)/shard_map/all_gather | solution.py:79
  296.4 23.0 %bitcast_convert_fusion = (bf16[2,32,64,1024]{3,2,0,1:T(8,128)(2,1)}, f32[32,1024,2,64]{1,3,2,0:T(8,128)}) fusion(bf16[1,32,64,512]{3,2,0,1:T(8,128)(2,1)} %maximum_bitcast_fusion.2, bf16[1,32,64,512]{3,2,0,1:T(8,128)(2,1)S(1)} %copy-done.3, bf16[32,1024,512]{2,1,0:T(8,128)(2,1)} %all-gather.2.cloned.1.call-done), kind=kOutput, calls=%fused_computation.160 | convolution fusion | flops 4311744512 | bytes 62914560 | tf_op jit(solution)/shard_map/rcit,cjt->rcij/dot_general | solution.py:76
  319.4 2.2 dynamic-slice_bitcast_fusion
  321.6 9.5 %fusion.19 = f32[32,1,64]{2,1,0:T(1,128)S(1)} fusion(f32[2,32,64,1024]{3,2,0,1:T(8,128)} %bitcast.187, f32[1024]{0:T(1024)S(1)} %subtract_convert_fusion), kind=kOutput, calls=%fused_computation.26 | convolution fusion | flops 25165824 | bytes 8400896 | tf_op jit(solution)/shard_map/cpq,cq->cp/dot_general | solution.py:43
  331.1 9.6 %fusion.9 = f32[32,1,64]{2,1,0:T(1,128)S(1)} fusion(f32[2,32,64,1024]{3,2,0,1:T(8,128)} %bitcast.188, f32[1024]{0:T(1024)S(1)} %subtract_convert_fusion), kind=kOutput, calls=%fused_computation.12 | convolution fusion | flops 25165824 | bytes 8400896 | tf_op jit(solution)/shard_map/cpq,cq->cp/dot_general | solution.py:43
  340.8 7.1 %fusion.11 = f32[32,1,64]{2,1,0:T(1,128)S(1)} fusion(f32[2,32,64,1024]{3,2,0,1:T(8,128)S(1)} %bitcast.191), kind=kOutput, calls=%fused_computation.14 | convolution fusion | flops 25165824 | bytes 8396800 | tf_op jit(solution)/shard_map/cpq,cq->cp/dot_general | solution.py:43
  347.9 7.4 %fusion.17 = f32[32,1,64]{2,1,0:T(1,128)S(1)} fusion(f32[2,32,64,1024]{3,2,0,1:T(8,128)S(1)} %bitcast.192), kind=kOutput, calls=%fused_computation.24 | convolution fusion | flops 25165824 | bytes 8396800 | tf_op jit(solution)/shard_map/cpq,cq->cp/dot_general | solution.py:43
  355.2 4.5 %copy.45 = f32[2,32,64,64]{1,0,3,2:T(2,128)} copy(f32[2,32,64,64]{3,2,0,1:T(8,128)S(1)} %dynamic-slice_bitcast_fusion) | data formatting | bytes 2097152 | tf_op jit(solution)/shard_map/dynamic_slice | solution.py:89
  359.7 2.9 gather_fusion
  363.2 22.6 %all_gather.10 = f32[2,32,1024]{1,2,0:T(8,128)S(1)} all-gather(f32[2,32,64]{1,2,0:T(8,128)S(1)} %fusion.44), channel_id=1, replica_groups=mesh['chan'=8,'tile'=16] {'tile'}, dimensions={2}, use_global_device_ids=true | all-gather | bytes 278528 | tf_op jit(solution)/shard_map/all_gather | solution.py:121
  385.9 0.3 multiply_reduce_fusion.1
  386.6 7.2 %fusion.5 = (f32[32,64]{1,0:T(8,128)S(1)}, f32[32,64]{1,0:T(8,128)S(1)}, f32[32,64]{1,0:T(8,128)S(1)}, f32[32,64]{1,0:T(8,128)S(1)}) fusion(f32[2,32,64,1024]{3,2,0,1:T(8,128)} %bitcast.189, f32[32,1024]{1,0:T(8,128)S(1)} %copy.105, f32[32,1024]{1,0:T(8,128)S(1)} %copy.104), kind=kLoop, calls=%fused_computation.8 | loop fusion | flops 16769024 | bytes 17072128
  394.2 23.9 %all_gather.11 = f32[2,32,1024]{1,2,0:T(8,128)S(1)} all-gather(f32[2,32,64]{1,2,0:T(8,128)S(1)} %fusion.47), channel_id=1, replica_groups=mesh['chan'=8,'tile'=16] {'tile'}, dimensions={2}, use_global_device_ids=true | all-gather | bytes 278528 | tf_op jit(solution)/shard_map/all_gather | solution.py:121
  418.8 7.2 %fusion.7 = (f32[32,64]{1,0:T(8,128)S(1)}, f32[32,64]{1,0:T(8,128)S(1)}, f32[32,64]{1,0:T(8,128)S(1)}, f32[32,64]{1,0:T(8,128)S(1)}) fusion(f32[2,32,64,1024]{3,2,0,1:T(8,128)} %bitcast.190, f32[32,1024]{1,0:T(8,128)S(1)} %copy.107, f32[32,1024]{1,0:T(8,128)S(1)} %copy.106), kind=kLoop, calls=%fused_computation.10 | loop fusion | flops 16769024 | bytes 17072128
  426.4 0.7 copy.48
  427.1 8.6 %copy.47 = bf16[2,32,64,1024]{3,2,1,0:T(8,128)(2,1)} copy(bf16[2,32,64,1024]{3,2,0,1:T(8,128)(2,1)} %get-tuple-element.56) | data formatting | bytes 16777216
  (53 shorter events, 3.7 us)
Async XLA Ops:
  7.2 289.2 %all-gather.2.cloned.1.call-start = ((), (), s32[]{:S(2)}) async-start(), calls=%async_computation.1 | async-start | bytes 35651584 | tf_op jit(solution)/shard_map/all_gather | solution.py:79
  7.2 9.8 %copy-start.1 = (bf16[2,64,8192]{2,1,0:T(8,128)(2,1)S(1)}, bf16[2,64,8192]{2,1,0:T(8,128)(2,1)}, u32[]{:S(2)}) copy-start(bf16[2,64,8192]{2,1,0:T(8,128)(2,1)} %param.2) | copy-start | bytes 6291460
  9.3 6.4 %collective-permute-start = (bf16[2,64,15,256]{3,1,2,0:T(8,128)(2,1)S(1)}, bf16[2,64,15,256]{3,1,2,0:T(8,128)(2,1)}, u32[]{:S(2)}, u32[]{:S(2)}) collective-permute-start(bf16[2,64,15,256]{3,1,2,0:T(8,128)(2,1)S(1)} %slice.247), channel_id=1, source_target_pairs={{0,16},{16,32},{32,48},{48,64},{64,80},{80,96},{96,112},{1,17},{17... | collective-permute-start | bytes 2949128 | tf_op jit(solution)/shard_map/ppermute | solution.py:16
  95.1 4.8 %copy-start.4 = (s32[1024]{0:T(1024)S(1)}, s32[1024]{0:T(1024)}, u32[]{:S(2)}) copy-start(s32[1024]{0:T(1024)} %param.3) | copy-start | bytes 12292
  99.9 5.3 %copy-start.2 = (bf16[32,64,512]{2,1,0:T(8,128)(2,1)S(1)}, bf16[32,64,512]{2,1,0:T(8,128)(2,1)}, u32[]{:S(2)}) copy-start(bf16[32,64,512]{2,1,0:T(8,128)(2,1)} %copy.40) | copy-start | bytes 6291460
  105.3 191.1 %copy-start.3 = (bf16[1,32,64,512]{3,2,0,1:T(8,128)(2,1)S(1)}, bf16[1,32,64,512]{3,2,0,1:T(8,128)(2,1)}, u32[]{:S(2)}) copy-start(bf16[1,32,64,512]{3,2,0,1:T(8,128)(2,1)} %copy.44) | copy-start | bytes 6291460
  321.6 19.1 %copy-start = (f32[32,1024,2,64]{1,3,2,0:T(8,128)S(1)}, f32[32,1024,2,64]{1,3,2,0:T(8,128)}, u32[]{:S(2)}) copy-start(f32[32,1024,2,64]{1,3,2,0:T(8,128)} %get-tuple-element.57) | copy-start | bytes 50331652
Sparse Core Ops, SparseCore 0:
  100.0 196.3 all-gather.1
where the time goes:
time: 450 us; the launch traced here: 443 us
  waiting for transfers between devices  190 us (42%)
  blocking collectives  88.6 us (20%)
  local copies, waits for them, and re-layouts  60.1 us (13%)
  matrix products  57.9 us (13%)
  other arithmetic  28.7 us (6%)
  between operations  15.5 us (3%)
    all_gather x1, waiting for transfers between devices, body(): lax.all_gather(own_series, 'tile', axis=1, tiled=True)  190 us
    all_gather x2, blocking collectives, body(): gains_full = lax.all_gather(gains_own, 'tile', axis=2, tiled=True)  46.6 us
    all_to_all x1, blocking collectives, body(): lax.all_to_all(spectra, 'chan', split_axis=0, concat_axis=3, tiled=True)  42.1 us
    dot_general x4, matrix products, rows_times(): jnp.einsum('cpq,cq->cp', matrix, vector, precision=lax.Precision.HIGHEST,...  33.6 us
    unnamed x19, local copies, waits for them, and re-layouts  25 us
    dot_general x1, matrix products, body(): jnp.einsum('rcit,cjt->rcij', row_pair, lax.all_gather(own_series, 'tile',...  23 us
    unnamed x2, other arithmetic  14.3 us
  transfers between devices with their start and end apart: 2, of which 1 were waited for; matrix products, arithmetic and copies ran while one was open for 2% of the time, Pallas kernels for 0%

commit v1 on v0

v1 whole, which is shorter than its diff:
```python
import functools
import math

import jax
import jax.numpy as jnp
import numpy as np
from jax import lax
from jax.experimental import pallas as pl
from jax.experimental.pallas import tpu as pltpu
from jax.sharding import PartitionSpec as P

NCH = 256
TAPS = 16
ITERS = 3
VMEM = 56 * 1024 * 1024


def taps_table():
    length = TAPS * NCH
    index = np.arange(length, dtype=np.float64)
    centre = (length - 1) / 2.0
    window = 0.5 - 0.5 * np.cos(2.0 * math.pi * (index + 0.5) / length)
    values = np.sinc((index - centre) / NCH) * window
    values = values * np.sqrt(NCH / np.sum(values * values))
    return values.reshape(TAPS, NCH).astype(np.float32)


def dft_table():
    index = np.arange(NCH)
    angle = (2.0 * math.pi / NCH) * (index[:, None] * index[None, :] % NCH)
    scale = 1.0 / math.sqrt(NCH)
    cosine = np.cos(angle) * scale
    sine = np.sin(angle) * scale
    real = np.concatenate([cosine, sine], axis=1)
    imag = np.concatenate([-sine, cosine], axis=1)
    return np.stack([real, imag], axis=1).reshape(2 * NCH, 2 * NCH).astype(np.float32)


def spectra_kernel(v_ref, h_ref, taps_ref, table_ref, out_ref, x_ref, wide_ref):
    history = TAPS - 1
    frames = v_ref.shape[2] // NCH

    def filter_tile(index, _):
        part = index // 8
        rows = pl.multiple_of((index // 2) % 4 * 16, 16)
        lane = pl.multiple_of(index % 2 * 128, 128)
        taps = [taps_ref[pl.ds(t, 1), pl.ds(lane, 128)] for t in range(TAPS)]
        window = []
        for f in range(history + frames):
            if f < history:
                tile = h_ref[part, pl.ds(rows, 16), pl.ds(lane + f * NCH, 128)]
            else:
                tile = v_ref[part, pl.ds(rows, 16), pl.ds(lane + (f - history) * NCH, 128)]
            window.append(tile.astype(jnp.float32))
            if f < history:
                continue
            m = f - history
            total = taps[0] * window[m]
            for t in range(1, TAPS):
                total = total + taps[t] * window[m + t]
            x_ref[pl.ds(rows + m * 64, 16), pl.ds(part * NCH + lane, 128)] = total.astype(jnp.bfloat16)
        return 0

    lax.fori_loop(0, 16, filter_tile, 0)

    pairs = frames // 2
    for block in range(pairs // 2):
        spectra = lax.dot_general(
            table_ref[...],
            x_ref[pl.ds(block * 256, 256), :],
            (((1,), (1,)), ((), ())),
            preferred_element_type=jnp.float32,
        )
        for half in range(2):
            wide_ref[pl.ds(block * 2 + half, 2 * NCH, stride=pairs), :] = spectra[:, half * 128 : half * 128 + 128]

    def narrow(index, _):
        rows = pl.multiple_of(index * 64, 64)
        tile = wide_ref[pl.ds(pl.multiple_of(index * 64 * pairs, 64), 64 * pairs), :]
        out_ref[pl.ds(rows, 64)] = tile.astype(jnp.bfloat16).reshape(64, pairs, 128)
        return 0

    lax.fori_loop(0, 2 * NCH // 64, narrow, 0)


def real_kernel(recv_ref, series_ref, across_ref, vis_ref):
    @pl.when(pl.program_id(1) == 0)
    def _():
        times = recv_ref.shape[0] * recv_ref.shape[4]
        for part in range(2):
            for pair in range(8):
                first = recv_ref[:, 2 * pair, 0, part].reshape(times, 128)
                second = recv_ref[:, 2 * pair + 1, 0, part].reshape(times, 128)
                low = jnp.concatenate([first[:, :64], second[:, :64]], axis=1)
                high = jnp.concatenate([first[:, 64:], second[:, 64:]], axis=1)
                start = part * 2 * times
                lanes = slice(pair * 128, pair * 128 + 128)
                series_ref[0, start : start + times, lanes] = low
                series_ref[0, start + times : start + 2 * times, lanes] = high
                across_ref[0, lanes, start : start + times] = low.T
                across_ref[0, lanes, start + times : start + 2 * times] = high.T

    tiles, _, rows, inputs = vis_ref.shape
    count = tiles * rows
    left = across_ref[0, pl.ds(pl.multiple_of(pl.program_id(1) * count, count), count), :]
    sums = jnp.dot(left, series_ref[0], preferred_element_type=jnp.float32)
    sums = sums * (2.0 / series_ref.shape[1])
    vis_ref[:, 0] = sums.astype(jnp.bfloat16).reshape(tiles, rows, inputs)


def imag_kernel(series_ref, across_ref, vis_ref):
    tiles, _, rows, inputs = vis_ref.shape
    half = series_ref.shape[1] // 2
    left = jnp.concatenate([across_ref[0, :, half:], -across_ref[0, :, :half]], axis=1)
    sums = jnp.dot(left, series_ref[0], preferred_element_type=jnp.float32)
    sums = sums * (1.0 / half)
    vis_ref[:, 0] = sums.astype(jnp.bfloat16).reshape(tiles, rows, inputs)


def gains_kernel(series_ref, flags_ref, out_ref):
    half = series_ref.shape[1] // 2
    step_rows = 32
    steps = half // step_rows
    inverse = 1.0 / half
    keep = (1 - flags_ref[...]).astype(jnp.float32)

    def load(step):
        start = pl.multiple_of(step * step_rows, step_rows)
        real = series_ref[0, pl.ds(start, step_rows), :].astype(jnp.float32)
        imag = series_ref[0, pl.ds(half + start, step_rows), :].astype(jnp.float32)
        return real, imag

    def fold(value):
        total = value[0:8]
        for row in range(8, step_rows, 8):
            total = total + value[row : row + 8]
        return total

    zeros = jnp.zeros((8, keep.shape[1]), jnp.float32)

    def diagonal_step(step, carry):
        real, imag = load(step)
        return (
            carry[0] + fold(real * real + imag * imag),
            carry[1] + fold(imag * real - real * imag),
        )

    diag = lax.fori_loop(0, steps, diagonal_step, (zeros, zeros))
    diag_real = jnp.sum(diag[0], axis=0, keepdims=True) * inverse
    diag_imag = jnp.sum(diag[1], axis=0, keepdims=True) * inverse

    gain_real = keep
    gain_imag = jnp.zeros_like(keep)
    for iteration in range(ITERS):

        def times_step(step, carry, gain_real=gain_real, gain_imag=gain_imag):
            real, imag = load(step)
            mix_real = jnp.sum(real * gain_real + imag * gain_imag, axis=1, keepdims=True)
            mix_imag = jnp.sum(real * gain_imag - imag * gain_real, axis=1, keepdims=True)
            return (
                carry[0] + fold(real * mix_real - imag * mix_imag),
                carry[1] + fold(real * mix_imag + imag * mix_real),
            )

        sums = lax.fori_loop(0, steps, times_step, (zeros, zeros))
        num_real = jnp.sum(sums[0], axis=0, keepdims=True) * inverse
        num_imag = jnp.sum(sums[1], axis=0, keepdims=True) * inverse
        num_real = num_real - (diag_real * gain_real - diag_imag * gain_imag)
        num_imag = num_imag - (diag_real * gain_imag + diag_imag * gain_real)
        power = gain_real * gain_real + gain_imag * gain_imag
        denominator = jnp.sum(power, axis=1, keepdims=True) - power
        new_real = keep * num_real / denominator
        new_imag = keep * num_imag / denominator
        if iteration % 2 == 1:
            new_real = 0.5 * (new_real + gain_real)
            new_imag = 0.5 * (new_imag + gain_imag)
        gain_real, gain_imag = new_real, new_imag
    out_ref[0, 0:1, :] = gain_real
    out_ref[0, 1:2, :] = gain_imag


def params():
    return pltpu.CompilerParams(vmem_limit_bytes=VMEM)


def body(voltages, flags):
    row_count = voltages.shape[1]
    frame_count = voltages.shape[2] // NCH
    chan_count = lax.axis_size("chan")
    tile_count = lax.axis_size("tile")
    inputs = row_count * tile_count
    device_count = chan_count * tile_count
    own = NCH // device_count
    pairs = frame_count // 2
    samples = frame_count * chan_count

    history = lax.ppermute(
        voltages[:, :, (frame_count - (TAPS - 1)) * NCH :], "chan", [(c, c + 1) for c in range(chan_count - 1)]
    )
    spectra = pl.pallas_call(
        spectra_kernel,
        out_shape=jax.ShapeDtypeStruct((2 * NCH, pairs, 128), jnp.bfloat16),
        scratch_shapes=[
            pltpu.VMEM((frame_count * row_count, 2 * NCH), jnp.bfloat16),
            pltpu.VMEM((2 * NCH * pairs, 128), jnp.float32),
        ],
        compiler_params=params(),
        name="spectra",
    )(voltages, history, jnp.asarray(taps_table()), jnp.asarray(dft_table(), jnp.bfloat16))

    turned = lax.all_to_all(
        spectra.reshape(device_count, own, 2, pairs, 128), ("chan", "tile"), split_axis=0, concat_axis=0, tiled=True
    )
    turned = turned.reshape(chan_count, tile_count, own, 2, pairs, 128)

    blocks = 4
    vis_shape = jax.ShapeDtypeStruct((tile_count, own, row_count, inputs), jnp.bfloat16)
    vis_spec = pl.BlockSpec((tile_count // blocks, 1, row_count, inputs), lambda a, b: (b, a, 0, 0))
    series_spec = pl.BlockSpec((1, 2 * samples, inputs), lambda a, b: (a, 0, 0))
    series, across, real = pl.pallas_call(
        real_kernel,
        grid=(own, blocks),
        in_specs=[pl.BlockSpec((chan_count, tile_count, 1, 2, pairs, 128), lambda a, b: (0, 0, a, 0, 0, 0))],
        out_specs=[series_spec, pl.BlockSpec((1, inputs, 2 * samples), lambda a, b: (a, 0, 0)), vis_spec],
        out_shape=[
            jax.ShapeDtypeStruct((own, 2 * samples, inputs), jnp.bfloat16),
            jax.ShapeDtypeStruct((own, inputs, 2 * samples), jnp.bfloat16),
            vis_shape,
        ],
        compiler_params=params(),
        name="real_sums",
    )(turned)
    real = lax.all_to_all(real, "tile", split_axis=0, concat_axis=0, tiled=True)
    imag = pl.pallas_call(
        imag_kernel,
        grid=(own, blocks),
        in_specs=[series_spec, pl.BlockSpec((1, inputs // blocks, 2 * samples), lambda a, b: (a, b, 0))],
        out_specs=vis_spec,
        out_shape=vis_shape,
        compiler_params=params(),
        cost_estimate=pl.CostEstimate(flops=2 * own * inputs * inputs * 2 * samples, bytes_accessed=8 << 20, transcendentals=0),
        name="imag_sums",
    )(series, across)
    imag = lax.all_to_all(imag, "tile", split_axis=0, concat_axis=0, tiled=True)

    gains = pl.pallas_call(
        gains_kernel,
        grid=(own,),
        in_specs=[
            pl.BlockSpec((1, 2 * samples, inputs), lambda a: (a, 0, 0)),
            pl.BlockSpec((1, inputs), lambda a: (0, 0)),
        ],
        out_specs=pl.BlockSpec((1, 2, inputs), lambda a: (a, 0, 0)),
        out_shape=jax.ShapeDtypeStruct((own, 2, inputs), jnp.float32),
        compiler_params=params(),
        cost_estimate=pl.CostEstimate(flops=own * inputs * samples * 64, bytes_accessed=2 << 20, transcendentals=0),
        name="gains",
    )(series, flags.reshape(1, inputs))
    gains = gains.reshape(own, 2, tile_count, row_count).transpose(2, 1, 0, 3)
    gains = lax.all_to_all(gains, "tile", split_axis=0, concat_axis=0, tiled=True)
    gains = gains.transpose(1, 0, 2, 3).reshape(2, tile_count * own, row_count)

    channels = tile_count * own
    visibilities = jnp.stack(
        [real.reshape(channels, row_count, inputs), imag.reshape(channels, row_count, inputs)]
    )
    return (visibilities, gains)


def solution(mesh):
    in_specs = (P(None, "tile", "chan"), P())
    out_specs = (P(None, "chan", "tile", None), P(None, "chan", "tile"))
    return jax.shard_map(body, mesh=mesh, in_specs=in_specs, out_specs=out_specs, check_vma=False)
```

time: 450 us -> 225 us (0.50)
  waiting for transfers between devices: 190 us -> 90 us
  matrix products: 57.9 us -> 0 us
  local copies, waits for them, and re-layouts: 60.1 us -> 4.36 us
  Pallas kernels: 0 us -> 40.4 us
  blocking collectives: 88.6 us -> 62.1 us
  other arithmetic: 28.7 us -> 8.31 us
  between operations: 15.5 us -> 0.67 us
  starting transfers between devices: 2.74 us -> 16.2 us
    all_gather x1 -> x0, waiting for transfers between devices: 190 us -> none  [body(): lax.all_gather(own_series, 'tile', axis=1, tiled=True)]
    all_to_all x0 -> x2, waiting for transfers between devices: none -> 87.9 us  [the longest x1 45.8 us: body(): imag = lax.all_to_all(imag, 'tile', split_axis=0, concat_axis=0, tiled=True)]
    dot_general x6 -> x0, matrix products: 57.9 us -> none  [the longest x4 33.6 us: rows_times(): jnp.einsum('cpq,cq->cp', matrix, vector, precision=lax.Precision.HIGHEST,...]
    all_gather x2 -> x0, blocking collectives: 46.6 us -> none  [body(): gains_full = lax.all_gather(gains_own, 'tile', axis=2, tiled=True)]
    pallas_call x0 -> x4, Pallas kernels: none -> 40.4 us  [the longest x1 11.2 us: body(): pl.pallas_call(real_kernel, grid=(own, blocks), in_specs=[pl.BlockSpec((c...]
    unnamed x19 -> x5, local copies, waits for them, and re-layouts: 25 us -> 1.77 us
    all_to_all x1 -> x2, blocking collectives: 42.1 us -> 62.1 us  [the longest x1 50.1 us: body(): lax.all_to_all(spectra.reshape(device_count, own, 2, pairs, 128), ('chan'...]
    all_to_all x0 -> x2, starting transfers between devices: none -> 14.4 us  [the longest x1 8.02 us: body(): imag = lax.all_to_all(imag, 'tile', split_axis=0, concat_axis=0, tiled=True)]
  transfers between devices with their start and end apart: 2 -> 3, of which waited for: 1 -> 3; matrix products, arithmetic and copies ran while one was open for 2% -> 1% of each run, Pallas kernels for 0% -> 4%
where the time goes in v1:
time: 225 us; the launch traced here: 222 us
  waiting for transfers between devices  90 us (40%)
  blocking collectives  62.1 us (28%)
  Pallas kernels  40.4 us (18%)
  starting transfers between devices  16.2 us (7%)
  other arithmetic  8.31 us (4%)
  local copies, waits for them, and re-layouts  4.36 us (2%)
    all_to_all x1, blocking collectives, body(): lax.all_to_all(spectra.reshape(device_count, own, 2, pairs, 128), ('chan'...  50.1 us
    all_to_all x1, waiting for transfers between devices, body(): imag = lax.all_to_all(imag, 'tile', split_axis=0, concat_axis=0, tiled=True)  45.8 us
    all_to_all x1, waiting for transfers between devices, body(): real = lax.all_to_all(real, 'tile', split_axis=0, concat_axis=0, tiled=True)  42.1 us
    all_to_all x1, blocking collectives, body(): lax.all_to_all(gains, 'tile', split_axis=0, concat_axis=0, tiled=True)  12.1 us
    pallas_call x1, Pallas kernels, body(): pl.pallas_call(real_kernel, grid=(own, blocks), in_specs=[pl.BlockSpec((c...  11.2 us
    pallas_call x1, Pallas kernels, body(): pl.pallas_call(spectra_kernel, out_shape=jax.ShapeDtypeStruct((2 * NCH, p...  10.8 us
    pallas_call x1, Pallas kernels, body(): pl.pallas_call(gains_kernel, grid=(own,), in_specs=[pl.BlockSpec((1, 2 *...  10.1 us
    pallas_call x1, Pallas kernels, body(): pl.pallas_call(imag_kernel, grid=(own, blocks), in_specs=[series_spec, pl...  8.31 us
  transfers between devices with their start and end apart: 3, of which 3 were waited for; matrix products, arithmetic and copies ran while one was open for 1% of the time, Pallas kernels for 4%

profile of v1, /device:TPU:6, one launch (start us, length us, event | category | flops | bytes accessed | tf_op | source)
XLA Modules:
  0.0 222.1 jit_solution(4691772350405462337)
XLA Ops:
  0.6 1.3 slice.3
  1.9 1.8 collective-permute-start
  3.7 2.1 collective-permute-done.h_ref
  5.8 0.0 copy-start
  5.8 1.0 copy-done
  6.8 10.8 %spectra.1 = bf16[512,16,128]{2,1,0:T(8,128)(2,1)} custom-call(bf16[2,64,8192]{2,1,0:T(8,128)(2,1)} %v_ref.1, bf16[2,64,3840]{2,1,0:T(8,128)(2,1)} %copy-done, f32[16,256]{1,0:T(8,128)} %constant.4.clone.taps_ref, bf16[512,512]{1,0:T(8,128)(2,1)} %constant.5.clone.table_ref), custom_call_target="tpu_custom_call" | custom-call | tf_op jit(solution)/shard_map/spectra/pallas_call | solution.py:200
  17.6 50.1 %all_to_all.20 = bf16[128,2,2,16,128]{4,3,2,1,0:T(8,128)(2,1)} all-to-all(bf16[128,2,2,16,128]{4,3,2,1,0:T(8,128)(2,1)} %bitcast.18), channel_id=1, replica_groups=mesh['chan'=8,'tile'=16] {'chan','tile'}, dimensions={0} | all-to-all | bytes 4194304 | tf_op jit(solution)/shard_map/all_to_all | solution.py:211
  67.7 11.2 %real_sums.1 = (bf16[2,512,1024]{2,1,0:T(8,128)(2,1)}, bf16[2,1024,512]{2,1,0:T(8,128)(2,1)}, bf16[16,2,64,1024]{3,2,1,0:T(8,128)(2,1)}) custom-call(bf16[8,16,2,2,16,128]{5,4,3,2,1,0:T(8,128)(2,1)} %bitcast.17), custom_call_target="tpu_custom_call" | custom-call | tf_op jit(solution)/shard_map/real_sums/pallas_call | solution.py:220
  78.9 10.1 %gains.1 = f32[2,2,1024]{2,1,0:T(2,128)} custom-call(bf16[2,512,1024]{2,1,0:T(8,128)(2,1)} %get-tuple-element.6.series_ref, s32[1,1024]{1,0:T(1,128)} %bitcast.21), custom_call_target="tpu_custom_call" | custom-call | flops 33554432 | bytes 2097152 | tf_op jit(solution)/shard_map/gains/pallas_call | solution.py:246
  88.9 0.8 reshape.22
  89.8 0.1 reshape.24
  89.9 12.1 %all_to_all.21 = f32[16,1,256]{2,1,0:T(1,128)S(1)} all-to-all(f32[16,1,256]{2,1,0:T(1,128)S(1)} %reshape.24), channel_id=1, replica_groups=mesh['chan'=8,'tile'=16] {'tile'}, dimensions={0} | all-to-all | bytes 32768 | tf_op jit(solution)/shard_map/all_to_all | solution.py:260
  101.9 6.4 %all-to-all-start.1 = ((bf16[16,2,64,1024]{3,2,1,0:T(8,128)(2,1)}), bf16[16,2,64,1024]{3,2,1,0:T(8,128)(2,1)}, u32[]{:S(2)}, u32[]{:S(2)}) async-start(bf16[16,2,64,1024]{3,2,1,0:T(8,128)(2,1)} %get-tuple-element.5), calls=%async_computation.1 | async-start | bytes 8388608 | tf_op jit(solution)/shard_map/all_to_all | solution.py:233
  108.4 8.3 %imag_sums.1 = bf16[16,2,64,1024]{3,2,1,0:T(8,128)(2,1)} custom-call(bf16[2,512,1024]{2,1,0:T(8,128)(2,1)} %get-tuple-element.6.series_ref, bf16[2,1024,512]{2,1,0:T(8,128)(2,1)} %get-tuple-element.7.across_ref), custom_call_target="tpu_custom_call" | custom-call | flops 2147483648 | bytes 8388608 | tf_op jit(solution)/shard_map/imag_sums/pallas_call | solution.py:234
  116.7 42.1 %all-to-all-done.1 = bf16[16,2,64,1024]{3,2,1,0:T(8,128)(2,1)} async-done(((bf16[16,2,64,1024]{3,2,1,0:T(8,128)(2,1)}), bf16[16,2,64,1024]{3,2,1,0:T(8,128)(2,1)}, u32[]{:S(2)}, u32[]{:S(2)}) %all-to-all-start.1) | async-done | bytes 4194336 | tf_op jit(solution)/shard_map/all_to_all | solution.py:233
  158.8 8.0 %all-to-all-start.2 = ((bf16[16,2,64,1024]{3,2,1,0:T(8,128)(2,1)}), bf16[16,2,64,1024]{3,2,1,0:T(8,128)(2,1)}, u32[]{:S(2)}, u32[]{:S(2)}) async-start(bf16[16,2,64,1024]{3,2,1,0:T(8,128)(2,1)} %imag_sums.1), calls=%async_computation.2 | async-start | bytes 8388608 | tf_op jit(solution)/shard_map/all_to_all | solution.py:244
  166.8 0.5 broadcast
  167.3 0.7 reduce
  168.0 0.1 reshape.25
  168.1 0.6 copy.8
  168.7 45.8 %all-to-all-done.2 = bf16[16,2,64,1024]{3,2,1,0:T(8,128)(2,1)} async-done(((bf16[16,2,64,1024]{3,2,1,0:T(8,128)(2,1)}), bf16[16,2,64,1024]{3,2,1,0:T(8,128)(2,1)}, u32[]{:S(2)}, u32[]{:S(2)}) %all-to-all-start.2) | async-done | bytes 4194336 | tf_op jit(solution)/shard_map/all_to_all | solution.py:244
  214.5 7.6 %pad_maximum_fusion = bf16[2,32,64,1024]{3,2,1,0:T(8,128)(2,1)} fusion(bf16[1,32,64,1024]{3,2,1,0:T(8,128)(2,1)} %bitcast.3, bf16[1,32,64,1024]{3,2,1,0:T(8,128)(2,1)} %bitcast.2), kind=kLoop, calls=%fused_computation | loop fusion | flops 4194304 | bytes 16777216 | tf_op jit(solution)/shard_map/stack | solution.py:264
  (1 shorter events, 0.0 us)
Async XLA Ops:
  1.9 3.9 %collective-permute-start = (bf16[2,64,3840]{2,1,0:T(8,128)(2,1)S(1)}, bf16[2,64,3840]{2,1,0:T(8,128)(2,1)S(1)}, u32[]{:S(2)}, u32[]{:S(2)}) collective-permute-start(bf16[2,64,3840]{2,1,0:T(8,128)(2,1)S(1)} %slice.3), channel_id=1, source_target_pairs={{0,16},{16,32},{32,48},{48,64},{64,80},{80,96},{96,112},{1,17},{17... | collective-permute-start | bytes 2949128 | tf_op jit(solution)/shard_map/ppermute | solution.py:197
  5.8 1.0 copy-start
  101.9 56.9 %all-to-all-start.1 = ((bf16[16,2,64,1024]{3,2,1,0:T(8,128)(2,1)}), bf16[16,2,64,1024]{3,2,1,0:T(8,128)(2,1)}, u32[]{:S(2)}, u32[]{:S(2)}) async-start(bf16[16,2,64,1024]{3,2,1,0:T(8,128)(2,1)} %get-tuple-element.5), calls=%async_computation.1 | async-start | bytes 8388608 | tf_op jit(solution)/shard_map/all_to_all | solution.py:233
  158.8 55.7 %all-to-all-start.2 = ((bf16[16,2,64,1024]{3,2,1,0:T(8,128)(2,1)}), bf16[16,2,64,1024]{3,2,1,0:T(8,128)(2,1)}, u32[]{:S(2)}, u32[]{:S(2)}) async-start(bf16[16,2,64,1024]{3,2,1,0:T(8,128)(2,1)} %imag_sums.1), calls=%async_computation.2 | async-start | bytes 8388608 | tf_op jit(solution)/shard_map/all_to_all | solution.py:244

commit v2 on v1

v2 whole, which is shorter than its diff:
```python
import functools
import math

import jax
import jax.numpy as jnp
import numpy as np
from jax import lax
from jax.experimental import pallas as pl
from jax.experimental.pallas import tpu as pltpu
from jax.sharding import PartitionSpec as P

NCH = 256
TAPS = 16
ITERS = 3
SHIFTS = (1, 3, 2, 0)
VMEM = 56 * 1024 * 1024


def taps_table():
    length = TAPS * NCH
    index = np.arange(length, dtype=np.float64)
    centre = (length - 1) / 2.0
    window = 0.5 - 0.5 * np.cos(2.0 * math.pi * (index + 0.5) / length)
    values = np.sinc((index - centre) / NCH) * window
    values = values * np.sqrt(NCH / np.sum(values * values))
    return values.reshape(TAPS, NCH).astype(np.float32)


def dft_table():
    index = np.arange(NCH)
    angle = (2.0 * math.pi / NCH) * (index[:, None] * index[None, :] % NCH)
    scale = 1.0 / math.sqrt(NCH)
    cosine = np.cos(angle) * scale
    sine = np.sin(angle) * scale
    real = np.concatenate([cosine, sine], axis=1)
    imag = np.concatenate([-sine, cosine], axis=1)
    return np.stack([real, imag], axis=1).reshape(2 * NCH, 2 * NCH).astype(np.float32)


def filter_frames(read, taps_ref, x_ref):
    frames = x_ref.shape[0] // 64

    def filter_tile(index, _):
        part = index // 8
        rows = pl.multiple_of((index // 2) % 4 * 16, 16)
        lane = pl.multiple_of(index % 2 * 128, 128)
        taps = [taps_ref[pl.ds(t, 1), pl.ds(lane, 128)] for t in range(TAPS)]
        window = []
        for f in range(frames + TAPS - 1):
            window.append(read(f, part, rows, lane).astype(jnp.float32))
            m = f - (TAPS - 1)
            if m < 0:
                continue
            total = taps[0] * window[m]
            for t in range(1, TAPS):
                total = total + taps[t] * window[m + t]
            x_ref[pl.ds(rows + m * 64, 16), pl.ds(part * NCH + lane, 128)] = total.astype(jnp.bfloat16)
        return 0

    lax.fori_loop(0, 16, filter_tile, 0)


def transform(x_ref, table_ref, wide_ref, store):
    pairs = x_ref.shape[0] // 128
    for block in range(pairs // 2):
        spectra = lax.dot_general(
            table_ref[...],
            x_ref[pl.ds(block * 256, 256), :],
            (((1,), (1,)), ((), ())),
            preferred_element_type=jnp.float32,
        )
        for half in range(2):
            wide_ref[pl.ds(block * 2 + half, 2 * NCH, stride=pairs), :] = spectra[:, half * 128 : half * 128 + 128]

    def narrow(index, _):
        rows = 64 * pairs
        tile = wide_ref[pl.ds(pl.multiple_of(index * rows, rows), rows), :]
        store(pl.multiple_of(index * 16, 16), tile.astype(jnp.bfloat16).reshape(16, 2, 2 * pairs, 128))
        return 0

    lax.fori_loop(0, 8, narrow, 0)


def late_kernel(v_ref, taps_ref, table_ref, out_ref, x_ref, wide_ref):
    first = v_ref.shape[2] // NCH // 2 - (TAPS - 1)

    def read(f, part, rows, lane):
        return v_ref[part, pl.ds(rows, 16), pl.ds(lane + (first + f) * NCH, 128)]

    def store(device, tile):
        out_ref[pl.ds(device, 16)] = tile

    filter_frames(read, taps_ref, x_ref)
    transform(x_ref, table_ref, wide_ref, store)


def early_kernel(v_ref, h_ref, late_ref, taps_ref, table_ref, out_ref, x_ref, wide_ref):
    history = TAPS - 1

    def read(f, part, rows, lane):
        if f < history:
            return h_ref[part, pl.ds(rows, 16), pl.ds(lane + f * NCH, 128)]
        return v_ref[part, pl.ds(rows, 16), pl.ds(lane + (f - history) * NCH, 128)]

    def store(device, tile):
        out_ref[pl.ds(device, 16), 0] = tile
        out_ref[pl.ds(device, 16), 1] = late_ref[pl.ds(device, 16)]

    filter_frames(read, taps_ref, x_ref)
    transform(x_ref, table_ref, wide_ref, store)


def order_kernel(recv_ref, *series_refs):
    chans, tiles, halves, own, sub, _ = recv_ref.shape
    rows = chans * halves * sub // 2
    for channel in range(own):
        for pair in range(tiles // 2):

            def parts(tile):
                both = recv_ref[:, tile, :, channel].astype(jnp.float32)
                both = both.reshape(chans * halves, 2, sub // 2, 128)
                return [both[:, part].reshape(rows, 128).astype(jnp.bfloat16) for part in range(2)]

            first, second = parts(2 * pair), parts(2 * pair + 1)
            lanes = slice(pair * 128, pair * 128 + 128)
            for part in range(2):
                low = jnp.concatenate([first[part][:, :64], second[part][:, :64]], axis=1)
                high = jnp.concatenate([first[part][:, 64:], second[part][:, 64:]], axis=1)
                start = 2 * part * rows
                series_refs[channel][start : start + rows, lanes] = low
                series_refs[channel][start + rows : start + 2 * rows, lanes] = high


def form_sums(series_ref, tiles, outs, slot):
    samples, inputs = series_ref.shape
    rows = inputs // 16
    left = []
    for tile in tiles:
        across = series_ref[:, pl.ds(pl.multiple_of(tile // 2 * 128, 128), 128)].T
        left.append(jnp.where(tile % 2 == 0, across[:rows], across[rows:]))
    left = jnp.concatenate(left, axis=0)
    count = left.shape[0]
    turned = jnp.concatenate([left[:, samples // 2 :], -left[:, : samples // 2]], axis=1)
    both = jnp.concatenate([left, turned], axis=0)
    sums = jnp.dot(both, series_ref[...], preferred_element_type=jnp.float32) * (2.0 / samples)
    for n, out_ref in enumerate(outs):
        for part in range(2):
            start = part * count + n * rows
            out_ref[slot, part] = sums[start : start + rows].astype(jnp.bfloat16)


def row_tiles(position_ref, axis, shifts):
    x, y = position_ref[0] // 4, position_ref[0] % 4
    if axis == 0:
        return [(x + shift) % 4 * 4 + y for shift in shifts]
    return [x * 4 + (y + shift) % 4 for shift in shifts]


def own_kernel(position_ref, first_ref, second_ref, *outs):
    for axis, series_ref in enumerate((first_ref, second_ref)):
        form_sums(series_ref, row_tiles(position_ref, axis, SHIFTS), outs[4 * axis : 4 * axis + 4], 0)


def near_kernel(position_ref, *refs):
    series, outs = refs[:4], refs[12:]
    for axis in range(2):
        tiles = row_tiles(position_ref, axis, SHIFTS)
        for slot in range(2):
            form_sums(series[2 * axis + slot], tiles, outs[4 * axis : 4 * axis + 4], slot)


def far_kernel(shifts, position_ref, *refs):
    halves, outs, series_ref = refs[:4], refs[8:12], refs[12]
    for axis in range(2):
        rows = halves[0].shape[0]
        series_ref[axis, 0:rows, :] = halves[2 * axis][...]
        series_ref[axis, rows : 2 * rows, :] = halves[2 * axis + 1][...]
        tiles = row_tiles(position_ref, axis, shifts)
        form_sums(series_ref.at[axis], tiles, outs[2 * axis : 2 * axis + 2], 0)


def place_kernel(moves, position_ref, *refs):
    out_ref, sems = refs[-2:]
    x, y = position_ref[0] // 4, position_ref[0] % 4
    copies = []
    for (axis, shift), part_ref in zip(moves, refs):
        for slot, step in enumerate((0, 2, 3, 1)):
            if axis == 0:
                owner = (x + 4 - shift) % 4 * 4 + (y + step) % 4
            else:
                owner = (x + step) % 4 * 4 + (y + 4 - shift) % 4
            for part in range(2):
                copy = pltpu.make_async_copy(
                    part_ref.at[slot, part], out_ref.at[part, owner * 2 + axis], sems.at[len(copies)]
                )
                copy.start()
                copies.append(copy)
    for copy in copies:
        copy.wait()


def gains_kernel(first_ref, second_ref, flags_ref, out_ref):
    keep = (1 - flags_ref[...]).astype(jnp.float32)
    for channel, series_ref in enumerate((first_ref, second_ref)):
        gain_real, gain_imag = stefcal(series_ref, keep)
        out_ref[channel, 0:1, :] = gain_real
        out_ref[channel, 1:2, :] = gain_imag


def stefcal(series_ref, keep):
    half = series_ref.shape[0] // 2
    steps = half // 16
    inverse = 2.0 / series_ref.shape[0]

    def load(step):
        start = pl.multiple_of(step * 16, 16)
        real = series_ref[pl.ds(start, 16), :].astype(jnp.float32)
        imag = series_ref[pl.ds(half + start, 16), :].astype(jnp.float32)
        return real, imag

    def fold(value):
        return value[0:8] + value[8:16]

    zeros = jnp.zeros((8, keep.shape[1]), jnp.float32)

    def diagonal_step(step, carry):
        real, imag = load(step)
        return (
            carry[0] + fold(real * real + imag * imag),
            carry[1] + fold(imag * real - real * imag),
        )

    diag = lax.fori_loop(0, steps, diagonal_step, (zeros, zeros), unroll=4)
    diag_real = jnp.sum(diag[0], axis=0, keepdims=True) * inverse
    diag_imag = jnp.sum(diag[1], axis=0, keepdims=True) * inverse

    gain_real = keep
    gain_imag = jnp.zeros_like(keep)
    for iteration in range(ITERS):

        def times_step(step, carry, gain_real=gain_real, gain_imag=gain_imag):
            real, imag = load(step)
            mix_real = jnp.sum(real * gain_real + imag * gain_imag, axis=1, keepdims=True)
            mix_imag = jnp.sum(real * gain_imag - imag * gain_real, axis=1, keepdims=True)
            return (
                carry[0] + fold(real * mix_real - imag * mix_imag),
                carry[1] + fold(real * mix_imag + imag * mix_real),
            )

        sums = lax.fori_loop(0, steps, times_step, (zeros, zeros), unroll=4)
        num_real = jnp.sum(sums[0], axis=0, keepdims=True) * inverse
        num_imag = jnp.sum(sums[1], axis=0, keepdims=True) * inverse
        num_real = num_real - (diag_real * gain_real - diag_imag * gain_imag)
        num_imag = num_imag - (diag_real * gain_imag + diag_imag * gain_real)
        power = gain_real * gain_real + gain_imag * gain_imag
        denominator = jnp.sum(power, axis=1, keepdims=True) - power
        new_real = keep * num_real / denominator
        new_imag = keep * num_imag / denominator
        if iteration % 2 == 1:
            new_real = 0.5 * (new_real + gain_real)
            new_imag = 0.5 * (new_imag + gain_imag)
        gain_real, gain_imag = new_real, new_imag
    return gain_real, gain_imag


def params():
    return pltpu.CompilerParams(vmem_limit_bytes=VMEM)


def cost(flops, size):
    return pl.CostEstimate(flops=int(flops), bytes_accessed=int(size), transcendentals=0)


def turn(value, axis, shift):
    pairs = []
    for x in range(4):
        for y in range(4):
            to = ((x + shift) % 4, y) if axis == 0 else (x, (y + shift) % 4)
            pairs.append((x * 4 + y, to[0] * 4 + to[1]))
    return lax.ppermute(value, "tile", pairs)


def place(position, parts, moves, out_shape, previous=None):
    operands = list(parts) + ([] if previous is None else [previous])
    anywhere = pl.BlockSpec(memory_space=pl.ANY)
    return pl.pallas_call(
        functools.partial(place_kernel, moves),
        in_specs=[pl.BlockSpec(memory_space=pltpu.SMEM)]
        + [pl.BlockSpec(memory_space=pltpu.VMEM)] * len(parts)
        + [anywhere] * (len(operands) - len(parts)),
        out_specs=anywhere,
        out_shape=out_shape,
        scratch_shapes=[pltpu.SemaphoreType.DMA((8 * len(parts),))],
        input_output_aliases={} if previous is None else {len(operands): 0},
        compiler_params=params(),
        cost_estimate=cost(0, len(parts) << 21),
        name="place",
    )(position, *operands)


def body(voltages, flags):
    row_count = voltages.shape[1]
    frame_count = voltages.shape[2] // NCH
    chan_count = lax.axis_size("chan")
    tile_count = lax.axis_size("tile")
    inputs = row_count * tile_count
    device_count = chan_count * tile_count
    own = NCH // device_count
    samples = frame_count * chan_count
    half = frame_count // 2
    sub = half

    taps = jnp.asarray(taps_table())
    table = jnp.asarray(dft_table(), jnp.bfloat16)
    scratch = [
        pltpu.VMEM((half * row_count, 2 * NCH), jnp.bfloat16),
        pltpu.VMEM((NCH * half, 128), jnp.float32),
    ]
    history = lax.ppermute(
        voltages[:, :, (frame_count - (TAPS - 1)) * NCH :], "chan", [(c, c + 1) for c in range(chan_count - 1)]
    )
    late = pl.pallas_call(
        late_kernel,
        out_shape=jax.ShapeDtypeStruct((device_count, own, sub, 128), jnp.bfloat16),
        scratch_shapes=scratch,
        compiler_params=params(),
        cost_estimate=cost(1.5e9, 4 << 20),
        name="late_spectra",
    )(voltages, taps, table)
    spectra = pl.pallas_call(
        early_kernel,
        out_shape=jax.ShapeDtypeStruct((device_count, 2, own, sub, 128), jnp.bfloat16),
        scratch_shapes=scratch,
        compiler_params=params(),
        cost_estimate=cost(1.5e9, 6 << 20),
        name="early_spectra",
    )(voltages, history, late, taps, table)

    turned = lax.all_to_all(spectra, ("chan", "tile"), split_axis=0, concat_axis=0, tiled=True)
    turned = turned.reshape(chan_count, tile_count, 2, own, sub, 128)
    series_shape = jax.ShapeDtypeStruct((2 * samples, inputs), jnp.bfloat16)
    series = pl.pallas_call(
        order_kernel,
        out_shape=[series_shape] * own,
        compiler_params=params(),
        cost_estimate=cost(1e6, 4 << 20),
        name="order",
    )(turned)

    position = lax.axis_index("tile").astype(jnp.int32).reshape(1)
    smem = pl.BlockSpec(memory_space=pltpu.SMEM)
    block_shape = jax.ShapeDtypeStruct((4, 2, row_count, inputs), jnp.bfloat16)
    anywhere = pl.BlockSpec(memory_space=pl.ANY)

    def slots(count, index):
        return pl.BlockSpec((count, 2, row_count, inputs), lambda i: (index, 0, 0, 0))

    def whole(shape):
        return pl.BlockSpec(shape, lambda i: (0,) * len(shape))

    flops = 8 * 4 * row_count * inputs * samples
    up = [turn(series[axis], 1 - axis, 1) for axis in range(2)]
    down = [turn(series[axis], 1 - axis, 3) for axis in range(2)]
    blocks = pl.pallas_call(
        own_kernel,
        grid=(1,),
        in_specs=[smem] + [whole((2 * samples, inputs))] * 2,
        out_specs=[slots(1, 0)] * 8,
        out_shape=[block_shape] * 8,
        compiler_params=params(),
        cost_estimate=cost(2 * flops, 4 << 20),
        name="own_sums",
    )(position, *series)
    gains = pl.pallas_call(
        gains_kernel,
        in_specs=[pl.BlockSpec(memory_space=pltpu.VMEM)] * 3,
        out_specs=pl.BlockSpec(memory_space=pltpu.VMEM),
        out_shape=jax.ShapeDtypeStruct((own, 2, inputs), jnp.float32),
        compiler_params=params(),
        cost_estimate=cost(own * inputs * samples * 64, 2 << 20),
        name="gains",
    )(*series, flags.reshape(1, inputs))
    up, down, blocks, gains = lax.optimization_barrier((up, down, blocks, gains))

    far = []
    for axis in range(2):
        far.append(turn(up[axis][:samples], 1 - axis, 1))
        far.append(turn(down[axis][samples:], 1 - axis, 3))
    blocks = pl.pallas_call(
        near_kernel,
        grid=(1,),
        in_specs=[smem] + [whole((2 * samples, inputs))] * 4 + [anywhere] * 8,
        out_specs=[slots(2, 1)] * 8,
        out_shape=[block_shape] * 8,
        input_output_aliases={5 + n: n for n in range(8)},
        compiler_params=params(),
        cost_estimate=cost(4 * flops, 8 << 20),
        name="near_sums",
    )(position, up[0], down[0], up[1], down[1], *blocks)

    def far_sums(shifts, chosen):
        return pl.pallas_call(
            functools.partial(far_kernel, shifts),
            grid=(1,),
            in_specs=[smem] + [whole((samples, inputs))] * 4 + [anywhere] * 4,
            out_specs=[slots(1, 1)] * 4,
            out_shape=[block_shape] * 4,
            scratch_shapes=[pltpu.VMEM((2, 2 * samples, inputs), jnp.bfloat16)],
            input_output_aliases={5 + n: n for n in range(4)},
            compiler_params=params(),
            cost_estimate=cost(flops, 6 << 20),
            name="far_sums",
        )(position, *far, *chosen)

    two = far_sums((2, 0), [blocks[n] for n in (2, 3, 6, 7)])
    one = far_sums((1, 3), [blocks[n] for n in (0, 1, 4, 5)])
    last = [turn(two[0], 0, 2), turn(two[2], 1, 2)]
    sent = [turn(one[0], 0, 1), turn(one[1], 0, 3), turn(one[2], 1, 1), turn(one[3], 1, 3)]

    out_shape = jax.ShapeDtypeStruct((2, tile_count * own, row_count, inputs), jnp.bfloat16)
    visibilities = place(position, [two[1], two[3]], [(0, 0), (1, 0)], out_shape)
    visibilities = place(position, last, [(0, 2), (1, 2)], out_shape, visibilities)
    visibilities = place(position, sent[:3], [(0, 1), (0, 3), (1, 1)], out_shape, visibilities)
    visibilities = place(position, sent[3:], [(1, 3)], out_shape, visibilities)

    gains = gains.reshape(own, 2, tile_count, row_count).transpose(2, 1, 0, 3)
    gains = lax.all_to_all(gains, "tile", split_axis=0, concat_axis=0, tiled=True)
    gains = gains.transpose(1, 0, 2, 3).reshape(2, tile_count * own, row_count)
    return (visibilities, gains)


def solution(mesh):
    in_specs = (P(None, "tile", "chan"), P())
    out_specs = (P(None, "chan", "tile", None), P(None, "chan", "tile"))
    return jax.shard_map(body, mesh=mesh, in_specs=in_specs, out_specs=out_specs, check_vma=False)
```

time: 225 us -> 190 us (0.84)
  waiting for transfers between devices: 90 us -> 37.9 us
  Pallas kernels: 40.4 us -> 53.1 us
  other arithmetic: 8.31 us -> 0.68 us
  blocking collectives: 62.1 us -> 68.2 us
  local copies, waits for them, and re-layouts: 4.36 us -> 8.03 us
  starting transfers between devices: 16.2 us -> 18.9 us
    all_to_all x2 -> x0, waiting for transfers between devices: 87.9 us -> none  [the longest x1 45.8 us: body(): imag = lax.all_to_all(imag, 'tile', split_axis=0, concat_axis=0, tiled=True)]
    ppermute x0 -> x14, waiting for transfers between devices: none -> 37.9 us  [turn(): return lax.ppermute(value, 'tile', pairs)]
    ppermute x0 -> x14, starting transfers between devices: none -> 17.1 us  [turn(): return lax.ppermute(value, 'tile', pairs)]
    all_to_all x2 -> x0, starting transfers between devices: 14.4 us -> none  [the longest x1 8.02 us: body(): imag = lax.all_to_all(imag, 'tile', split_axis=0, concat_axis=0, tiled=True)]
    pallas_call x4 -> x12, Pallas kernels: 40.4 us -> 53.1 us  [the longest x4 11.9 us: place(): pl.pallas_call(functools.partial(place_kernel, moves), in_specs=[pl.Block...]
    all_to_all x1, blocking collectives: 12.1 us -> 22.4 us  [body(): lax.all_to_all(gains, 'tile', split_axis=0, concat_axis=0, tiled=True)]
    another operation x1 -> x0, other arithmetic: 7.63 us -> none  [body(): jnp.stack([real.reshape(channels, row_count, inputs), imag.reshape(channe...]
    all_to_all x1, blocking collectives: 50.1 us -> 45.8 us  [body(): lax.all_to_all(spectra, ('chan', 'tile'), split_axis=0, concat_axis=0, ti...]
  transfers between devices with their start and end apart: 3 -> 15, of which waited for: 3 -> 7; matrix products, arithmetic and copies ran while one was open for 1% -> 2% of each run, Pallas kernels for 4% -> 20%
where the time goes in v2:
time: 190 us; the launch traced here: 188 us
  blocking collectives  68.2 us (36%)
  Pallas kernels  53.1 us (28%)
  waiting for transfers between devices  37.9 us (20%)
  starting transfers between devices  18.9 us (10%)
  local copies, waits for them, and re-layouts  8.03 us (4%)
    all_to_all x1, blocking collectives, body(): lax.all_to_all(spectra, ('chan', 'tile'), split_axis=0, concat_axis=0, ti...  45.8 us
    ppermute x14, waiting for transfers between devices, turn(): return lax.ppermute(value, 'tile', pairs)  37.9 us
    all_to_all x1, blocking collectives, body(): lax.all_to_all(gains, 'tile', split_axis=0, concat_axis=0, tiled=True)  22.4 us
    ppermute x14, starting transfers between devices, turn(): return lax.ppermute(value, 'tile', pairs)  17.1 us
    pallas_call x4, Pallas kernels, place(): pl.pallas_call(functools.partial(place_kernel, moves), in_specs=[pl.Block...  11.9 us
    pallas_call x1, Pallas kernels, body(): pl.pallas_call(gains_kernel, in_specs=[pl.BlockSpec(memory_space=pltpu.VM...  7.93 us
    pallas_call x1, Pallas kernels, body(): pl.pallas_call(early_kernel, out_shape=jax.ShapeDtypeStruct((device_count...  7.43 us
    pallas_call x2, Pallas kernels, far_sums(): pl.pallas_call(functools.partial(far_kernel, shifts), grid=(1,), in_specs...  6.4 us
  transfers between devices with their start and end apart: 15, of which 7 were waited for; matrix products, arithmetic and copies ran while one was open for 2% of the time, Pallas kernels for 20%

profile of v2, /device:TPU:6, one launch (start us, length us, event | category | flops | bytes accessed | tf_op | source)
XLA Modules:
  0.0 187.7 jit_solution(15806607429060200912)
XLA Ops:
  0.6 1.3 slice.15
  1.9 1.8 collective-permute-start
  3.7 6.4 %late_spectra.1.late_ref = bf16[128,2,16,128]{3,2,1,0:T(8,128)(2,1)} custom-call(bf16[2,64,8192]{2,1,0:T(8,128)(2,1)} %v_ref.3, f32[16,256]{1,0:T(8,128)} %constant.8.clone.taps_ref, bf16[512,512]{1,0:T(8,128)(2,1)} %constant.9.clone.table_ref), custom_call_target="tpu_custom_call" | custom-call | flops 1500000000 | bytes 4194304 | tf_op jit(solution)/shard_map/late_spectra/pallas_call | solution.py:322
  10.1 0.9 copy-done.10
  11.0 7.4 %early_spectra.1 = bf16[128,2,2,16,128]{4,3,2,1,0:T(8,128)(2,1)} custom-call(bf16[2,64,8192]{2,1,0:T(8,128)(2,1)} %v_ref.3, bf16[2,64,3840]{2,1,0:T(8,128)(2,1)} %copy-done.10, bf16[128,2,16,128]{3,2,1,0:T(8,128)(2,1)} %late_spectra.1.late_ref, f32[16,256]{1,0:T(8,128)} %constant.8.clone.taps_ref, bf16[512,512]{1,0:T(8,128)(2,1)} %constant.9.clone.table_ref), custom_call_target="tpu_custom_call" | custom-call | flops 1500000000 | bytes 6291456 | tf_op jit(solution)/shard_map/early_spectra/pallas_call | solution.py:330
  18.5 45.8 %all_to_all.10 = bf16[128,2,2,16,128]{4,3,2,1,0:T(8,128)(2,1)} all-to-all(bf16[128,2,2,16,128]{4,3,2,1,0:T(8,128)(2,1)} %early_spectra.1), channel_id=1, replica_groups=mesh['chan'=8,'tile'=16] {'chan','tile'}, dimensions={0} | all-to-all | bytes 4194304 | tf_op jit(solution)/shard_map/all_to_all | solution.py:339
  64.2 3.3 %order.1 = (bf16[512,1024]{1,0:T(8,128)(2,1)}, bf16[512,1024]{1,0:T(8,128)(2,1)}) custom-call(bf16[8,16,2,2,16,128]{5,4,3,2,1,0:T(8,128)(2,1)} %bitcast.15), custom_call_target="tpu_custom_call" | custom-call | flops 1000000 | bytes 4194304 | tf_op jit(solution)/shard_map/order/pallas_call | solution.py:342
  67.6 0.9 collective-permute-start.1
  68.5 2.9 %collective-permute-start.2 = (bf16[512,1024]{1,0:T(8,128)(2,1)}, bf16[512,1024]{1,0:T(8,128)(2,1)S(1)}, u32[]{:S(2)}, u32[]{:S(2)}) collective-permute-start(bf16[512,1024]{1,0:T(8,128)(2,1)} %get-tuple-element.42.second_ref), channel_id=1, source_target_pairs={{0,4},{1,5},{2,6},{3,7},{4,8},{5,9},{6,10},{7,11},{8,12},{9,13},{1... | collective-permute-start | bytes 3145736 | tf_op jit(solution)/shard_map/ppermute | solution.py:280
  71.4 2.3 %collective-permute-start.3 = (bf16[512,1024]{1,0:T(8,128)(2,1)}, bf16[512,1024]{1,0:T(8,128)(2,1)S(1)}, u32[]{:S(2)}, u32[]{:S(2)}) collective-permute-start(bf16[512,1024]{1,0:T(8,128)(2,1)} %get-tuple-element.41.first_ref), channel_id=1, source_target_pairs={{0,3},{1,0},{2,1},{3,2},{4,7},{5,4},{6,5},{7,6},{8,11},{9,8},{10,9... | collective-permute-start | bytes 3145736 | tf_op jit(solution)/shard_map/ppermute | solution.py:280
  73.6 7.9 %gains.1 = f32[2,2,1024]{2,1,0:T(2,128)} custom-call(bf16[512,1024]{1,0:T(8,128)(2,1)} %get-tuple-element.41.first_ref, bf16[512,1024]{1,0:T(8,128)(2,1)} %get-tuple-element.42.second_ref, s32[1,1024]{1,0:T(1,128)} %bitcast.18), custom_call_target="tpu_custom_call" | custom-call | flops 33554432 | bytes 2097152 | tf_op jit(solution)/shard_map/gains/pallas_call | solution.py:374
  81.5 3.8 %own_sums.1 = (bf16[4,2,64,1024]{3,2,1,0:T(8,128)(2,1)}, bf16[4,2,64,1024]{3,2,1,0:T(8,128)(2,1)}, bf16[4,2,64,1024]{3,2,1,0:T(8,128)(2,1)}, bf16[4,2,64,1024]{3...) custom-call(s32[1]{0:T(128)} %bitcast.position_ref, ...), custom_call_target="tpu_custom_call" | custom-call | flops 1073741824 | bytes 4194304 | tf_op jit(solution)/shard_map/own_sums/pallas_call | solution.py:364
  85.4 9.2 %collective-permute-done.1.refs_0_ = bf16[512,1024]{1,0:T(8,128)(2,1)S(1)} collective-permute-done((bf16[512,1024]{1,0:T(8,128)(2,1)}, bf16[512,1024]{1,0:T(8,128)(2,1)S(1)}, u32[]{:S(2)}, u32[]{:S(2)}) %collective-permute-start.1) | collective-permute-done | bytes 1048608 | tf_op jit(solution)/shard_map/ppermute | solution.py:280
  95.4 3.4 %collective-permute-done.4.refs_3_ = bf16[512,1024]{1,0:T(8,128)(2,1)} collective-permute-done((bf16[512,1024]{1,0:T(8,128)(2,1)}, bf16[512,1024]{1,0:T(8,128)(2,1)}, u32[]{:S(2)}, u32[]{:S(2)}) %collective-permute-start.4) | collective-permute-done | bytes 1048608 | tf_op jit(solution)/shard_map/ppermute | solution.py:280
  99.0 3.3 %collective-permute-start.6 = (bf16[256,1024]{1,0:T(8,128)(2,1)S(1)}, bf16[256,1024]{1,0:T(8,128)(2,1)S(1)}, u32[]{:S(2)}, u32[]{:S(2)}) collective-permute-start(bf16[256,1024]{1,0:T(8,128)(2,1)S(1)} %slice.17), channel_id=1, source_target_pairs={{0,3},{1,0},{2,1},{3,2},{4,7},{5,4},{6,5},{7,6},{8,11},{9,8},{10,9... | collective-permute-start | bytes 1572872 | tf_op jit(solution)/shard_map/ppermute | solution.py:280
  102.4 1.1 slice.19
  103.5 2.3 %collective-permute-start.8 = (bf16[256,1024]{1,0:T(8,128)(2,1)S(1)}, bf16[256,1024]{1,0:T(8,128)(2,1)S(1)}, u32[]{:S(2)}, u32[]{:S(2)}) collective-permute-start(bf16[256,1024]{1,0:T(8,128)(2,1)S(1)} %slice.19), channel_id=1, source_target_pairs={{0,12},{1,13},{2,14},{3,15},{4,0},{5,1},{6,2},{7,3},{8,4},{9,5},{1... | collective-permute-start | bytes 1572872 | tf_op jit(solution)/shard_map/ppermute | solution.py:280
  105.8 5.9 %near_sums.1 = (bf16[4,2,64,1024]{3,2,1,0:T(8,128)(2,1)}, bf16[4,2,64,1024]{3,2,1,0:T(8,128)(2,1)}, bf16[4,2,64,1024]{3,2,1,0:T(8,128)(2,1)}, bf16[4,2,64,1024]{...) custom-call(s32[1]{0:T(128)} %bitcast.position_ref, ...), custom_call_target="tpu_custom_call", output_to_operand_aliasing={{0}: (5, {}), {1}: (6, {}), {2}: (7, {}), {3}: (8, {}), {4}... | custom-call | flops 2147483648 | bytes 8388608 | tf_op jit(solution)/shard_map/near_sums/pallas_call | solution.py:389
  111.7 1.7 collective-permute-done.7.refs_2_
  113.4 2.6 %collective-permute-done.8.refs_3_ = bf16[256,1024]{1,0:T(8,128)(2,1)S(1)} collective-permute-done((bf16[256,1024]{1,0:T(8,128)(2,1)S(1)}, bf16[256,1024]{1,0:T(8,128)(2,1)S(1)}, u32[]{:S(2)}, u32[]{:S(2)}) %collective-permute-start.8) | collective-permute-done | bytes 524320 | tf_op jit(solution)/shard_map/ppermute | solution.py:280
  116.8 3.2 %far_sums.3 = (bf16[4,2,64,1024]{3,2,1,0:T(8,128)(2,1)}, bf16[4,2,64,1024]{3,2,1,0:T(8,128)(2,1)}, bf16[4,2,64,1024]{3,2,1,0:T(8,128)(2,1)}, bf16[4,2,64,1024]{3,2,1,0:T(8,128)(2,1)}) custom-call(s32[1]{0:T(128)} %bitcast.position_ref, bf16[256,1024]{1,0:T(8,128)(2,1)} %copy-done.3, ...), custom_call_target="tpu_custom_call", output_to_operand_aliasing={{0}: (5, {}), {1}: (6, {}), {2}: (7, {}), {3}: (8, {})} | custom-call | flops 536870912 | bytes 6291456 | tf_op jit(solution)/shard_map/far_sums/pallas_call | solution.py:402
  120.9 3.2 %far_sums.2 = (bf16[4,2,64,1024]{3,2,1,0:T(8,128)(2,1)}, bf16[4,2,64,1024]{3,2,1,0:T(8,128)(2,1)}, bf16[4,2,64,1024]{3,2,1,0:T(8,128)(2,1)}, bf16[4,2,64,1024]{3,2,1,0:T(8,128)(2,1)}) custom-call(s32[1]{0:T(128)} %bitcast.position_ref, bf16[256,1024]{1,0:T(8,128)(2,1)} %copy-done.3, ...), custom_call_target="tpu_custom_call", output_to_operand_aliasing={{0}: (5, {}), {1}: (6, {}), {2}: (7, {}), {3}: (8, {})} | custom-call | flops 536870912 | bytes 6291456 | tf_op jit(solution)/shard_map/far_sums/pallas_call | solution.py:402
  124.0 2.3 %collective-permute-start.10 = (bf16[4,2,64,1024]{3,2,1,0:T(8,128)(2,1)}, bf16[4,2,64,1024]{3,2,1,0:T(8,128)(2,1)S(1)}, u32[]{:S(2)}, u32[]{:S(2)}) collective-permute-start(bf16[4,2,64,1024]{3,2,1,0:T(8,128)(2,1)} %get-tuple-element.68), channel_id=1, source_target_pairs={{0,4},{1,5},{2,6},{3,7},{4,8},{5,9},{6,10},{7,11},{8,12},{9,13},{1... | collective-permute-start | bytes 3145736 | tf_op jit(solution)/shard_map/ppermute | solution.py:280
  126.8 1.1 collective-permute-start.12
  127.9 20.0 %collective-permute-done.13.refs_0_ = bf16[4,2,64,1024]{3,2,1,0:T(8,128)(2,1)} collective-permute-done((bf16[4,2,64,1024]{3,2,1,0:T(8,128)(2,1)}, bf16[4,2,64,1024]{3,2,1,0:T(8,128)(2,1)}, u32[]{:S(2)}, u32[]{:S(2)}) %collective-permute-start.13) | collective-permute-done | bytes 1048608 | tf_op jit(solution)/shard_map/ppermute | solution.py:280
  148.8 22.4 %all_to_all.11 = f32[16,1,256]{2,1,0:T(1,128)S(1)} all-to-all(f32[16,1,256]{2,1,0:T(1,128)S(1)} %reshape.24), channel_id=1, replica_groups=mesh['chan'=8,'tile'=16] {'tile'}, dimensions={0} | all-to-all | bytes 32768 | tf_op jit(solution)/shard_map/all_to_all | solution.py:427
  173.1 3.0 %place.4.refs_2_ = bf16[2,32,64,1024]{3,2,1,0:T(8,128)(2,1)} custom-call(s32[1]{0:T(128)} %bitcast.position_ref, bf16[4,2,64,1024]{3,2,1,0:T(8,128)(2,1)} %get-tuple-element.77.refs_0_, bf16[4,2,64,1024]{3,2,1,0:T(8,128)(2,1)} %get-tuple-element.78.refs_1_), custom_call_target="tpu_custom_call" | custom-call | bytes 4194304 | tf_op jit(solution)/shard_map/place/pallas_call | solution.py:286
  176.1 3.0 %place.5.refs_3_ = bf16[2,32,64,1024]{3,2,1,0:T(8,128)(2,1)} custom-call(s32[1]{0:T(128)} %bitcast.position_ref, bf16[4,2,64,1024]{3,2,1,0:T(8,128)(2,1)} %collective-permute-done.13.refs_0_, bf16[4,2,64,1024]{3,2,1,0:T(8,128)(2,1)} %collective-permute-done.14.refs_1_, bf16[2,32,64,1024]{3,2,1,0:T(8,128)(2,1)} %place.4.refs_2_), custom_call_target="tpu_custom_call", output_to_operand_aliasing={{}: (3, {})} | custom-call | bytes 4194304 | tf_op jit(solution)/shard_map/place/pallas_call | solution.py:286
  179.2 0.9 copy-done.7
  180.5 1.1 copy-done.9
  181.6 3.7 %place.6.refs_1_ = bf16[2,32,64,1024]{3,2,1,0:T(8,128)(2,1)} custom-call(s32[1]{0:T(128)} %bitcast.position_ref, bf16[4,2,64,1024]{3,2,1,0:T(8,128)(2,1)} %copy-done.7, bf16[4,2,64,1024]{3,2,1,0:T(8,128)(2,1)} %copy-done.8, bf16[4,2,64,1024]{3,2,1,0:T(8,128)(2,1)} %copy-done.9, bf16[2,32,64,1024]{3,2,1,0:T(8,128)(2,1)} %place.5.refs_3_), custom_call_target="tpu_custom_call", output_to_operand_aliasing={{}: (4, {})} | custom-call | bytes 6291456 | tf_op jit(solution)/shard_map/place/pallas_call | solution.py:286
  185.3 2.3 %place.7 = bf16[2,32,64,1024]{3,2,1,0:T(8,128)(2,1)} custom-call(s32[1]{0:T(128)} %bitcast.position_ref, bf16[4,2,64,1024]{3,2,1,0:T(8,128)(2,1)} %collective-permute-done.9.refs_0_, bf16[2,32,64,1024]{3,2,1,0:T(8,128)(2,1)} %place.6.refs_1_), custom_call_target="tpu_custom_call", output_to_operand_aliasing={{}: (2, {})} | custom-call | bytes 2097152 | tf_op jit(solution)/shard_map/place/pallas_call | solution.py:286
  (48 shorter events, 6.5 us)
Async XLA Ops:
  1.9 8.2 %collective-permute-start = (bf16[2,64,3840]{2,1,0:T(8,128)(2,1)S(1)}, bf16[2,64,3840]{2,1,0:T(8,128)(2,1)S(1)}, u32[]{:S(2)}, u32[]{:S(2)}) collective-permute-start(bf16[2,64,3840]{2,1,0:T(8,128)(2,1)S(1)} %slice.15), channel_id=1, source_target_pairs={{0,16},{16,32},{32,48},{48,64},{64,80},{80,96},{96,112},{1,17},{17... | collective-permute-start | bytes 2949128 | tf_op jit(solution)/shard_map/ppermute | solution.py:319
  10.1 0.9 copy-start.10
  67.6 27.0 %collective-permute-start.1 = (bf16[512,1024]{1,0:T(8,128)(2,1)}, bf16[512,1024]{1,0:T(8,128)(2,1)S(1)}, u32[]{:S(2)}, u32[]{:S(2)}) collective-permute-start(bf16[512,1024]{1,0:T(8,128)(2,1)} %get-tuple-element.41.first_ref), channel_id=1, source_target_pairs={{0,1},{1,2},{2,3},{3,0},{4,5},{5,6},{6,7},{7,4},{8,9},{9,10},{10,1... | collective-permute-start | bytes 3145736 | tf_op jit(solution)/shard_map/ppermute | solution.py:280
  68.5 26.1 %collective-permute-start.2 = (bf16[512,1024]{1,0:T(8,128)(2,1)}, bf16[512,1024]{1,0:T(8,128)(2,1)S(1)}, u32[]{:S(2)}, u32[]{:S(2)}) collective-permute-start(bf16[512,1024]{1,0:T(8,128)(2,1)} %get-tuple-element.42.second_ref), channel_id=1, source_target_pairs={{0,4},{1,5},{2,6},{3,7},{4,8},{5,9},{6,10},{7,11},{8,12},{9,13},{1... | collective-permute-start | bytes 3145736 | tf_op jit(solution)/shard_map/ppermute | solution.py:280
  71.4 24.1 %collective-permute-start.3 = (bf16[512,1024]{1,0:T(8,128)(2,1)}, bf16[512,1024]{1,0:T(8,128)(2,1)S(1)}, u32[]{:S(2)}, u32[]{:S(2)}) collective-permute-start(bf16[512,1024]{1,0:T(8,128)(2,1)} %get-tuple-element.41.first_ref), channel_id=1, source_target_pairs={{0,3},{1,0},{2,1},{3,2},{4,7},{5,4},{6,5},{7,6},{8,11},{9,8},{10,9... | collective-permute-start | bytes 3145736 | tf_op jit(solution)/shard_map/ppermute | solution.py:280
  73.6 25.2 %collective-permute-start.4 = (bf16[512,1024]{1,0:T(8,128)(2,1)}, bf16[512,1024]{1,0:T(8,128)(2,1)}, u32[]{:S(2)}, u32[]{:S(2)}) collective-permute-start(bf16[512,1024]{1,0:T(8,128)(2,1)} %get-tuple-element.42.second_ref), channel_id=1, source_target_pairs={{0,12},{1,13},{2,14},{3,15},{4,0},{5,1},{6,2},{7,3},{8,4},{9,5},{1... | collective-permute-start | bytes 3145736 | tf_op jit(solution)/shard_map/ppermute | solution.py:280
  94.6 11.2 %copy-start = (bf16[512,1024]{1,0:T(8,128)(2,1)}, bf16[512,1024]{1,0:T(8,128)(2,1)S(1)}, u32[]{:S(2)}) copy-start(bf16[512,1024]{1,0:T(8,128)(2,1)S(1)} %collective-permute-done.1.refs_0_) | copy-start | bytes 3145732
  94.6 11.2 %copy-start.1 = (bf16[512,1024]{1,0:T(8,128)(2,1)}, bf16[512,1024]{1,0:T(8,128)(2,1)S(1)}, u32[]{:S(2)}) copy-start(bf16[512,1024]{1,0:T(8,128)(2,1)S(1)} %collective-permute-done.2.refs_2_) | copy-start | bytes 3145732
  95.4 10.3 %copy-start.2 = (bf16[512,1024]{1,0:T(8,128)(2,1)}, bf16[512,1024]{1,0:T(8,128)(2,1)S(1)}, u32[]{:S(2)}) copy-start(bf16[512,1024]{1,0:T(8,128)(2,1)S(1)} %collective-permute-done.3.refs_1_) | copy-start | bytes 3145732
  98.9 12.8 %collective-permute-start.5 = (bf16[256,1024]{1,0:T(8,128)(2,1)S(1)}, bf16[256,1024]{1,0:T(8,128)(2,1)S(1)}, u32[]{:S(2)}, u32[]{:S(2)}) collective-permute-start(bf16[256,1024]{1,0:T(8,128)(2,1)S(1)} %slice.16), channel_id=1, source_target_pairs={{0,1},{1,2},{2,3},{3,0},{4,5},{5,6},{6,7},{7,4},{8,9},{9,10},{10,1... | collective-permute-start | bytes 1572872 | tf_op jit(solution)/shard_map/ppermute | solution.py:280
  99.0 12.7 %collective-permute-start.6 = (bf16[256,1024]{1,0:T(8,128)(2,1)S(1)}, bf16[256,1024]{1,0:T(8,128)(2,1)S(1)}, u32[]{:S(2)}, u32[]{:S(2)}) collective-permute-start(bf16[256,1024]{1,0:T(8,128)(2,1)S(1)} %slice.17), channel_id=1, source_target_pairs={{0,3},{1,0},{2,1},{3,2},{4,7},{5,4},{6,5},{7,6},{8,11},{9,8},{10,9... | collective-permute-start | bytes 1572872 | tf_op jit(solution)/shard_map/ppermute | solution.py:280
  102.3 11.1 %collective-permute-start.7 = (bf16[256,1024]{1,0:T(8,128)(2,1)S(1)}, bf16[256,1024]{1,0:T(8,128)(2,1)S(1)}, u32[]{:S(2)}, u32[]{:S(2)}) collective-permute-start(bf16[256,1024]{1,0:T(8,128)(2,1)S(1)} %slice.18), channel_id=1, source_target_pairs={{0,4},{1,5},{2,6},{3,7},{4,8},{5,9},{6,10},{7,11},{8,12},{9,13},{1... | collective-permute-start | bytes 1572872 | tf_op jit(solution)/shard_map/ppermute | solution.py:280
  103.5 12.5 %collective-permute-start.8 = (bf16[256,1024]{1,0:T(8,128)(2,1)S(1)}, bf16[256,1024]{1,0:T(8,128)(2,1)S(1)}, u32[]{:S(2)}, u32[]{:S(2)}) collective-permute-start(bf16[256,1024]{1,0:T(8,128)(2,1)S(1)} %slice.19), channel_id=1, source_target_pairs={{0,12},{1,13},{2,14},{3,15},{4,0},{5,1},{6,2},{7,3},{8,4},{9,5},{1... | collective-permute-start | bytes 1572872 | tf_op jit(solution)/shard_map/ppermute | solution.py:280
  111.6 37.0 %copy-start.11 = (f32[2,2,1024]{2,1,0:T(2,128)S(1)}, f32[2,2,1024]{2,1,0:T(2,128)}, u32[]{:S(2)}) copy-start(f32[2,2,1024]{2,1,0:T(2,128)} %gains.1) | copy-start | bytes 49156
  111.7 4.2 %copy-start.3 = (bf16[256,1024]{1,0:T(8,128)(2,1)}, bf16[256,1024]{1,0:T(8,128)(2,1)S(1)}, u32[]{:S(2)}) copy-start(bf16[256,1024]{1,0:T(8,128)(2,1)S(1)} %collective-permute-done.5.refs_0_) | copy-start | bytes 1572868
  111.7 4.2 %copy-start.4 = (bf16[256,1024]{1,0:T(8,128)(2,1)}, bf16[256,1024]{1,0:T(8,128)(2,1)S(1)}, u32[]{:S(2)}) copy-start(bf16[256,1024]{1,0:T(8,128)(2,1)S(1)} %collective-permute-done.6.refs_1_) | copy-start | bytes 1572868
  113.4 2.6 %copy-start.5 = (bf16[256,1024]{1,0:T(8,128)(2,1)}, bf16[256,1024]{1,0:T(8,128)(2,1)S(1)}, u32[]{:S(2)}) copy-start(bf16[256,1024]{1,0:T(8,128)(2,1)S(1)} %collective-permute-done.7.refs_2_) | copy-start | bytes 1572868
  116.0 0.8 copy-start.6
  120.0 28.0 %collective-permute-start.13 = (bf16[4,2,64,1024]{3,2,1,0:T(8,128)(2,1)}, bf16[4,2,64,1024]{3,2,1,0:T(8,128)(2,1)}, u32[]{:S(2)}, u32[]{:S(2)}) collective-permute-start(bf16[4,2,64,1024]{3,2,1,0:T(8,128)(2,1)} %get-tuple-element.75), channel_id=1, source_target_pairs={{0,8},{1,9},{2,10},{3,11},{4,12},{5,13},{6,14},{7,15},{8,0},{9,1},... | collective-permute-start | bytes 3145736 | tf_op jit(solution)/shard_map/ppermute | solution.py:280
  124.0 55.1 %collective-permute-start.10 = (bf16[4,2,64,1024]{3,2,1,0:T(8,128)(2,1)}, bf16[4,2,64,1024]{3,2,1,0:T(8,128)(2,1)S(1)}, u32[]{:S(2)}, u32[]{:S(2)}) collective-permute-start(bf16[4,2,64,1024]{3,2,1,0:T(8,128)(2,1)} %get-tuple-element.68), channel_id=1, source_target_pairs={{0,4},{1,5},{2,6},{3,7},{4,8},{5,9},{6,10},{7,11},{8,12},{9,13},{1... | collective-permute-start | bytes 3145736 | tf_op jit(solution)/shard_map/ppermute | solution.py:280
  126.4 49.7 %collective-permute-start.14 = (bf16[4,2,64,1024]{3,2,1,0:T(8,128)(2,1)}, bf16[4,2,64,1024]{3,2,1,0:T(8,128)(2,1)}, u32[]{:S(2)}, u32[]{:S(2)}) collective-permute-start(bf16[4,2,64,1024]{3,2,1,0:T(8,128)(2,1)} %get-tuple-element.76), channel_id=1, source_target_pairs={{0,2},{1,3},{2,0},{3,1},{4,6},{5,7},{6,4},{7,5},{8,10},{9,11},{10,... | collective-permute-start | bytes 3145736 | tf_op jit(solution)/shard_map/ppermute | solution.py:280
  126.8 52.3 %collective-permute-start.11 = (bf16[4,2,64,1024]{3,2,1,0:T(8,128)(2,1)}, bf16[4,2,64,1024]{3,2,1,0:T(8,128)(2,1)S(1)}, u32[]{:S(2)}, u32[]{:S(2)}) collective-permute-start(bf16[4,2,64,1024]{3,2,1,0:T(8,128)(2,1)} %get-tuple-element.69), channel_id=1, source_target_pairs={{0,12},{1,13},{2,14},{3,15},{4,0},{5,1},{6,2},{7,3},{8,4},{9,5},{1... | collective-permute-start | bytes 3145736 | tf_op jit(solution)/shard_map/ppermute | solution.py:280
  126.8 52.4 %collective-permute-start.12 = (bf16[4,2,64,1024]{3,2,1,0:T(8,128)(2,1)}, bf16[4,2,64,1024]{3,2,1,0:T(8,128)(2,1)S(1)}, u32[]{:S(2)}, u32[]{:S(2)}) collective-permute-start(bf16[4,2,64,1024]{3,2,1,0:T(8,128)(2,1)} %get-tuple-element.70), channel_id=1, source_target_pairs={{0,1},{1,2},{2,3},{3,0},{4,5},{5,6},{6,7},{7,4},{8,9},{9,10},{10,1... | collective-permute-start | bytes 3145736 | tf_op jit(solution)/shard_map/ppermute | solution.py:280
  147.9 37.3 %collective-permute-start.9 = (bf16[4,2,64,1024]{3,2,1,0:T(8,128)(2,1)}, bf16[4,2,64,1024]{3,2,1,0:T(8,128)(2,1)}, u32[]{:S(2)}, u32[]{:S(2)}) collective-permute-start(bf16[4,2,64,1024]{3,2,1,0:T(8,128)(2,1)} %get-tuple-element.67), channel_id=1, source_target_pairs={{0,3},{1,0},{2,1},{3,2},{4,7},{5,4},{6,5},{7,6},{8,11},{9,8},{10,9... | collective-permute-start | bytes 3145736 | tf_op jit(solution)/shard_map/ppermute | solution.py:280
  179.1 1.0 copy-start.7
  179.2 1.3 copy-start.8
  180.5 1.1 copy-start.9

commit v3 on v2

--- a/solution.py
+++ b/solution.py
@@ -13,7 +13,7 @@
 TAPS = 16
 ITERS = 3
 SHIFTS = (1, 3, 2, 0)
-VMEM = 56 * 1024 * 1024
+VMEM = 28 * 1024 * 1024
 
 
 def taps_table():
@@ -110,39 +110,45 @@
     transform(x_ref, table_ref, wide_ref, store)
 
 
-def order_kernel(recv_ref, *series_refs):
-    chans, tiles, halves, own, sub, _ = recv_ref.shape
+def order_kernel(recv_ref, series_ref):
+    chans, tiles, halves, _, sub, _ = recv_ref.shape
     rows = chans * halves * sub // 2
-    for channel in range(own):
-        for pair in range(tiles // 2):
-
-            def parts(tile):
-                both = recv_ref[:, tile, :, channel].astype(jnp.float32)
-                both = both.reshape(chans * halves, 2, sub // 2, 128)
-                return [both[:, part].reshape(rows, 128).astype(jnp.bfloat16) for part in range(2)]
-
-            first, second = parts(2 * pair), parts(2 * pair + 1)
-            lanes = slice(pair * 128, pair * 128 + 128)
-            for part in range(2):
-                low = jnp.concatenate([first[part][:, :64], second[part][:, :64]], axis=1)
-                high = jnp.concatenate([first[part][:, 64:], second[part][:, 64:]], axis=1)
-                start = 2 * part * rows
-                series_refs[channel][start : start + rows, lanes] = low
-                series_refs[channel][start + rows : start + 2 * rows, lanes] = high
-
-
-def form_sums(series_ref, tiles, outs, slot):
-    samples, inputs = series_ref.shape
+    for pair in range(tiles // 2):
+
+        def parts(tile):
+            both = recv_ref[:, tile, :, 0].astype(jnp.float32)
+            both = both.reshape(chans * halves, 2, sub // 2, 128)
+            return [both[:, part].reshape(rows, 128).astype(jnp.bfloat16) for part in range(2)]
+
+        first, second = parts(2 * pair), parts(2 * pair + 1)
+        lanes = slice(pair * 128, pair * 128 + 128)
+        for part in range(2):
+            low = jnp.concatenate([first[part][:, :64], second[part][:, :64]], axis=1)
+            high = jnp.concatenate([first[part][:, 64:], second[part][:, 64:]], axis=1)
+            start = 2 * part * rows
+            series_ref[start : start + rows, lanes] = low
+            series_ref[start + rows : start + 2 * rows, lanes] = high
+
+
+def form_sums(series_refs, tiles, outs, slot):
+    inputs = series_refs[0].shape[1]
+    samples = len(series_refs) * series_refs[0].shape[0] // 2
     rows = inputs // 16
     left = []
     for tile in tiles:
-        across = series_ref[:, pl.ds(pl.multiple_of(tile // 2 * 128, 128), 128)].T
+        lanes = pl.ds(pl.multiple_of(tile // 2 * 128, 128), 128)
+        across = jnp.concatenate([ref[:, lanes].T for ref in series_refs], axis=1)
         left.append(jnp.where(tile % 2 == 0, across[:rows], across[rows:]))
     left = jnp.concatenate(left, axis=0)
+    turned = jnp.concatenate([left[:, samples:], -left[:, :samples]], axis=1)
+    both = jnp.concatenate([left, turned], axis=0)
+    sums, start = 0.0, 0
+    for ref in series_refs:
+        depth = ref.shape[0]
+        sums = sums + jnp.dot(both[:, start : start + depth], ref[...], preferred_element_type=jnp.float32)
+        start += depth
+    sums = sums * (1.0 / samples)
     count = left.shape[0]
-    turned = jnp.concatenate([left[:, samples // 2 :], -left[:, : samples // 2]], axis=1)
-    both = jnp.concatenate([left, turned], axis=0)
-    sums = jnp.dot(both, series_ref[...], preferred_element_type=jnp.float32) * (2.0 / samples)
     for n, out_ref in enumerate(outs):
         for part in range(2):
             start = part * count + n * rows
@@ -156,42 +162,49 @@
     return [x * 4 + (y + shift) % 4 for shift in shifts]
 
 
-def own_kernel(position_ref, first_ref, second_ref, *outs):
-    for axis, series_ref in enumerate((first_ref, second_ref)):
-        form_sums(series_ref, row_tiles(position_ref, axis, SHIFTS), outs[4 * axis : 4 * axis + 4], 0)
-
-
-def near_kernel(position_ref, *refs):
-    series, outs = refs[:4], refs[12:]
+def split_kernel(*refs):
+    rows = refs[4].shape[0]
+    for n in range(4):
+        start = n % 2 * rows
+        refs[4 + n][...] = refs[n][start : start + rows, :]
+
+
+def main_kernel(position_ref, *refs):
+    series, outs = refs[:6], refs[6:]
     for axis in range(2):
         tiles = row_tiles(position_ref, axis, SHIFTS)
-        for slot in range(2):
-            form_sums(series[2 * axis + slot], tiles, outs[4 * axis : 4 * axis + 4], slot)
-
-
-def far_kernel(shifts, position_ref, *refs):
-    halves, outs, series_ref = refs[:4], refs[8:12], refs[12]
+        for slot in range(3):
+            form_sums([series[3 * axis + slot]], tiles, outs[4 * axis : 4 * axis + 4], slot)
+
+
+def far_kernel(position_ref, *refs):
+    halves, blocks, outs = refs[:4], refs[4:12], refs[12:]
     for axis in range(2):
-        rows = halves[0].shape[0]
-        series_ref[axis, 0:rows, :] = halves[2 * axis][...]
-        series_ref[axis, rows : 2 * rows, :] = halves[2 * axis + 1][...]
-        tiles = row_tiles(position_ref, axis, shifts)
-        form_sums(series_ref.at[axis], tiles, outs[2 * axis : 2 * axis + 2], 0)
+        tiles = row_tiles(position_ref, axis, SHIFTS)
+        form_sums(halves[2 * axis : 2 * axis + 2], tiles, outs[4 * axis : 4 * axis + 4], 3)
+    for block_ref, out_ref in zip(blocks, outs):
+        out_ref[0:3] = block_ref[...]
 
 
 def place_kernel(moves, position_ref, *refs):
-    out_ref, sems = refs[-2:]
+    out_ref, held, in_sems, out_sems = refs[-2 - len(moves) - 1], refs[-2 - len(moves) : -2], refs[-2], refs[-1]
     x, y = position_ref[0] // 4, position_ref[0] % 4
+    loads = []
+    for n, part_ref in enumerate(refs[: len(moves)]):
+        load = pltpu.make_async_copy(part_ref, held[n], in_sems.at[n])
+        load.start()
+        loads.append(load)
     copies = []
-    for (axis, shift), part_ref in zip(moves, refs):
-        for slot, step in enumerate((0, 2, 3, 1)):
+    for n, (axis, shift) in enumerate(moves):
+        loads[n].wait()
+        for slot, step in enumerate((3, 1, 0, 2)):
             if axis == 0:
                 owner = (x + 4 - shift) % 4 * 4 + (y + step) % 4
             else:
                 owner = (x + step) % 4 * 4 + (y + 4 - shift) % 4
             for part in range(2):
                 copy = pltpu.make_async_copy(
-                    part_ref.at[slot, part], out_ref.at[part, owner * 2 + axis], sems.at[len(copies)]
+                    held[n].at[slot, part], out_ref.at[part, owner * 2 + axis], out_sems.at[len(copies)]
                 )
                 copy.start()
                 copies.append(copy)
@@ -201,10 +214,12 @@
 
 def gains_kernel(first_ref, second_ref, flags_ref, out_ref):
     keep = (1 - flags_ref[...]).astype(jnp.float32)
+    out_ref[...] = jnp.zeros_like(out_ref)
     for channel, series_ref in enumerate((first_ref, second_ref)):
-        gain_real, gain_imag = stefcal(series_ref, keep)
-        out_ref[channel, 0:1, :] = gain_real
-        out_ref[channel, 1:2, :] = gain_imag
+        for part, gain in enumerate(stefcal(series_ref, keep)):
+            for tile in range(16):
+                place = part * 2 + channel
+                out_ref[tile, place : place + 1, 0:64] = gain[:, tile * 64 : tile * 64 + 64]
 
 
 def stefcal(series_ref, keep):
@@ -285,12 +300,14 @@
     anywhere = pl.BlockSpec(memory_space=pl.ANY)
     return pl.pallas_call(
         functools.partial(place_kernel, moves),
-        in_specs=[pl.BlockSpec(memory_space=pltpu.SMEM)]
-        + [pl.BlockSpec(memory_space=pltpu.VMEM)] * len(parts)
-        + [anywhere] * (len(operands) - len(parts)),
+        in_specs=[pl.BlockSpec(memory_space=pltpu.SMEM)] + [anywhere] * len(operands),
         out_specs=anywhere,
         out_shape=out_shape,
-        scratch_shapes=[pltpu.SemaphoreType.DMA((8 * len(parts),))],
+        scratch_shapes=[pltpu.VMEM(part.shape, part.dtype) for part in parts]
+        + [
+            pltpu.SemaphoreType.DMA((len(parts),)),
+            pltpu.SemaphoreType.DMA((8 * len(parts),)),
+        ],
         input_output_aliases={} if previous is None else {len(operands): 0},
         compiler_params=params(),
         cost_estimate=cost(0, len(parts) << 21),
@@ -338,94 +355,79 @@
 
     turned = lax.all_to_all(spectra, ("chan", "tile"), split_axis=0, concat_axis=0, tiled=True)
     turned = turned.reshape(chan_count, tile_count, 2, own, sub, 128)
-    series_shape = jax.ShapeDtypeStruct((2 * samples, inputs), jnp.bfloat16)
-    series = pl.pallas_call(
-        order_kernel,
-        out_shape=[series_shape] * own,
-        compiler_params=params(),
-        cost_estimate=cost(1e6, 4 << 20),
-        name="order",
-    )(turned)
+    series = [
+        pl.pallas_call(
+            order_kernel,
+            grid=(1,),
+            in_specs=[
+                pl.BlockSpec(
+                    (chan_count, tile_count, 2, 1, sub, 128), lambda i, channel=channel: (0, 0, 0, channel, 0, 0)
+                )
+            ],
+            out_specs=pl.BlockSpec((2 * samples, inputs), lambda i: (0, 0)),
+            out_shape=jax.ShapeDtypeStruct((2 * samples, inputs), jnp.bfloat16),
+            compiler_params=params(),
+            cost_estimate=cost(1e6, 2 << 20),
+            name="order",
+        )(turned)
+        for channel in range(own)
+    ]
 
     position = lax.axis_index("tile").astype(jnp.int32).reshape(1)
     smem = pl.BlockSpec(memory_space=pltpu.SMEM)
-    block_shape = jax.ShapeDtypeStruct((4, 2, row_count, inputs), jnp.bfloat16)
-    anywhere = pl.BlockSpec(memory_space=pl.ANY)
-
-    def slots(count, index):
-        return pl.BlockSpec((count, 2, row_count, inputs), lambda i: (index, 0, 0, 0))
-
-    def whole(shape):
-        return pl.BlockSpec(shape, lambda i: (0,) * len(shape))
-
+    vmem = pl.BlockSpec(memory_space=pltpu.VMEM)
     flops = 8 * 4 * row_count * inputs * samples
     up = [turn(series[axis], 1 - axis, 1) for axis in range(2)]
     down = [turn(series[axis], 1 - axis, 3) for axis in range(2)]
-    blocks = pl.pallas_call(
-        own_kernel,
-        grid=(1,),
-        in_specs=[smem] + [whole((2 * samples, inputs))] * 2,
-        out_specs=[slots(1, 0)] * 8,
-        out_shape=[block_shape] * 8,
-        compiler_params=params(),
-        cost_estimate=cost(2 * flops, 4 << 20),
-        name="own_sums",
-    )(position, *series)
     gains = pl.pallas_call(
         gains_kernel,
-        in_specs=[pl.BlockSpec(memory_space=pltpu.VMEM)] * 3,
-        out_specs=pl.BlockSpec(memory_space=pltpu.VMEM),
-        out_shape=jax.ShapeDtypeStruct((own, 2, inputs), jnp.float32),
+        in_specs=[vmem] * 3,
+        out_specs=vmem,
+        out_shape=jax.ShapeDtypeStruct((tile_count, 8, 128), jnp.float32),
         compiler_params=params(),
         cost_estimate=cost(own * inputs * samples * 64, 2 << 20),
         name="gains",
     )(*series, flags.reshape(1, inputs))
-    up, down, blocks, gains = lax.optimization_barrier((up, down, blocks, gains))
-
-    far = []
-    for axis in range(2):
-        far.append(turn(up[axis][:samples], 1 - axis, 1))
-        far.append(turn(down[axis][samples:], 1 - axis, 3))
+    gains = lax.all_to_all(gains, "tile", split_axis=0, concat_axis=0, tiled=True)
+    up, down, gains = lax.optimization_barrier((up, down, gains))
+    half_shape = jax.ShapeDtypeStruct((samples, inputs), jnp.bfloat16)
+    parts = pl.pallas_call(
+        split_kernel,
+        in_specs=[vmem] * 4,
+        out_specs=[vmem] * 4,
+        out_shape=[half_shape] * 4,
+        compiler_params=params(),
+        cost_estimate=cost(0, 4 << 20),
+        name="split",
+    )(up[0], down[0], up[1], down[1])
+    far = [turn(parts[n], 1 - n // 2, (1, 3)[n % 2]) for n in range(4)]
     blocks = pl.pallas_call(
-        near_kernel,
-        grid=(1,),
-        in_specs=[smem] + [whole((2 * samples, inputs))] * 4 + [anywhere] * 8,
-        out_specs=[slots(2, 1)] * 8,
-        out_shape=[block_shape] * 8,
-        input_output_aliases={5 + n: n for n in range(8)},
-        compiler_params=params(),
-        cost_estimate=cost(4 * flops, 8 << 20),
-        name="near_sums",
-    )(position, up[0], down[0], up[1], down[1], *blocks)
-
-    def far_sums(shifts, chosen):
-        return pl.pallas_call(
-            functools.partial(far_kernel, shifts),
-            grid=(1,),
-            in_specs=[smem] + [whole((samples, inputs))] * 4 + [anywhere] * 4,
-            out_specs=[slots(1, 1)] * 4,
-            out_shape=[block_shape] * 4,
-            scratch_shapes=[pltpu.VMEM((2, 2 * samples, inputs), jnp.bfloat16)],
-            input_output_aliases={5 + n: n for n in range(4)},
-            compiler_params=params(),
-            cost_estimate=cost(flops, 6 << 20),
-            name="far_sums",
-        )(position, *far, *chosen)
-
-    two = far_sums((2, 0), [blocks[n] for n in (2, 3, 6, 7)])
-    one = far_sums((1, 3), [blocks[n] for n in (0, 1, 4, 5)])
-    last = [turn(two[0], 0, 2), turn(two[2], 1, 2)]
-    sent = [turn(one[0], 0, 1), turn(one[1], 0, 3), turn(one[2], 1, 1), turn(one[3], 1, 3)]
+        main_kernel,
+        in_specs=[smem] + [vmem] * 6,
+        out_specs=[vmem] * 8,
+        out_shape=[jax.ShapeDtypeStruct((3, 2, row_count, inputs), jnp.bfloat16)] * 8,
+        compiler_params=params(),
+        cost_estimate=cost(6 * flops, 12 << 20),
+        name="main_sums",
+    )(position, up[0], down[0], series[0], up[1], down[1], series[1])
+    blocks = pl.pallas_call(
+        far_kernel,
+        in_specs=[smem] + [vmem] * 12,
+        out_specs=[vmem] * 8,
+        out_shape=[jax.ShapeDtypeStruct((4, 2, row_count, inputs), jnp.bfloat16)] * 8,
+        compiler_params=params(),
+        cost_estimate=cost(2 * flops, 16 << 20),
+        name="far_sums",
+    )(position, *far, *blocks)
+
+    moves = [(axis, shift) for shift in (2, 1, 3) for axis in range(2)]
+    sent = [turn(blocks[4 * axis + SHIFTS.index(shift)], axis, shift) for axis, shift in moves]
 
     out_shape = jax.ShapeDtypeStruct((2, tile_count * own, row_count, inputs), jnp.bfloat16)
-    visibilities = place(position, [two[1], two[3]], [(0, 0), (1, 0)], out_shape)
-    visibilities = place(position, last, [(0, 2), (1, 2)], out_shape, visibilities)
-    visibilities = place(position, sent[:3], [(0, 1), (0, 3), (1, 1)], out_shape, visibilities)
-    visibilities = place(position, sent[3:], [(1, 3)], out_shape, visibilities)
-
-    gains = gains.reshape(own, 2, tile_count, row_count).transpose(2, 1, 0, 3)
-    gains = lax.all_to_all(gains, "tile", split_axis=0, concat_axis=0, tiled=True)
-    gains = gains.transpose(1, 0, 2, 3).reshape(2, tile_count * own, row_count)
+    visibilities = place(position, [blocks[3], blocks[7]], [(0, 0), (1, 0)], out_shape)
+    visibilities = place(position, sent, moves, out_shape, visibilities)
+    gains = gains[:, : 2 * own, :row_count].reshape(tile_count, 2, own, row_count).transpose(1, 0, 2, 3)
+    gains = gains.reshape(2, tile_count * own, row_count)
     return (visibilities, gains)
 
 

time: 190 us -> 167 us (0.88)
  Pallas kernels: 53.1 us -> 27.9 us
  waiting for transfers between devices: 37.9 us -> 43.8 us
  blocking collectives: 68.2 us -> 64.4 us
    pallas_call x6, Pallas kernels: 27.3 us -> 15.1 us  [the longest x1 5.92 us: body(): pl.pallas_call(gains_kernel, in_specs=[vmem] * 3, out_specs=vmem, out_sha...]
    pallas_call x4 -> x2, Pallas kernels: 11.9 us -> 5.11 us  [place(): pl.pallas_call(functools.partial(place_kernel, moves), in_specs=[pl.Block...]
    ppermute x14, waiting for transfers between devices: 37.9 us -> 43.8 us  [turn(): return lax.ppermute(value, 'tile', pairs)]
    pallas_call x1, Pallas kernels: 7.43 us -> 3.87 us  [body(): pl.pallas_call(early_kernel, out_shape=jax.ShapeDtypeStruct((device_count...]
    unnamed x27 -> x20, local copies, waits for them, and re-layouts: 4.96 us -> 7.76 us
    all_to_all x1, blocking collectives: 22.4 us -> 19.8 us  [body(): lax.all_to_all(gains, 'tile', split_axis=0, concat_axis=0, tiled=True)]
    pallas_call x1, Pallas kernels: 6.37 us -> 3.78 us  [body(): pl.pallas_call(late_kernel, out_shape=jax.ShapeDtypeStruct((device_count,...]
  transfers between devices with their start and end apart: 15 -> 15, of which waited for: 7 -> 6; matrix products, arithmetic and copies ran while one was open for 2% -> 0% of each run, Pallas kernels for 20% -> 9%
where the time goes in v3:
time: 167 us; the launch traced here: 165 us
  blocking collectives  64.4 us (39%)
  waiting for transfers between devices  43.8 us (26%)
  Pallas kernels  27.9 us (17%)
  starting transfers between devices  18.4 us (11%)
  local copies, waits for them, and re-layouts  9.66 us (6%)
    all_to_all x1, blocking collectives, body(): lax.all_to_all(spectra, ('chan', 'tile'), split_axis=0, concat_axis=0, ti...  44.7 us
    ppermute x14, waiting for transfers between devices, turn(): return lax.ppermute(value, 'tile', pairs)  43.8 us
    all_to_all x1, blocking collectives, body(): lax.all_to_all(gains, 'tile', split_axis=0, concat_axis=0, tiled=True)  19.8 us
    ppermute x14, starting transfers between devices, turn(): return lax.ppermute(value, 'tile', pairs)  16.6 us
    unnamed x20, local copies, waits for them, and re-layouts  7.76 us
    pallas_call x1, Pallas kernels, body(): pl.pallas_call(gains_kernel, in_specs=[vmem] * 3, out_specs=vmem, out_sha...  5.92 us
    pallas_call x2, Pallas kernels, place(): pl.pallas_call(functools.partial(place_kernel, moves), in_specs=[pl.Block...  5.11 us
    pallas_call x1, Pallas kernels, body(): pl.pallas_call(early_kernel, out_shape=jax.ShapeDtypeStruct((device_count...  3.87 us
  transfers between devices with their start and end apart: 15, of which 6 were waited for; matrix products, arithmetic and copies ran while one was open for 0% of the time, Pallas kernels for 9%

profile of v3, /device:TPU:6, one launch (start us, length us, event | category | flops | bytes accessed | tf_op | source)
XLA Modules:
  0.0 165.2 jit_solution(15496096376766732520)
XLA Ops:
  0.6 1.3 slice.6
  1.9 1.8 %collective-permute-start = (bf16[2,64,3840]{2,1,0:T(8,128)(2,1)S(1)}, bf16[2,64,3840]{2,1,0:T(8,128)(2,1)S(1)}, u32[]{:S(2)}, u32[]{:S(2)}) collective-permute-start(bf16[2,64,3840]{2,1,0:T(8,128)(2,1)S(1)} %slice.6), channel_id=1, source_target_pairs={{0,16},{16,32},{32,48},{48,64},{64,80},{80,96},{96,112},{1,17},{17... | collective-permute-start | bytes 2949128 | tf_op jit(solution)/shard_map/ppermute | solution.py:336
  3.7 1.6 copy-done
  5.3 1.0 copy-done.7
  6.3 0.7 copy-done.8
  7.1 3.8 %late_spectra.1.late_ref = bf16[128,2,16,128]{3,2,1,0:T(8,128)(2,1)S(1)} custom-call(bf16[2,64,8192]{2,1,0:T(8,128)(2,1)S(1)} %copy-done, f32[16,256]{1,0:T(8,128)S(1)} %copy-done.8, bf16[512,512]{1,0:T(8,128)(2,1)S(1)} %copy-done.7), custom_call_target="tpu_custom_call" | custom-call | flops 1500000000 | bytes 4194304 | tf_op jit(solution)/shard_map/late_spectra/pallas_call | solution.py:339
  10.9 3.9 %early_spectra.1 = bf16[128,2,2,16,128]{4,3,2,1,0:T(8,128)(2,1)S(1)} custom-call(bf16[2,64,8192]{2,1,0:T(8,128)(2,1)S(1)} %copy-done, bf16[2,64,3840]{2,1,0:T(8,128)(2,1)S(1)} %collective-permute-done.h_ref, bf16[128,2,16,128]{3,2,1,0:T(8,128)(2,1)S(1)} %late_spectra.1.late_ref, f32[16,256]{1,0:T(8,128)S(1)} %copy-done.8, bf16[512,512]{1,0:T(8,128)(2,1)S(1)} %copy-done.7), custom_call_target="tpu_custom_call" | custom-call | flops 1500000000 | bytes 6291456 | tf_op jit(solution)/shard_map/early_spectra/pallas_call | solution.py:347
  14.7 44.7 %all_to_all.10 = bf16[128,2,2,16,128]{4,3,2,1,0:T(8,128)(2,1)S(1)} all-to-all(bf16[128,2,2,16,128]{4,3,2,1,0:T(8,128)(2,1)S(1)} %early_spectra.1), channel_id=1, replica_groups=mesh['chan'=8,'tile'=16] {'chan','tile'}, dimensions={0} | all-to-all | bytes 4194304 | tf_op jit(solution)/shard_map/all_to_all | solution.py:356
  60.3 2.8 %collective-permute-start.3 = (bf16[512,1024]{1,0:T(8,128)(2,1)S(1)}, bf16[512,1024]{1,0:T(8,128)(2,1)S(1)}, u32[]{:S(2)}, u32[]{:S(2)}) collective-permute-start(bf16[512,1024]{1,0:T(8,128)(2,1)S(1)} %order.2.first_ref.refs_2_), channel_id=1, source_target_pairs={{0,3},{1,0},{2,1},{3,2},{4,7},{5,4},{6,5},{7,6},{8,11},{9,8},{10,9... | collective-permute-start | bytes 3145736 | tf_op jit(solution)/shard_map/ppermute | solution.py:295
  63.1 1.1 collective-permute-start.4
  64.2 2.2 %collective-permute-start.2 = (bf16[512,1024]{1,0:T(8,128)(2,1)S(1)}, bf16[512,1024]{1,0:T(8,128)(2,1)S(1)}, u32[]{:S(2)}, u32[]{:S(2)}) collective-permute-start(bf16[512,1024]{1,0:T(8,128)(2,1)S(1)} %order.3.second_ref.refs_5_), channel_id=1, source_target_pairs={{0,4},{1,5},{2,6},{3,7},{4,8},{5,9},{6,10},{7,11},{8,12},{9,13},{1... | collective-permute-start | bytes 3145736 | tf_op jit(solution)/shard_map/ppermute | solution.py:295
  66.3 5.9 %gains.1 = f32[16,8,128]{2,1,0:T(8,128)S(1)} custom-call(bf16[512,1024]{1,0:T(8,128)(2,1)S(1)} %order.2.first_ref.refs_2_, bf16[512,1024]{1,0:T(8,128)(2,1)S(1)} %order.3.second_ref.refs_5_, s32[1,1024]{1,0:T(1,128)S(1)} %bitcast.9), custom_call_target="tpu_custom_call" | custom-call | flops 33554432 | bytes 2097152 | tf_op jit(solution)/shard_map/gains/pallas_call | solution.py:382
  72.2 19.8 %all_to_all.11 = f32[16,8,128]{2,1,0:T(8,128)S(1)} all-to-all(f32[16,8,128]{2,1,0:T(8,128)S(1)} %gains.1), channel_id=1, replica_groups=mesh['chan'=8,'tile'=16] {'tile'}, dimensions={0} | all-to-all | bytes 131072 | tf_op jit(solution)/shard_map/all_to_all | solution.py:391
  92.0 1.6 split.1
  95.0 2.6 %collective-permute-start.6 = (bf16[256,1024]{1,0:T(8,128)(2,1)}, bf16[256,1024]{1,0:T(8,128)(2,1)}, u32[]{:S(2)}, u32[]{:S(2)}) collective-permute-start(bf16[256,1024]{1,0:T(8,128)(2,1)} %get-tuple-element.32), channel_id=1, source_target_pairs={{0,3},{1,0},{2,1},{3,2},{4,7},{5,4},{6,5},{7,6},{8,11},{9,8},{10,9... | collective-permute-start | bytes 1572872 | tf_op jit(solution)/shard_map/ppermute | solution.py:295
  97.6 2.4 %collective-permute-start.7 = (bf16[256,1024]{1,0:T(8,128)(2,1)}, bf16[256,1024]{1,0:T(8,128)(2,1)}, u32[]{:S(2)}, u32[]{:S(2)}) collective-permute-start(bf16[256,1024]{1,0:T(8,128)(2,1)} %get-tuple-element.33), channel_id=1, source_target_pairs={{0,4},{1,5},{2,6},{3,7},{4,8},{5,9},{6,10},{7,11},{8,12},{9,13},{1... | collective-permute-start | bytes 1572872 | tf_op jit(solution)/shard_map/ppermute | solution.py:295
  100.0 1.2 copy-done.2
  101.2 1.2 copy-done.4
  102.4 1.2 copy-done.6
  103.7 3.6 %main_sums.1 = (bf16[3,2,64,1024]{3,2,1,0:T(8,128)(2,1)S(1)}, bf16[3,2,64,1024]{3,2,1,0:T(8,128)(2,1)S(1)}, bf16[3,2,64,1024]{3,2,1,0:T(8,128)(2,1)S(1)}, bf16[3...) custom-call(s32[1]{0:T(128)} %bitcast.position_ref, ...), custom_call_target="tpu_custom_call" | custom-call | flops 3221225472 | bytes 12582912 | tf_op jit(solution)/shard_map/main_sums/pallas_call | solution.py:404
  107.2 1.1 collective-permute-done.5.refs_0_
  108.3 1.5 collective-permute-done.7.refs_2_
  109.8 2.0 %collective-permute-done.8.refs_3_ = bf16[256,1024]{1,0:T(8,128)(2,1)} collective-permute-done((bf16[256,1024]{1,0:T(8,128)(2,1)}, bf16[256,1024]{1,0:T(8,128)(2,1)}, u32[]{:S(2)}, u32[]{:S(2)}) %collective-permute-start.8) | collective-permute-done | bytes 524320 | tf_op jit(solution)/shard_map/ppermute | solution.py:295
  111.7 3.2 %far_sums.1 = (bf16[4,2,64,1024]{3,2,1,0:T(8,128)(2,1)S(1)}, bf16[4,2,64,1024]{3,2,1,0:T(8,128)(2,1)S(1)}, bf16[4,2,64,1024]{3,2,1,0:T(8,128)(2,1)S(1)}, bf16[4,...) custom-call(s32[1]{0:T(128)} %bitcast.position_ref, ...), custom_call_target="tpu_custom_call" | custom-call | flops 1073741824 | bytes 16777216 | tf_op jit(solution)/shard_map/far_sums/pallas_call | solution.py:413
  115.0 1.0 collective-permute-start.9
  116.5 1.7 %collective-permute-start.11 = (bf16[4,2,64,1024]{3,2,1,0:T(8,128)(2,1)S(1)}, bf16[4,2,64,1024]{3,2,1,0:T(8,128)(2,1)S(1)}, u32[]{:S(2)}, u32[]{:S(2)}) collective-permute-start(bf16[4,2,64,1024]{3,2,1,0:T(8,128)(2,1)S(1)} %get-tuple-element.45), channel_id=1, source_target_pairs={{0,4},{1,5},{2,6},{3,7},{4,8},{5,9},{6,10},{7,11},{8,12},{9,13},{1... | collective-permute-start | bytes 3145736 | tf_op jit(solution)/shard_map/ppermute | solution.py:295
  118.2 1.1 collective-permute-start.12
  119.3 23.4 %collective-permute-done.9.refs_0_ = bf16[4,2,64,1024]{3,2,1,0:T(8,128)(2,1)S(1)} collective-permute-done((bf16[4,2,64,1024]{3,2,1,0:T(8,128)(2,1)S(1)}, bf16[4,2,64,1024]{3,2,1,0:T(8,128)(2,1)S(1)}, u32[]{:S(2)}, u32[]{:S(2)}) %collective-permute-start.9) | collective-permute-done | bytes 1048608 | tf_op jit(solution)/shard_map/ppermute | solution.py:295
  144.1 1.6 place.2.refs_6_
  145.7 12.4 %collective-permute-done.11.refs_2_ = bf16[4,2,64,1024]{3,2,1,0:T(8,128)(2,1)S(1)} collective-permute-done((bf16[4,2,64,1024]{3,2,1,0:T(8,128)(2,1)S(1)}, bf16[4,2,64,1024]{3,2,1,0:T(8,128)(2,1)S(1)}, u32[]{:S(2)}, u32[]{:S(2)}) %collective-permute-start.11) | collective-permute-done | bytes 1048608 | tf_op jit(solution)/shard_map/ppermute | solution.py:295
  158.1 3.5 %collective-permute-done.12.refs_3_ = bf16[4,2,64,1024]{3,2,1,0:T(8,128)(2,1)S(1)} collective-permute-done((bf16[4,2,64,1024]{3,2,1,0:T(8,128)(2,1)S(1)}, bf16[4,2,64,1024]{3,2,1,0:T(8,128)(2,1)S(1)}, u32[]{:S(2)}, u32[]{:S(2)}) %collective-permute-start.12) | collective-permute-done | bytes 1048608 | tf_op jit(solution)/shard_map/ppermute | solution.py:295
  161.6 3.5 %place.3 = bf16[2,32,64,1024]{3,2,1,0:T(8,128)(2,1)} custom-call(s32[1]{0:T(128)} %bitcast.position_ref, bf16[4,2,64,1024]{3,2,1,0:T(8,128)(2,1)S(1)} %collective-permute-done.9.refs_0_, bf16[4,2,64,1024]{3,2,1,0:T(8,128)(2,1)S(1)} %collective-permute-done.10.refs_1_, ...), custom_call_target="tpu_custom_call", output_to_operand_aliasing={{}: (7, {})} | custom-call | bytes 12582912 | tf_op jit(solution)/shard_map/place/pallas_call | solution.py:301
  (33 shorter events, 4.1 us)
Async XLA Ops:
  1.9 8.9 %collective-permute-start = (bf16[2,64,3840]{2,1,0:T(8,128)(2,1)S(1)}, bf16[2,64,3840]{2,1,0:T(8,128)(2,1)S(1)}, u32[]{:S(2)}, u32[]{:S(2)}) collective-permute-start(bf16[2,64,3840]{2,1,0:T(8,128)(2,1)S(1)} %slice.6), channel_id=1, source_target_pairs={{0,16},{16,32},{32,48},{48,64},{64,80},{80,96},{96,112},{1,17},{17... | collective-permute-start | bytes 2949128 | tf_op jit(solution)/shard_map/ppermute | solution.py:336
  3.7 1.6 copy-start
  5.3 1.0 copy-start.7
  6.3 0.7 copy-start.8
  59.9 6.5 %copy-start.9 = (s32[1024]{0:T(1024)S(1)}, s32[1024]{0:T(1024)}, u32[]{:S(2)}) copy-start(s32[1024]{0:T(1024)} %param.5) | copy-start | bytes 12292
  60.3 31.7 %collective-permute-start.3 = (bf16[512,1024]{1,0:T(8,128)(2,1)S(1)}, bf16[512,1024]{1,0:T(8,128)(2,1)S(1)}, u32[]{:S(2)}, u32[]{:S(2)}) collective-permute-start(bf16[512,1024]{1,0:T(8,128)(2,1)S(1)} %order.2.first_ref.refs_2_), channel_id=1, source_target_pairs={{0,3},{1,0},{2,1},{3,2},{4,7},{5,4},{6,5},{7,6},{8,11},{9,8},{10,9... | collective-permute-start | bytes 3145736 | tf_op jit(solution)/shard_map/ppermute | solution.py:295
  63.1 28.9 %collective-permute-start.1 = (bf16[512,1024]{1,0:T(8,128)(2,1)S(1)}, bf16[512,1024]{1,0:T(8,128)(2,1)S(1)}, u32[]{:S(2)}, u32[]{:S(2)}) collective-permute-start(bf16[512,1024]{1,0:T(8,128)(2,1)S(1)} %order.2.first_ref.refs_2_), channel_id=1, source_target_pairs={{0,1},{1,2},{2,3},{3,0},{4,5},{5,6},{6,7},{7,4},{8,9},{9,10},{10,1... | collective-permute-start | bytes 3145736 | tf_op jit(solution)/shard_map/ppermute | solution.py:295
  63.1 28.9 %collective-permute-start.4 = (bf16[512,1024]{1,0:T(8,128)(2,1)S(1)}, bf16[512,1024]{1,0:T(8,128)(2,1)S(1)}, u32[]{:S(2)}, u32[]{:S(2)}) collective-permute-start(bf16[512,1024]{1,0:T(8,128)(2,1)S(1)} %order.3.second_ref.refs_5_), channel_id=1, source_target_pairs={{0,12},{1,13},{2,14},{3,15},{4,0},{5,1},{6,2},{7,3},{8,4},{9,5},{1... | collective-permute-start | bytes 3145736 | tf_op jit(solution)/shard_map/ppermute | solution.py:295
  64.2 27.9 %collective-permute-start.2 = (bf16[512,1024]{1,0:T(8,128)(2,1)S(1)}, bf16[512,1024]{1,0:T(8,128)(2,1)S(1)}, u32[]{:S(2)}, u32[]{:S(2)}) collective-permute-start(bf16[512,1024]{1,0:T(8,128)(2,1)S(1)} %order.3.second_ref.refs_5_), channel_id=1, source_target_pairs={{0,4},{1,5},{2,6},{3,7},{4,8},{5,9},{6,10},{7,11},{8,12},{9,13},{1... | collective-permute-start | bytes 3145736 | tf_op jit(solution)/shard_map/ppermute | solution.py:295
  92.0 1.6 copy-start.1
  92.0 1.9 %copy-start.3 = (bf16[512,1024]{1,0:T(8,128)(2,1)}, bf16[512,1024]{1,0:T(8,128)(2,1)S(1)}, u32[]{:S(2)}) copy-start(bf16[512,1024]{1,0:T(8,128)(2,1)S(1)} %collective-permute-done.4.refs_3_.refs_4_) | copy-start | bytes 3145732
  92.0 2.3 %copy-start.5 = (bf16[512,1024]{1,0:T(8,128)(2,1)}, bf16[512,1024]{1,0:T(8,128)(2,1)S(1)}, u32[]{:S(2)}) copy-start(bf16[512,1024]{1,0:T(8,128)(2,1)S(1)} %collective-permute-done.2.refs_2_.refs_3_) | copy-start | bytes 3145732
  94.4 13.9 %collective-permute-start.5 = (bf16[256,1024]{1,0:T(8,128)(2,1)}, bf16[256,1024]{1,0:T(8,128)(2,1)}, u32[]{:S(2)}, u32[]{:S(2)}) collective-permute-start(bf16[256,1024]{1,0:T(8,128)(2,1)} %get-tuple-element.31), channel_id=1, source_target_pairs={{0,1},{1,2},{2,3},{3,0},{4,5},{5,6},{6,7},{7,4},{8,9},{9,10},{10,1... | collective-permute-start | bytes 1572872 | tf_op jit(solution)/shard_map/ppermute | solution.py:295
  95.0 13.3 %collective-permute-start.6 = (bf16[256,1024]{1,0:T(8,128)(2,1)}, bf16[256,1024]{1,0:T(8,128)(2,1)}, u32[]{:S(2)}, u32[]{:S(2)}) collective-permute-start(bf16[256,1024]{1,0:T(8,128)(2,1)} %get-tuple-element.32), channel_id=1, source_target_pairs={{0,3},{1,0},{2,1},{3,2},{4,7},{5,4},{6,5},{7,6},{8,11},{9,8},{10,9... | collective-permute-start | bytes 1572872 | tf_op jit(solution)/shard_map/ppermute | solution.py:295
  97.6 12.2 %collective-permute-start.7 = (bf16[256,1024]{1,0:T(8,128)(2,1)}, bf16[256,1024]{1,0:T(8,128)(2,1)}, u32[]{:S(2)}, u32[]{:S(2)}) collective-permute-start(bf16[256,1024]{1,0:T(8,128)(2,1)} %get-tuple-element.33), channel_id=1, source_target_pairs={{0,4},{1,5},{2,6},{3,7},{4,8},{5,9},{6,10},{7,11},{8,12},{9,13},{1... | collective-permute-start | bytes 1572872 | tf_op jit(solution)/shard_map/ppermute | solution.py:295
  100.0 11.8 %collective-permute-start.8 = (bf16[256,1024]{1,0:T(8,128)(2,1)}, bf16[256,1024]{1,0:T(8,128)(2,1)}, u32[]{:S(2)}, u32[]{:S(2)}) collective-permute-start(bf16[256,1024]{1,0:T(8,128)(2,1)} %get-tuple-element.34), channel_id=1, source_target_pairs={{0,12},{1,13},{2,14},{3,15},{4,0},{5,1},{6,2},{7,3},{8,4},{9,5},{1... | collective-permute-start | bytes 1572872 | tf_op jit(solution)/shard_map/ppermute | solution.py:295
  100.0 1.2 copy-start.2
  101.2 1.2 copy-start.4
  102.4 1.2 copy-start.6
  115.0 27.7 %collective-permute-start.9 = (bf16[4,2,64,1024]{3,2,1,0:T(8,128)(2,1)S(1)}, bf16[4,2,64,1024]{3,2,1,0:T(8,128)(2,1)S(1)}, u32[]{:S(2)}, u32[]{:S(2)}) collective-permute-start(bf16[4,2,64,1024]{3,2,1,0:T(8,128)(2,1)S(1)} %get-tuple-element.43), channel_id=1, source_target_pairs={{0,8},{1,9},{2,10},{3,11},{4,12},{5,13},{6,14},{7,15},{8,0},{9,1},... | collective-permute-start | bytes 3145736 | tf_op jit(solution)/shard_map/ppermute | solution.py:295
  116.0 29.6 %collective-permute-start.10 = (bf16[4,2,64,1024]{3,2,1,0:T(8,128)(2,1)S(1)}, bf16[4,2,64,1024]{3,2,1,0:T(8,128)(2,1)S(1)}, u32[]{:S(2)}, u32[]{:S(2)}) collective-permute-start(bf16[4,2,64,1024]{3,2,1,0:T(8,128)(2,1)S(1)} %get-tuple-element.44), channel_id=1, source_target_pairs={{0,2},{1,3},{2,0},{3,1},{4,6},{5,7},{6,4},{7,5},{8,10},{9,11},{10,... | collective-permute-start | bytes 3145736 | tf_op jit(solution)/shard_map/ppermute | solution.py:295
  116.5 41.6 %collective-permute-start.11 = (bf16[4,2,64,1024]{3,2,1,0:T(8,128)(2,1)S(1)}, bf16[4,2,64,1024]{3,2,1,0:T(8,128)(2,1)S(1)}, u32[]{:S(2)}, u32[]{:S(2)}) collective-permute-start(bf16[4,2,64,1024]{3,2,1,0:T(8,128)(2,1)S(1)} %get-tuple-element.45), channel_id=1, source_target_pairs={{0,4},{1,5},{2,6},{3,7},{4,8},{5,9},{6,10},{7,11},{8,12},{9,13},{1... | collective-permute-start | bytes 3145736 | tf_op jit(solution)/shard_map/ppermute | solution.py:295
  118.2 43.4 %collective-permute-start.12 = (bf16[4,2,64,1024]{3,2,1,0:T(8,128)(2,1)S(1)}, bf16[4,2,64,1024]{3,2,1,0:T(8,128)(2,1)S(1)}, u32[]{:S(2)}, u32[]{:S(2)}) collective-permute-start(bf16[4,2,64,1024]{3,2,1,0:T(8,128)(2,1)S(1)} %get-tuple-element.46), channel_id=1, source_target_pairs={{0,1},{1,2},{2,3},{3,0},{4,5},{5,6},{6,7},{7,4},{8,9},{9,10},{10,1... | collective-permute-start | bytes 3145736 | tf_op jit(solution)/shard_map/ppermute | solution.py:295
  119.3 42.3 %collective-permute-start.13 = (bf16[4,2,64,1024]{3,2,1,0:T(8,128)(2,1)S(1)}, bf16[4,2,64,1024]{3,2,1,0:T(8,128)(2,1)S(1)}, u32[]{:S(2)}, u32[]{:S(2)}) collective-permute-start(bf16[4,2,64,1024]{3,2,1,0:T(8,128)(2,1)S(1)} %get-tuple-element.47), channel_id=1, source_target_pairs={{0,12},{1,13},{2,14},{3,15},{4,0},{5,1},{6,2},{7,3},{8,4},{9,5},{1... | collective-permute-start | bytes 3145736 | tf_op jit(solution)/shard_map/ppermute | solution.py:295
  142.7 18.8 %collective-permute-start.14 = (bf16[4,2,64,1024]{3,2,1,0:T(8,128)(2,1)S(1)}, bf16[4,2,64,1024]{3,2,1,0:T(8,128)(2,1)S(1)}, u32[]{:S(2)}, u32[]{:S(2)}) collective-permute-start(bf16[4,2,64,1024]{3,2,1,0:T(8,128)(2,1)S(1)} %get-tuple-element.48), channel_id=1, source_target_pairs={{0,3},{1,0},{2,1},{3,2},{4,7},{5,4},{6,5},{7,6},{8,11},{9,8},{10,9... | collective-permute-start | bytes 3145736 | tf_op jit(solution)/shard_map/ppermute | solution.py:295

commit v4 on v3

--- a/solution.py
+++ b/solution.py
@@ -13,7 +13,6 @@
 TAPS = 16
 ITERS = 3
 SHIFTS = (1, 3, 2, 0)
-VMEM = 28 * 1024 * 1024
 
 
 def taps_table():
@@ -110,27 +109,27 @@
     transform(x_ref, table_ref, wide_ref, store)
 
 
-def order_kernel(recv_ref, series_ref):
-    chans, tiles, halves, _, sub, _ = recv_ref.shape
+def order_kernel(recv_ref, real_ref, imag_ref):
+    chans, tiles, halves, own, sub, _ = recv_ref.shape
     rows = chans * halves * sub // 2
-    for pair in range(tiles // 2):
-
-        def parts(tile):
-            both = recv_ref[:, tile, :, 0].astype(jnp.float32)
-            both = both.reshape(chans * halves, 2, sub // 2, 128)
-            return [both[:, part].reshape(rows, 128).astype(jnp.bfloat16) for part in range(2)]
-
-        first, second = parts(2 * pair), parts(2 * pair + 1)
-        lanes = slice(pair * 128, pair * 128 + 128)
-        for part in range(2):
-            low = jnp.concatenate([first[part][:, :64], second[part][:, :64]], axis=1)
-            high = jnp.concatenate([first[part][:, 64:], second[part][:, 64:]], axis=1)
-            start = 2 * part * rows
-            series_ref[start : start + rows, lanes] = low
-            series_ref[start + rows : start + 2 * rows, lanes] = high
-
-
-def form_sums(series_refs, tiles, outs, slot):
+    for channel in range(own):
+        for pair in range(tiles // 2):
+
+            def parts(tile):
+                both = recv_ref[:, tile, :, channel].astype(jnp.float32)
+                both = both.reshape(chans * halves, 2, sub // 2, 128)
+                return [both[:, part].reshape(rows, 128).astype(jnp.bfloat16) for part in range(2)]
+
+            first, second = parts(2 * pair), parts(2 * pair + 1)
+            lanes = slice(pair * 128, pair * 128 + 128)
+            for part, series_ref in enumerate((real_ref, imag_ref)):
+                low = jnp.concatenate([first[part][:, :64], second[part][:, :64]], axis=1)
+                high = jnp.concatenate([first[part][:, 64:], second[part][:, 64:]], axis=1)
+                series_ref[channel, 0:rows, lanes] = low
+                series_ref[channel, rows : 2 * rows, lanes] = high
+
+
+def form_sums(series_refs, tiles, outs, channel, slot):
     inputs = series_refs[0].shape[1]
     samples = len(series_refs) * series_refs[0].shape[0] // 2
     rows = inputs // 16
@@ -152,85 +151,68 @@
     for n, out_ref in enumerate(outs):
         for part in range(2):
             start = part * count + n * rows
-            out_ref[slot, part] = sums[start : start + rows].astype(jnp.bfloat16)
-
-
-def row_tiles(position_ref, axis, shifts):
-    x, y = position_ref[0] // 4, position_ref[0] % 4
-    if axis == 0:
-        return [(x + shift) % 4 * 4 + y for shift in shifts]
-    return [x * 4 + (y + shift) % 4 for shift in shifts]
-
-
-def split_kernel(*refs):
-    rows = refs[4].shape[0]
-    for n in range(4):
-        start = n % 2 * rows
-        refs[4 + n][...] = refs[n][start : start + rows, :]
+            out_ref[channel, slot, part] = sums[start : start + rows].astype(jnp.bfloat16)
+
+
+def moved(position_ref, across, along):
+    x, y, core = position_ref[0] // 4, position_ref[0] % 4, position_ref[1]
+    dx, dy = jnp.where(core == 0, across, along), jnp.where(core == 0, along, across)
+    return (x + dx) % 4 * 4 + (y + dy) % 4
 
 
 def main_kernel(position_ref, *refs):
     series, outs = refs[:6], refs[6:]
-    for axis in range(2):
-        tiles = row_tiles(position_ref, axis, SHIFTS)
+    tiles = [moved(position_ref, shift, 0) for shift in SHIFTS]
+    for channel in range(2):
         for slot in range(3):
-            form_sums([series[3 * axis + slot]], tiles, outs[4 * axis : 4 * axis + 4], slot)
+            pieces = [ref.at[channel] for ref in series[2 * slot : 2 * slot + 2]]
+            form_sums(pieces, tiles, outs, channel, slot)
 
 
 def far_kernel(position_ref, *refs):
-    halves, blocks, outs = refs[:4], refs[4:12], refs[12:]
-    for axis in range(2):
-        tiles = row_tiles(position_ref, axis, SHIFTS)
-        form_sums(halves[2 * axis : 2 * axis + 2], tiles, outs[4 * axis : 4 * axis + 4], 3)
-    for block_ref, out_ref in zip(blocks, outs):
-        out_ref[0:3] = block_ref[...]
+    series, outs = refs[:2], refs[2:]
+    tiles = [moved(position_ref, shift, 0) for shift in SHIFTS]
+    for channel in range(2):
+        form_sums([ref.at[channel] for ref in series], tiles, outs, channel, 0)
 
 
 def place_kernel(moves, position_ref, *refs):
-    out_ref, held, in_sems, out_sems = refs[-2 - len(moves) - 1], refs[-2 - len(moves) : -2], refs[-2], refs[-1]
-    x, y = position_ref[0] // 4, position_ref[0] % 4
-    loads = []
-    for n, part_ref in enumerate(refs[: len(moves)]):
-        load = pltpu.make_async_copy(part_ref, held[n], in_sems.at[n])
-        load.start()
-        loads.append(load)
+    out_ref, out_sems = refs[-2:]
     copies = []
-    for n, (axis, shift) in enumerate(moves):
-        loads[n].wait()
-        for slot, step in enumerate((3, 1, 0, 2)):
-            if axis == 0:
-                owner = (x + 4 - shift) % 4 * 4 + (y + step) % 4
-            else:
-                owner = (x + step) % 4 * 4 + (y + 4 - shift) % 4
-            for part in range(2):
-                copy = pltpu.make_async_copy(
-                    held[n].at[slot, part], out_ref.at[part, owner * 2 + axis], out_sems.at[len(copies)]
-                )
-                copy.start()
-                copies.append(copy)
+    for n, (shift, steps) in enumerate(moves):
+        for channel in range(2):
+            for slot, step in enumerate(steps):
+                owner = moved(position_ref, 4 - shift, step)
+                for part in range(2):
+                    copy = pltpu.make_async_copy(
+                        refs[n].at[channel, slot, part],
+                        out_ref.at[part, owner * 2 + channel],
+                        out_sems.at[len(copies)],
+                    )
+                    copy.start()
+                    copies.append(copy)
     for copy in copies:
         copy.wait()
 
 
-def gains_kernel(first_ref, second_ref, flags_ref, out_ref):
+def gains_kernel(real_ref, imag_ref, flags_ref, out_ref):
     keep = (1 - flags_ref[...]).astype(jnp.float32)
     out_ref[...] = jnp.zeros_like(out_ref)
-    for channel, series_ref in enumerate((first_ref, second_ref)):
-        for part, gain in enumerate(stefcal(series_ref, keep)):
+    for channel in range(2):
+        for part, gain in enumerate(stefcal(real_ref.at[channel], imag_ref.at[channel], keep)):
             for tile in range(16):
                 place = part * 2 + channel
                 out_ref[tile, place : place + 1, 0:64] = gain[:, tile * 64 : tile * 64 + 64]
 
 
-def stefcal(series_ref, keep):
-    half = series_ref.shape[0] // 2
-    steps = half // 16
-    inverse = 2.0 / series_ref.shape[0]
+def stefcal(real_ref, imag_ref, keep):
+    steps = real_ref.shape[0] // 16
+    inverse = 1.0 / real_ref.shape[0]
 
     def load(step):
         start = pl.multiple_of(step * 16, 16)
-        real = series_ref[pl.ds(start, 16), :].astype(jnp.float32)
-        imag = series_ref[pl.ds(half + start, 16), :].astype(jnp.float32)
+        real = real_ref[pl.ds(start, 16), :].astype(jnp.float32)
+        imag = imag_ref[pl.ds(start, 16), :].astype(jnp.float32)
         return real, imag
 
     def fold(value):
@@ -278,21 +260,22 @@
     return gain_real, gain_imag
 
 
-def params():
-    return pltpu.CompilerParams(vmem_limit_bytes=VMEM)
+def params(mib=22):
+    return pltpu.CompilerParams(vmem_limit_bytes=mib << 20)
 
 
 def cost(flops, size):
     return pl.CostEstimate(flops=int(flops), bytes_accessed=int(size), transcendentals=0)
 
 
-def turn(value, axis, shift):
+def turn(value, stage, shift):
     pairs = []
-    for x in range(4):
-        for y in range(4):
-            to = ((x + shift) % 4, y) if axis == 0 else (x, (y + shift) % 4)
-            pairs.append((x * 4 + y, to[0] * 4 + to[1]))
-    return lax.ppermute(value, "tile", pairs)
+    for chan in range(lax.axis_size("chan")):
+        for x in range(4):
+            for y in range(4):
+                to = (x, (y + shift) % 4) if chan % 2 == stage else ((x + shift) % 4, y)
+                pairs.append((chan * 16 + x * 4 + y, chan * 16 + to[0] * 4 + to[1]))
+    return lax.ppermute(value, ("chan", "tile"), pairs)
 
 
 def place(position, parts, moves, out_shape, previous=None):
@@ -300,17 +283,15 @@
     anywhere = pl.BlockSpec(memory_space=pl.ANY)
     return pl.pallas_call(
         functools.partial(place_kernel, moves),
-        in_specs=[pl.BlockSpec(memory_space=pltpu.SMEM)] + [anywhere] * len(operands),
+        in_specs=[pl.BlockSpec(memory_space=pltpu.SMEM)]
+        + [pl.BlockSpec(memory_space=pltpu.VMEM)] * len(parts)
+        + [anywhere] * (len(operands) - len(parts)),
         out_specs=anywhere,
         out_shape=out_shape,
-        scratch_shapes=[pltpu.VMEM(part.shape, part.dtype) for part in parts]
-        + [
-            pltpu.SemaphoreType.DMA((len(parts),)),
-            pltpu.SemaphoreType.DMA((8 * len(parts),)),
-        ],
+        scratch_shapes=[pltpu.SemaphoreType.DMA((sum(4 * len(move[1]) for move in moves),))],
         input_output_aliases={} if previous is None else {len(operands): 0},
-        compiler_params=params(),
-        cost_estimate=cost(0, len(parts) << 21),
+        compiler_params=params(10),
+        cost_estimate=cost(0, len(parts) << 22),
         name="place",
     )(position, *operands)
 
@@ -355,30 +336,23 @@
 
     turned = lax.all_to_all(spectra, ("chan", "tile"), split_axis=0, concat_axis=0, tiled=True)
     turned = turned.reshape(chan_count, tile_count, 2, own, sub, 128)
-    series = [
-        pl.pallas_call(
-            order_kernel,
-            grid=(1,),
-            in_specs=[
-                pl.BlockSpec(
-                    (chan_count, tile_count, 2, 1, sub, 128), lambda i, channel=channel: (0, 0, 0, channel, 0, 0)
-                )
-            ],
-            out_specs=pl.BlockSpec((2 * samples, inputs), lambda i: (0, 0)),
-            out_shape=jax.ShapeDtypeStruct((2 * samples, inputs), jnp.bfloat16),
-            compiler_params=params(),
-            cost_estimate=cost(1e6, 2 << 20),
-            name="order",
-        )(turned)
-        for channel in range(own)
-    ]
-
-    position = lax.axis_index("tile").astype(jnp.int32).reshape(1)
+    vmem = pl.BlockSpec(memory_space=pltpu.VMEM)
     smem = pl.BlockSpec(memory_space=pltpu.SMEM)
-    vmem = pl.BlockSpec(memory_space=pltpu.VMEM)
-    flops = 8 * 4 * row_count * inputs * samples
-    up = [turn(series[axis], 1 - axis, 1) for axis in range(2)]
-    down = [turn(series[axis], 1 - axis, 3) for axis in range(2)]
+    series_shape = jax.ShapeDtypeStruct((own, samples, inputs), jnp.bfloat16)
+    real, imag = pl.pallas_call(
+        order_kernel,
+        in_specs=[vmem],
+        out_specs=[vmem] * 2,
+        out_shape=[series_shape] * 2,
+        compiler_params=params(),
+        cost_estimate=cost(1e6, 4 << 20),
+        name="order",
+    )(turned)
+
+    position = jnp.stack([lax.axis_index("tile"), lax.axis_index("chan") % 2]).astype(jnp.int32)
+    up_real, down_imag = turn(real, 0, 1), turn(imag, 0, 3)
+    up_imag, down_real = turn(imag, 0, 1), turn(real, 0, 3)
+    far_real, far_imag = turn(up_real, 0, 1), turn(down_imag, 0, 3)
     gains = pl.pallas_call(
         gains_kernel,
         in_specs=[vmem] * 3,
@@ -387,45 +361,40 @@
         compiler_params=params(),
         cost_estimate=cost(own * inputs * samples * 64, 2 << 20),
         name="gains",
-    )(*series, flags.reshape(1, inputs))
-    gains = lax.all_to_all(gains, "tile", split_axis=0, concat_axis=0, tiled=True)
-    up, down, gains = lax.optimization_barrier((up, down, gains))
-    half_shape = jax.ShapeDtypeStruct((samples, inputs), jnp.bfloat16)
-    parts = pl.pallas_call(
-        split_kernel,
-        in_specs=[vmem] * 4,
-        out_specs=[vmem] * 4,
-        out_shape=[half_shape] * 4,
-        compiler_params=params(),
-        cost_estimate=cost(0, 4 << 20),
-        name="split",
-    )(up[0], down[0], up[1], down[1])
-    far = [turn(parts[n], 1 - n // 2, (1, 3)[n % 2]) for n in range(4)]
+    )(real, imag, flags.reshape(1, inputs))
+    up_imag, down_real, gains = lax.optimization_barrier((up_imag, down_real, gains))
+
+    flops = 8 * 4 * row_count * inputs * samples
     blocks = pl.pallas_call(
         main_kernel,
         in_specs=[smem] + [vmem] * 6,
-        out_specs=[vmem] * 8,
-        out_shape=[jax.ShapeDtypeStruct((3, 2, row_count, inputs), jnp.bfloat16)] * 8,
+        out_specs=[vmem] * 4,
+        out_shape=[jax.ShapeDtypeStruct((own, 3, 2, row_count, inputs), jnp.bfloat16)] * 4,
         compiler_params=params(),
         cost_estimate=cost(6 * flops, 12 << 20),
         name="main_sums",
-    )(position, up[0], down[0], series[0], up[1], down[1], series[1])
-    blocks = pl.pallas_call(
+    )(position, up_real, up_imag, down_real, down_imag, real, imag)
+    blocks, far_real, far_imag = lax.optimization_barrier((blocks, far_real, far_imag))
+    far_blocks = pl.pallas_call(
         far_kernel,
-        in_specs=[smem] + [vmem] * 12,
-        out_specs=[vmem] * 8,
-        out_shape=[jax.ShapeDtypeStruct((4, 2, row_count, inputs), jnp.bfloat16)] * 8,
-        compiler_params=params(),
-        cost_estimate=cost(2 * flops, 16 << 20),
+        in_specs=[smem] + [vmem] * 2,
+        out_specs=[vmem] * 4,
+        out_shape=[jax.ShapeDtypeStruct((own, 1, 2, row_count, inputs), jnp.bfloat16)] * 4,
+        compiler_params=params(),
+        cost_estimate=cost(2 * flops, 4 << 20),
         name="far_sums",
-    )(position, *far, *blocks)
-
-    moves = [(axis, shift) for shift in (2, 1, 3) for axis in range(2)]
-    sent = [turn(blocks[4 * axis + SHIFTS.index(shift)], axis, shift) for axis, shift in moves]
-
+    )(position, far_real, far_imag)
+
+    near, far = (3, 1, 0), (2,)
+    order = (1, 3, 2)
+    sent = [turn(blocks[SHIFTS.index(shift)], 1, shift) for shift in order]
+    sent_far = [turn(far_blocks[SHIFTS.index(shift)], 1, shift) for shift in order]
     out_shape = jax.ShapeDtypeStruct((2, tile_count * own, row_count, inputs), jnp.bfloat16)
-    visibilities = place(position, [blocks[3], blocks[7]], [(0, 0), (1, 0)], out_shape)
-    visibilities = place(position, sent, moves, out_shape, visibilities)
+    visibilities = place(position, [blocks[3], far_blocks[3]], [(0, near), (0, far)], out_shape)
+    gains, sent[0], visibilities = lax.optimization_barrier((gains, sent[0], visibilities))
+    gains = lax.all_to_all(gains, "tile", split_axis=0, concat_axis=0, tiled=True)
+    moves = [(shift, steps) for steps in (near, far) for shift in order]
+    visibilities = place(position, sent + sent_far, moves, out_shape, visibilities)
     gains = gains[:, : 2 * own, :row_count].reshape(tile_count, 2, own, row_count).transpose(1, 0, 2, 3)
     gains = gains.reshape(2, tile_count * own, row_count)
     return (visibilities, gains)

time: 167 us -> 159 us (0.952); the launches traced: 165 us -> 159 us
  starting transfers between devices: 18.4 us -> 41.6 us
  blocking collectives: 64.4 us -> 46.4 us
  waiting for transfers between devices: 43.8 us -> 33.3 us
  local copies, waits for them, and re-layouts: 9.66 us -> 3.56 us
  Pallas kernels: 27.9 us -> 33.2 us
    all_to_all x0 -> x1, starting transfers between devices: none -> 22.6 us  [body(): lax.all_to_all(gains, 'tile', split_axis=0, concat_axis=0, tiled=True)]
    all_to_all x1 -> x0, blocking collectives: 19.8 us -> none  [body(): lax.all_to_all(gains, 'tile', split_axis=0, concat_axis=0, tiled=True)]
    ppermute x14 -> x12, waiting for transfers between devices: 43.8 us -> 33.3 us  [turn(): return lax.ppermute(value, ('chan', 'tile'), pairs)]
    unnamed x20 -> x8, local copies, waits for them, and re-layouts: 7.76 us -> 1.6 us
    pallas_call x1, Pallas kernels: 3.55 us -> 7.4 us  [body(): pl.pallas_call(main_kernel, in_specs=[smem] + [vmem] * 6, out_specs=[vmem...]
    pallas_call x2, Pallas kernels: 5.11 us -> 6.89 us  [place(): pl.pallas_call(functools.partial(place_kernel, moves), in_specs=[pl.Block...]
    all_to_all x1, blocking collectives: 44.7 us -> 46.4 us  [body(): lax.all_to_all(spectra, ('chan', 'tile'), split_axis=0, concat_axis=0, ti...]
    pallas_call x4 -> x2, Pallas kernels: 5.66 us -> 4.76 us  [the longest x1 4.05 us: body(): pl.pallas_call(far_kernel, in_specs=[smem] + [vmem] * 2, out_specs=[vmem]...]
  transfers between devices with their start and end apart: 15 -> 14, of which waited for: 6 -> 6; matrix products, arithmetic and copies ran while one was open for 0% -> 0% of each run, Pallas kernels for 9% -> 18%
where the time goes in v4:
time: 159 us
  blocking collectives  46.4 us (29%)
  starting transfers between devices  41.6 us (26%)
  waiting for transfers between devices  33.3 us (21%)
  Pallas kernels  33.2 us (21%)
  local copies, waits for them, and re-layouts  3.56 us (2%)
    all_to_all x1, blocking collectives, body(): lax.all_to_all(spectra, ('chan', 'tile'), split_axis=0, concat_axis=0, ti...  46.4 us
    ppermute x12, waiting for transfers between devices, turn(): return lax.ppermute(value, ('chan', 'tile'), pairs)  33.3 us
    all_to_all x1, starting transfers between devices, body(): lax.all_to_all(gains, 'tile', split_axis=0, concat_axis=0, tiled=True)  22.6 us
    ppermute x12, starting transfers between devices, turn(): return lax.ppermute(value, ('chan', 'tile'), pairs)  17.2 us
    pallas_call x1, Pallas kernels, body(): pl.pallas_call(main_kernel, in_specs=[smem] + [vmem] * 6, out_specs=[vmem...  7.4 us
    pallas_call x2, Pallas kernels, place(): pl.pallas_call(functools.partial(place_kernel, moves), in_specs=[pl.Block...  6.89 us
    pallas_call x1, Pallas kernels, body(): pl.pallas_call(gains_kernel, in_specs=[vmem] * 3, out_specs=vmem, out_sha...  6.55 us
    pallas_call x1, Pallas kernels, body(): pl.pallas_call(far_kernel, in_specs=[smem] + [vmem] * 2, out_specs=[vmem]...  4.05 us
  transfers between devices with their start and end apart: 14, of which 6 were waited for; matrix products, arithmetic and copies ran while one was open for 0% of the time, Pallas kernels for 18%

profile of v4, /device:TPU:6, one launch (start us, length us, event | category | flops | bytes accessed | tf_op | source)
XLA Modules:
  0.0 159.0 jit_solution(12349303576518679206)
XLA Ops:
  0.6 0.0 copy-start.1
  0.7 1.3 slice.6
  2.0 1.8 %collective-permute-start = (bf16[2,64,3840]{2,1,0:T(8,128)(2,1)S(1)}, bf16[2,64,3840]{2,1,0:T(8,128)(2,1)S(1)}, u32[]{:S(2)}, u32[]{:S(2)}) collective-permute-start(bf16[2,64,3840]{2,1,0:T(8,128)(2,1)S(1)} %slice.6), channel_id=1, source_target_pairs={{0,16},{16,32},{32,48},{48,64},{64,80},{80,96},{96,112},{1,17},{17... | collective-permute-start | bytes 2949128 | tf_op jit(solution)/shard_map/ppermute | solution.py:317
  3.8 1.6 copy-done
  5.4 3.8 %late_spectra.1.late_ref = bf16[128,2,16,128]{3,2,1,0:T(8,128)(2,1)S(1)} custom-call(bf16[2,64,8192]{2,1,0:T(8,128)(2,1)S(1)} %copy-done, f32[16,256]{1,0:T(8,128)S(1)} %copy-done.2, bf16[512,512]{1,0:T(8,128)(2,1)S(1)} %copy-done.1), custom_call_target="tpu_custom_call" | custom-call | flops 1500000000 | bytes 4194304 | tf_op jit(solution)/shard_map/late_spectra/pallas_call | solution.py:320
  9.2 3.9 %early_spectra.1 = bf16[128,2,2,16,128]{4,3,2,1,0:T(8,128)(2,1)S(1)} custom-call(bf16[2,64,8192]{2,1,0:T(8,128)(2,1)S(1)} %copy-done, bf16[2,64,3840]{2,1,0:T(8,128)(2,1)S(1)} %collective-permute-done.h_ref, bf16[128,2,16,128]{3,2,1,0:T(8,128)(2,1)S(1)} %late_spectra.1.late_ref, f32[16,256]{1,0:T(8,128)S(1)} %copy-done.2, bf16[512,512]{1,0:T(8,128)(2,1)S(1)} %copy-done.1), custom_call_target="tpu_custom_call" | custom-call | flops 1500000000 | bytes 6291456 | tf_op jit(solution)/shard_map/early_spectra/pallas_call | solution.py:328
  13.1 46.4 %all_to_all.10 = bf16[128,2,2,16,128]{4,3,2,1,0:T(8,128)(2,1)S(1)} all-to-all(bf16[128,2,2,16,128]{4,3,2,1,0:T(8,128)(2,1)S(1)} %early_spectra.1), channel_id=1, replica_groups=mesh['chan'=8,'tile'=16] {'chan','tile'}, dimensions={0} | all-to-all | bytes 4194304 | tf_op jit(solution)/shard_map/all_to_all | solution.py:337
  59.5 0.7 order.1
  60.2 2.8 %collective-permute-start.4 = (bf16[2,256,1024]{2,1,0:T(8,128)(2,1)S(1)}, bf16[2,256,1024]{2,1,0:T(8,128)(2,1)}, u32[]{:S(2)}, u32[]{:S(2)}) collective-permute-start(bf16[2,256,1024]{2,1,0:T(8,128)(2,1)S(1)} %get-tuple-element.24.imag_ref.refs_5_), channel_id=1, source_target_pairs={{0,3},{1,0},{2,1},{3,2},{4,7},{5,4},{6,5},{7,6},{8,11},{9,8},{10,9... | collective-permute-start | bytes 3145736 | tf_op jit(solution)/shard_map/ppermute | solution.py:278
  63.0 0.2 collective-permute-start.1
  63.2 3.0 %collective-permute-start.2 = (bf16[2,256,1024]{2,1,0:T(8,128)(2,1)S(1)}, bf16[2,256,1024]{2,1,0:T(8,128)(2,1)}, u32[]{:S(2)}, u32[]{:S(2)}) collective-permute-start(bf16[2,256,1024]{2,1,0:T(8,128)(2,1)S(1)} %get-tuple-element.25.real_ref.refs_4_), channel_id=1, source_target_pairs={{0,3},{1,0},{2,1},{3,2},{4,7},{5,4},{6,5},{7,6},{8,11},{9,8},{10,9... | collective-permute-start | bytes 3145736 | tf_op jit(solution)/shard_map/ppermute | solution.py:278
  66.3 9.0 %collective-permute-done.4.refs_3_ = bf16[2,256,1024]{2,1,0:T(8,128)(2,1)} collective-permute-done((bf16[2,256,1024]{2,1,0:T(8,128)(2,1)S(1)}, bf16[2,256,1024]{2,1,0:T(8,128)(2,1)}, u32[]{:S(2)}, u32[]{:S(2)}) %collective-permute-start.4) | collective-permute-done | bytes 1048608 | tf_op jit(solution)/shard_map/ppermute | solution.py:278
  75.3 3.8 %collective-permute-start.6 = (bf16[2,256,1024]{2,1,0:T(8,128)(2,1)}, bf16[2,256,1024]{2,1,0:T(8,128)(2,1)}, u32[]{:S(2)}, u32[]{:S(2)}) collective-permute-start(bf16[2,256,1024]{2,1,0:T(8,128)(2,1)} %collective-permute-done.4.refs_3_), channel_id=1, source_target_pairs={{0,3},{1,0},{2,1},{3,2},{4,7},{5,4},{6,5},{7,6},{8,11},{9,8},{10,9... | collective-permute-start | bytes 3145736 | tf_op jit(solution)/shard_map/ppermute | solution.py:278
  79.1 0.1 pad_add_fusion.position_ref
  79.2 6.6 %gains.1 = f32[16,8,128]{2,1,0:T(8,128)} custom-call(bf16[2,256,1024]{2,1,0:T(8,128)(2,1)S(1)} %get-tuple-element.25.real_ref.refs_4_, bf16[2,256,1024]{2,1,0:T(8,128)(2,1)S(1)} %get-tuple-element.24.imag_ref.refs_5_, s32[1,1024]{1,0:T(1,128)S(1)} %bitcast.9), custom_call_target="tpu_custom_call" | custom-call | flops 33554432 | bytes 2097152 | tf_op jit(solution)/shard_map/gains/pallas_call | solution.py:356
  85.8 4.6 %collective-permute-done.1.refs_1_ = bf16[2,256,1024]{2,1,0:T(8,128)(2,1)} collective-permute-done((bf16[2,256,1024]{2,1,0:T(8,128)(2,1)S(1)}, bf16[2,256,1024]{2,1,0:T(8,128)(2,1)}, u32[]{:S(2)}, u32[]{:S(2)}) %collective-permute-start.1) | collective-permute-done | bytes 1048608 | tf_op jit(solution)/shard_map/ppermute | solution.py:278
  90.4 7.4 %main_sums.1 = (bf16[2,3,2,64,1024]{4,3,2,1,0:T(8,128)(2,1)S(1)}, bf16[2,3,2,64,1024]{4,3,2,1,0:T(8,128)(2,1)}, bf16[2,3,2,64,1024]{4,3,2,1,0:T(8,128)(2,1)}, bf16[2,3,2,64,1024]{4,3,2,1,0:T(8,128)(2,1)S(1)}) custom-call(s32[2]{0:T(128)S(1)} %pad_add_fusion.position_ref, bf16[2,256,1024]{2,1,0:T(8,128)(2,1)} %collective-permute-done.3.refs_0_, ...), custom_call_target="tpu_custom_call" | custom-call | flops 3221225472 | bytes 12582912 | tf_op jit(solution)/shard_map/main_sums/pallas_call | solution.py:368
  97.8 0.1 collective-permute-done.6.refs_1_
  97.9 3.7 %collective-permute-done.5.refs_0_ = bf16[2,256,1024]{2,1,0:T(8,128)(2,1)} collective-permute-done((bf16[2,256,1024]{2,1,0:T(8,128)(2,1)}, bf16[2,256,1024]{2,1,0:T(8,128)(2,1)}, u32[]{:S(2)}, u32[]{:S(2)}) %collective-permute-start.5) | collective-permute-done | bytes 1048608 | tf_op jit(solution)/shard_map/ppermute | solution.py:278
  101.6 1.3 collective-permute-start.7
  102.9 0.7 collective-permute-start.8
  103.6 1.6 %collective-permute-start.9 = (bf16[2,3,2,64,1024]{4,3,2,1,0:T(8,128)(2,1)}, bf16[2,3,2,64,1024]{4,3,2,1,0:T(8,128)(2,1)}, u32[]{:S(2)}, u32[]{:S(2)}) collective-permute-start(bf16[2,3,2,64,1024]{4,3,2,1,0:T(8,128)(2,1)} %get-tuple-element.40), channel_id=1, source_target_pairs={{0,8},{1,9},{2,10},{3,11},{4,12},{5,13},{6,14},{7,15},{8,0},{9,1},... | collective-permute-start | bytes 4718600 | tf_op jit(solution)/shard_map/ppermute | solution.py:278
  105.3 4.1 %far_sums.1 = (bf16[2,1,2,64,1024]{4,3,2,1,0:T(8,128)(2,1)}, bf16[2,1,2,64,1024]{4,3,2,1,0:T(8,128)(2,1)}, bf16[2,1,2,64,1024]{4,3,2,1,0:T(8,128)(2,1)}, bf16[2,1,2,64,1024]{4,3,2,1,0:T(8,128)(2,1)S(1)}) custom-call(s32[2]{0:T(128)S(1)} %pad_add_fusion.position_ref, bf16[2,256,1024]{2,1,0:T(8,128)(2,1)} %collective-permute-done.5.refs_0_, ...), custom_call_target="tpu_custom_call" | custom-call | flops 1073741824 | bytes 4194304 | tf_op jit(solution)/shard_map/far_sums/pallas_call | solution.py:378
  109.3 1.0 collective-permute-start.10
  110.3 1.0 collective-permute-start.11
  111.3 10.7 %collective-permute-done.7.refs_0_ = bf16[2,3,2,64,1024]{4,3,2,1,0:T(8,128)(2,1)S(1)} collective-permute-done((bf16[2,3,2,64,1024]{4,3,2,1,0:T(8,128)(2,1)S(1)}, bf16[2,3,2,64,1024]{4,3,2,1,0:T(8,128)(2,1)S(1)}, u32[]{:S(2)}, u32[]{:S(2)}) %collective-permute-start.7) | collective-permute-done | bytes 1572896 | tf_op jit(solution)/shard_map/ppermute | solution.py:278
  122.0 1.6 %collective-permute-start.12 = (bf16[2,1,2,64,1024]{4,3,2,1,0:T(8,128)(2,1)}, bf16[2,1,2,64,1024]{4,3,2,1,0:T(8,128)(2,1)}, u32[]{:S(2)}, u32[]{:S(2)}) collective-permute-start(bf16[2,1,2,64,1024]{4,3,2,1,0:T(8,128)(2,1)} %get-tuple-element.43), channel_id=1, source_target_pairs={{0,8},{1,9},{2,10},{3,11},{4,12},{5,13},{6,14},{7,15},{8,0},{9,1},... | collective-permute-start | bytes 1572872 | tf_op jit(solution)/shard_map/ppermute | solution.py:278
  123.7 2.0 %place.2.refs_6_ = bf16[2,32,64,1024]{3,2,1,0:T(8,128)(2,1)} custom-call(s32[2]{0:T(128)S(1)} %pad_add_fusion.position_ref, bf16[2,3,2,64,1024]{4,3,2,1,0:T(8,128)(2,1)S(1)} %get-tuple-element.34.refs_0_, bf16[2,1,2,64,1024]{4,3,2,1,0:T(8,128)(2,1)S(1)} %get-tuple-element.37.refs_1_), custom_call_target="tpu_custom_call" | custom-call | bytes 8388608 | tf_op jit(solution)/shard_map/place/pallas_call | solution.py:284
  125.7 22.6 %all-to-all-start.1 = ((f32[16,8,128]{2,1,0:T(8,128)}), f32[16,8,128]{2,1,0:T(8,128)S(1)}, u32[]{:S(2)}, u32[]{:S(2)}) async-start(f32[16,8,128]{2,1,0:T(8,128)} %gains.1), calls=%async_computation.1 | async-start | bytes 131072 | tf_op jit(solution)/shard_map/all_to_all | solution.py:395
  148.3 5.2 %collective-permute-done.11.refs_4_ = bf16[2,1,2,64,1024]{4,3,2,1,0:T(8,128)(2,1)} collective-permute-done((bf16[2,1,2,64,1024]{4,3,2,1,0:T(8,128)(2,1)}, bf16[2,1,2,64,1024]{4,3,2,1,0:T(8,128)(2,1)}, u32[]{:S(2)}, u32[]{:S(2)}) %collective-permute-start.11) | collective-permute-done | bytes 524320 | tf_op jit(solution)/shard_map/ppermute | solution.py:278
  153.4 4.9 %place.3 = bf16[2,32,64,1024]{3,2,1,0:T(8,128)(2,1)} custom-call(s32[2]{0:T(128)S(1)} %pad_add_fusion.position_ref, bf16[2,3,2,64,1024]{4,3,2,1,0:T(8,128)(2,1)S(1)} %collective-permute-done.7.refs_0_, bf16[2,3,2,64,1024]{4,3,2,1,0:T(8,128)(2,1)S(1)} %collective-permute-done.8.refs_1_, ...), custom_call_target="tpu_custom_call", output_to_operand_aliasing={{}: (7, {})} | custom-call | bytes 25165824 | tf_op jit(solution)/shard_map/place/pallas_call | solution.py:284
  158.4 0.6 copy.7
  (17 shorter events, 0.0 us)
Async XLA Ops:
  0.6 3.2 %copy-start.1 = (bf16[512,512]{1,0:T(8,128)(2,1)S(1)}, bf16[512,512]{1,0:T(8,128)(2,1)}, u32[]{:S(2)}) copy-start(bf16[512,512]{1,0:T(8,128)(2,1)} %constant.27.clone.table_ref) | copy-start | bytes 1572868
  0.6 3.2 %copy-start.2 = (f32[16,256]{1,0:T(8,128)S(1)}, f32[16,256]{1,0:T(8,128)}, u32[]{:S(2)}) copy-start(f32[16,256]{1,0:T(8,128)} %constant.26.clone.taps_ref) | copy-start | bytes 49156
  2.0 7.2 %collective-permute-start = (bf16[2,64,3840]{2,1,0:T(8,128)(2,1)S(1)}, bf16[2,64,3840]{2,1,0:T(8,128)(2,1)S(1)}, u32[]{:S(2)}, u32[]{:S(2)}) collective-permute-start(bf16[2,64,3840]{2,1,0:T(8,128)(2,1)S(1)} %slice.6), channel_id=1, source_target_pairs={{0,16},{16,32},{32,48},{48,64},{64,80},{80,96},{96,112},{1,17},{17... | collective-permute-start | bytes 2949128 | tf_op jit(solution)/shard_map/ppermute | solution.py:317
  3.8 1.6 %copy-start = (bf16[2,64,8192]{2,1,0:T(8,128)(2,1)S(1)}, bf16[2,64,8192]{2,1,0:T(8,128)(2,1)}, u32[]{:S(2)}) copy-start(bf16[2,64,8192]{2,1,0:T(8,128)(2,1)} %v_ref.3) | copy-start | bytes 6291460
  59.5 19.7 %copy-start.3 = (s32[1024]{0:T(1024)S(1)}, s32[1024]{0:T(1024)}, u32[]{:S(2)}) copy-start(s32[1024]{0:T(1024)} %param.5) | copy-start | bytes 12292
  60.2 15.1 %collective-permute-start.4 = (bf16[2,256,1024]{2,1,0:T(8,128)(2,1)S(1)}, bf16[2,256,1024]{2,1,0:T(8,128)(2,1)}, u32[]{:S(2)}, u32[]{:S(2)}) collective-permute-start(bf16[2,256,1024]{2,1,0:T(8,128)(2,1)S(1)} %get-tuple-element.24.imag_ref.refs_5_), channel_id=1, source_target_pairs={{0,3},{1,0},{2,1},{3,2},{4,7},{5,4},{6,5},{7,6},{8,11},{9,8},{10,9... | collective-permute-start | bytes 3145736 | tf_op jit(solution)/shard_map/ppermute | solution.py:278
  63.0 16.1 %collective-permute-start.3 = (bf16[2,256,1024]{2,1,0:T(8,128)(2,1)S(1)}, bf16[2,256,1024]{2,1,0:T(8,128)(2,1)}, u32[]{:S(2)}, u32[]{:S(2)}) collective-permute-start(bf16[2,256,1024]{2,1,0:T(8,128)(2,1)S(1)} %get-tuple-element.25.real_ref.refs_4_), channel_id=1, source_target_pairs={{0,1},{1,2},{2,3},{3,0},{4,5},{5,6},{6,7},{7,4},{8,9},{9,10},{10,1... | collective-permute-start | bytes 3145736 | tf_op jit(solution)/shard_map/ppermute | solution.py:278
  63.0 27.3 %collective-permute-start.1 = (bf16[2,256,1024]{2,1,0:T(8,128)(2,1)S(1)}, bf16[2,256,1024]{2,1,0:T(8,128)(2,1)}, u32[]{:S(2)}, u32[]{:S(2)}) collective-permute-start(bf16[2,256,1024]{2,1,0:T(8,128)(2,1)S(1)} %get-tuple-element.24.imag_ref.refs_5_), channel_id=1, source_target_pairs={{0,1},{1,2},{2,3},{3,0},{4,5},{5,6},{6,7},{7,4},{8,9},{9,10},{10,1... | collective-permute-start | bytes 3145736 | tf_op jit(solution)/shard_map/ppermute | solution.py:278
  63.2 27.1 %collective-permute-start.2 = (bf16[2,256,1024]{2,1,0:T(8,128)(2,1)S(1)}, bf16[2,256,1024]{2,1,0:T(8,128)(2,1)}, u32[]{:S(2)}, u32[]{:S(2)}) collective-permute-start(bf16[2,256,1024]{2,1,0:T(8,128)(2,1)S(1)} %get-tuple-element.25.real_ref.refs_4_), channel_id=1, source_target_pairs={{0,3},{1,0},{2,1},{3,2},{4,7},{5,4},{6,5},{7,6},{8,11},{9,8},{10,9... | collective-permute-start | bytes 3145736 | tf_op jit(solution)/shard_map/ppermute | solution.py:278
  75.3 22.6 %collective-permute-start.6 = (bf16[2,256,1024]{2,1,0:T(8,128)(2,1)}, bf16[2,256,1024]{2,1,0:T(8,128)(2,1)}, u32[]{:S(2)}, u32[]{:S(2)}) collective-permute-start(bf16[2,256,1024]{2,1,0:T(8,128)(2,1)} %collective-permute-done.4.refs_3_), channel_id=1, source_target_pairs={{0,3},{1,0},{2,1},{3,2},{4,7},{5,4},{6,5},{7,6},{8,11},{9,8},{10,9... | collective-permute-start | bytes 3145736 | tf_op jit(solution)/shard_map/ppermute | solution.py:278
  79.1 22.5 %collective-permute-start.5 = (bf16[2,256,1024]{2,1,0:T(8,128)(2,1)}, bf16[2,256,1024]{2,1,0:T(8,128)(2,1)}, u32[]{:S(2)}, u32[]{:S(2)}) collective-permute-start(bf16[2,256,1024]{2,1,0:T(8,128)(2,1)} %collective-permute-done.3.refs_0_), channel_id=1, source_target_pairs={{0,1},{1,2},{2,3},{3,0},{4,5},{5,6},{6,7},{7,4},{8,9},{9,10},{10,1... | collective-permute-start | bytes 3145736 | tf_op jit(solution)/shard_map/ppermute | solution.py:278
  101.6 20.4 %collective-permute-start.7 = (bf16[2,3,2,64,1024]{4,3,2,1,0:T(8,128)(2,1)S(1)}, bf16[2,3,2,64,1024]{4,3,2,1,0:T(8,128)(2,1)S(1)}, u32[]{:S(2)}, u32[]{:S(2)}) collective-permute-start(bf16[2,3,2,64,1024]{4,3,2,1,0:T(8,128)(2,1)S(1)} %get-tuple-element.33), channel_id=1, source_target_pairs={{0,4},{1,5},{2,6},{3,7},{4,8},{5,9},{6,10},{7,11},{8,12},{9,13},{1... | collective-permute-start | bytes 4718600 | tf_op jit(solution)/shard_map/ppermute | solution.py:278
  102.9 50.6 %collective-permute-start.8 = (bf16[2,3,2,64,1024]{4,3,2,1,0:T(8,128)(2,1)}, bf16[2,3,2,64,1024]{4,3,2,1,0:T(8,128)(2,1)S(1)}, u32[]{:S(2)}, u32[]{:S(2)}) collective-permute-start(bf16[2,3,2,64,1024]{4,3,2,1,0:T(8,128)(2,1)} %get-tuple-element.39), channel_id=1, source_target_pairs={{0,12},{1,13},{2,14},{3,15},{4,0},{5,1},{6,2},{7,3},{8,4},{9,5},{1... | collective-permute-start | bytes 4718600 | tf_op jit(solution)/shard_map/ppermute | solution.py:278
  103.6 49.8 %collective-permute-start.9 = (bf16[2,3,2,64,1024]{4,3,2,1,0:T(8,128)(2,1)}, bf16[2,3,2,64,1024]{4,3,2,1,0:T(8,128)(2,1)}, u32[]{:S(2)}, u32[]{:S(2)}) collective-permute-start(bf16[2,3,2,64,1024]{4,3,2,1,0:T(8,128)(2,1)} %get-tuple-element.40), channel_id=1, source_target_pairs={{0,8},{1,9},{2,10},{3,11},{4,12},{5,13},{6,14},{7,15},{8,0},{9,1},... | collective-permute-start | bytes 4718600 | tf_op jit(solution)/shard_map/ppermute | solution.py:278
  109.3 38.9 %collective-permute-start.10 = (bf16[2,1,2,64,1024]{4,3,2,1,0:T(8,128)(2,1)}, bf16[2,1,2,64,1024]{4,3,2,1,0:T(8,128)(2,1)}, u32[]{:S(2)}, u32[]{:S(2)}) collective-permute-start(bf16[2,1,2,64,1024]{4,3,2,1,0:T(8,128)(2,1)} %get-tuple-element.41), channel_id=1, source_target_pairs={{0,4},{1,5},{2,6},{3,7},{4,8},{5,9},{6,10},{7,11},{8,12},{9,13},{1... | collective-permute-start | bytes 1572872 | tf_op jit(solution)/shard_map/ppermute | solution.py:278
  110.3 43.1 %collective-permute-start.11 = (bf16[2,1,2,64,1024]{4,3,2,1,0:T(8,128)(2,1)}, bf16[2,1,2,64,1024]{4,3,2,1,0:T(8,128)(2,1)}, u32[]{:S(2)}, u32[]{:S(2)}) collective-permute-start(bf16[2,1,2,64,1024]{4,3,2,1,0:T(8,128)(2,1)} %get-tuple-element.42), channel_id=1, source_target_pairs={{0,12},{1,13},{2,14},{3,15},{4,0},{5,1},{6,2},{7,3},{8,4},{9,5},{1... | collective-permute-start | bytes 1572872 | tf_op jit(solution)/shard_map/ppermute | solution.py:278
  122.0 31.4 %collective-permute-start.12 = (bf16[2,1,2,64,1024]{4,3,2,1,0:T(8,128)(2,1)}, bf16[2,1,2,64,1024]{4,3,2,1,0:T(8,128)(2,1)}, u32[]{:S(2)}, u32[]{:S(2)}) collective-permute-start(bf16[2,1,2,64,1024]{4,3,2,1,0:T(8,128)(2,1)} %get-tuple-element.43), channel_id=1, source_target_pairs={{0,8},{1,9},{2,10},{3,11},{4,12},{5,13},{6,14},{7,15},{8,0},{9,1},... | collective-permute-start | bytes 1572872 | tf_op jit(solution)/shard_map/ppermute | solution.py:278
  125.7 32.7 %all-to-all-start.1 = ((f32[16,8,128]{2,1,0:T(8,128)}), f32[16,8,128]{2,1,0:T(8,128)S(1)}, u32[]{:S(2)}, u32[]{:S(2)}) async-start(f32[16,8,128]{2,1,0:T(8,128)} %gains.1), calls=%async_computation.1 | async-start | bytes 131072 | tf_op jit(solution)/shard_map/all_to_all | solution.py:395

commit v5 on v4

--- a/solution.py
+++ b/solution.py
@@ -93,19 +93,30 @@
     transform(x_ref, table_ref, wide_ref, store)
 
 
-def early_kernel(v_ref, h_ref, late_ref, taps_ref, table_ref, out_ref, x_ref, wide_ref):
+def early_kernel(last_ref, v_ref, before_ref, after_ref, late_ref, taps_ref, table_ref, out_ref, x_ref, wide_ref):
     history = TAPS - 1
-
-    def read(f, part, rows, lane):
+    frames = v_ref.shape[2] // NCH
+    behind = before_ref.shape[2] // NCH
+    middle = x_ref.shape[0] // 2
+    kept = jnp.where(last_ref[0] == 1, 0.0, 1.0)
+
+    def read_own(f, part, rows, lane):
+        if f < behind:
+            return before_ref[part, pl.ds(rows, 16), pl.ds(lane + f * NCH, 128)]
+        return v_ref[part, pl.ds(rows, 16), pl.ds(lane + (f - behind) * NCH, 128)]
+
+    def read_next(f, part, rows, lane):
         if f < history:
-            return h_ref[part, pl.ds(rows, 16), pl.ds(lane + f * NCH, 128)]
-        return v_ref[part, pl.ds(rows, 16), pl.ds(lane + (f - history) * NCH, 128)]
+            tile = v_ref[part, pl.ds(rows, 16), pl.ds(lane + (frames - history + f) * NCH, 128)]
+            return tile.astype(jnp.float32) * kept
+        return after_ref[part, pl.ds(rows, 16), pl.ds(lane + (f - history) * NCH, 128)]
 
     def store(device, tile):
         out_ref[pl.ds(device, 16), 0] = tile
         out_ref[pl.ds(device, 16), 1] = late_ref[pl.ds(device, 16)]
 
-    filter_frames(read, taps_ref, x_ref)
+    filter_frames(read_own, taps_ref, x_ref.at[pl.ds(0, middle)])
+    filter_frames(read_next, taps_ref, x_ref.at[pl.ds(middle, middle)])
     transform(x_ref, table_ref, wide_ref, store)
 
 
@@ -314,9 +325,14 @@
         pltpu.VMEM((half * row_count, 2 * NCH), jnp.bfloat16),
         pltpu.VMEM((NCH * half, 128), jnp.float32),
     ]
-    history = lax.ppermute(
-        voltages[:, :, (frame_count - (TAPS - 1)) * NCH :], "chan", [(c, c + 1) for c in range(chan_count - 1)]
+    behind = TAPS - 1 - half // 2
+    before = lax.ppermute(
+        voltages[:, :, (frame_count - behind) * NCH :], "chan", [(c, c + 1) for c in range(chan_count - 1)]
     )
+    after = lax.ppermute(
+        voltages[:, :, : half // 2 * NCH], "chan", [(c, (c - 1) % chan_count) for c in range(chan_count)]
+    )
+    last = (lax.axis_index("chan") == chan_count - 1).astype(jnp.int32).reshape(1)
     late = pl.pallas_call(
         late_kernel,
         out_shape=jax.ShapeDtypeStruct((device_count, own, sub, 128), jnp.bfloat16),
@@ -327,12 +343,13 @@
     )(voltages, taps, table)
     spectra = pl.pallas_call(
         early_kernel,
+        in_specs=[pl.BlockSpec(memory_space=pltpu.SMEM)] + [pl.BlockSpec(memory_space=pltpu.VMEM)] * 6,
         out_shape=jax.ShapeDtypeStruct((device_count, 2, own, sub, 128), jnp.bfloat16),
         scratch_shapes=scratch,
         compiler_params=params(),
         cost_estimate=cost(1.5e9, 6 << 20),
         name="early_spectra",
-    )(voltages, history, late, taps, table)
+    )(last, voltages, before, after, late, taps, table)
 
     turned = lax.all_to_all(spectra, ("chan", "tile"), split_axis=0, concat_axis=0, tiled=True)
     turned = turned.reshape(chan_count, tile_count, 2, own, sub, 128)

time: 159 us -> 155 us (0.975)
  blocking collectives: 46.4 us -> 37.8 us
  starting transfers between devices: 41.6 us -> 44.6 us
    all_to_all x1, blocking collectives: 46.4 us -> 37.8 us  [body(): lax.all_to_all(spectra, ('chan', 'tile'), split_axis=0, concat_axis=0, ti...]
    ppermute x1 -> x2, starting transfers between devices: 1.8 us -> 4.81 us  [the longest x1 3.49 us: body(): lax.ppermute(voltages[:, :, :half // 2 * NCH], 'chan', [(c, (c - 1) % cha...]
  transfers between devices with their start and end apart: 14 -> 15, of which waited for: 6 -> 6; matrix products, arithmetic and copies ran while one was open for 0% -> 1% of each run, Pallas kernels for 18% -> 19%
where the time goes in v5:
time: 155 us
  starting transfers between devices  44.6 us (29%)
  blocking collectives  37.8 us (24%)
  Pallas kernels  33.7 us (22%)
  waiting for transfers between devices  33.3 us (21%)
  local copies, waits for them, and re-layouts  4.42 us (3%)
    all_to_all x1, blocking collectives, body(): lax.all_to_all(spectra, ('chan', 'tile'), split_axis=0, concat_axis=0, ti...  37.8 us
    ppermute x12, waiting for transfers between devices, turn(): return lax.ppermute(value, ('chan', 'tile'), pairs)  33.3 us
    all_to_all x1, starting transfers between devices, body(): lax.all_to_all(gains, 'tile', split_axis=0, concat_axis=0, tiled=True)  22.6 us
    ppermute x12, starting transfers between devices, turn(): return lax.ppermute(value, ('chan', 'tile'), pairs)  17.2 us
    pallas_call x1, Pallas kernels, body(): pl.pallas_call(main_kernel, in_specs=[smem] + [vmem] * 6, out_specs=[vmem...  7.41 us
    pallas_call x2, Pallas kernels, place(): pl.pallas_call(functools.partial(place_kernel, moves), in_specs=[pl.Block...  6.89 us
    pallas_call x1, Pallas kernels, body(): pl.pallas_call(gains_kernel, in_specs=[vmem] * 3, out_specs=vmem, out_sha...  6.56 us
    pallas_call x1, Pallas kernels, body(): pl.pallas_call(early_kernel, in_specs=[pl.BlockSpec(memory_space=pltpu.SM...  4.28 us
  transfers between devices with their start and end apart: 15, of which 6 were waited for; matrix products, arithmetic and copies ran while one was open for 1% of the time, Pallas kernels for 19%

profile of v5, /device:TPU:6, one launch (start us, length us, event | category | flops | bytes accessed | tf_op | source)
XLA Modules:
  0.0 154.7 jit_solution(16783390788362277791)
XLA Ops:
  0.7 1.1 slice.10
  1.8 3.5 %collective-permute-start.1 = (bf16[2,64,2048]{2,1,0:T(8,128)(2,1)S(1)}, bf16[2,64,2048]{2,1,0:T(8,128)(2,1)S(1)}, u32[]{:S(2)}, u32[]{:S(2)}) collective-permute-start(bf16[2,64,2048]{2,1,0:T(8,128)(2,1)S(1)} %slice.10), channel_id=1, source_target_pairs={{0,112},{16,0},{32,16},{48,32},{64,48},{80,64},{96,80},{112,96},{1... | collective-permute-start | bytes 1572872 | tf_op jit(solution)/shard_map/ppermute | solution.py:332
  5.3 1.0 slice.9
  6.3 1.3 collective-permute-start
  7.7 1.6 %copy-done = bf16[2,64,8192]{2,1,0:T(8,128)(2,1)S(1)} copy-done((bf16[2,64,8192]{2,1,0:T(8,128)(2,1)S(1)}, bf16[2,64,8192]{2,1,0:T(8,128)(2,1)}, u32[]{:S(2)}) %copy-start) | copy-done | bytes 2097176
  9.3 3.8 %late_spectra.1.late_ref = bf16[128,2,16,128]{3,2,1,0:T(8,128)(2,1)S(1)} custom-call(bf16[2,64,8192]{2,1,0:T(8,128)(2,1)S(1)} %copy-done, f32[16,256]{1,0:T(8,128)S(1)} %copy-done.2, bf16[512,512]{1,0:T(8,128)(2,1)S(1)} %copy-done.1), custom_call_target="tpu_custom_call" | custom-call | flops 1500000000 | bytes 4194304 | tf_op jit(solution)/shard_map/late_spectra/pallas_call | solution.py:336
  13.1 4.3 %early_spectra.1 = bf16[128,2,2,16,128]{4,3,2,1,0:T(8,128)(2,1)S(1)} custom-call(s32[1]{0:T(128)} %bitcast.2.last_ref, bf16[2,64,8192]{2,1,0:T(8,128)(2,1)S(1)} %copy-done, bf16[2,64,1792]{2,1,0:T(8,128)(2,1)S(1)} %collective-permute-done.before_ref, bf16[2,64,2048]{2,1,0:T(8,128)(2,1)S(1)} %collective-permute-done.1.after_ref, ...), custom_call_target="tpu_custom_call" | custom-call | flops 1500000000 | bytes 6291456 | tf_op jit(solution)/shard_map/early_spectra/pallas_call | solution.py:344
  17.4 37.8 %all_to_all.10 = bf16[128,2,2,16,128]{4,3,2,1,0:T(8,128)(2,1)S(1)} all-to-all(bf16[128,2,2,16,128]{4,3,2,1,0:T(8,128)(2,1)S(1)} %early_spectra.1), channel_id=1, replica_groups=mesh['chan'=8,'tile'=16] {'chan','tile'}, dimensions={0} | all-to-all | bytes 4194304 | tf_op jit(solution)/shard_map/all_to_all | solution.py:354
  55.2 0.7 order.1
  55.9 2.8 %collective-permute-start.5 = (bf16[2,256,1024]{2,1,0:T(8,128)(2,1)S(1)}, bf16[2,256,1024]{2,1,0:T(8,128)(2,1)}, u32[]{:S(2)}, u32[]{:S(2)}) collective-permute-start(bf16[2,256,1024]{2,1,0:T(8,128)(2,1)S(1)} %get-tuple-element.24.imag_ref.refs_5_), channel_id=1, source_target_pairs={{0,3},{1,0},{2,1},{3,2},{4,7},{5,4},{6,5},{7,6},{8,11},{9,8},{10,9... | collective-permute-start | bytes 3145736 | tf_op jit(solution)/shard_map/ppermute | solution.py:289
  58.7 0.2 collective-permute-start.2
  58.9 3.0 %collective-permute-start.3 = (bf16[2,256,1024]{2,1,0:T(8,128)(2,1)S(1)}, bf16[2,256,1024]{2,1,0:T(8,128)(2,1)}, u32[]{:S(2)}, u32[]{:S(2)}) collective-permute-start(bf16[2,256,1024]{2,1,0:T(8,128)(2,1)S(1)} %get-tuple-element.25.real_ref.refs_4_), channel_id=1, source_target_pairs={{0,3},{1,0},{2,1},{3,2},{4,7},{5,4},{6,5},{7,6},{8,11},{9,8},{10,9... | collective-permute-start | bytes 3145736 | tf_op jit(solution)/shard_map/ppermute | solution.py:289
  62.0 9.0 %collective-permute-done.5.refs_3_ = bf16[2,256,1024]{2,1,0:T(8,128)(2,1)} collective-permute-done((bf16[2,256,1024]{2,1,0:T(8,128)(2,1)S(1)}, bf16[2,256,1024]{2,1,0:T(8,128)(2,1)}, u32[]{:S(2)}, u32[]{:S(2)}) %collective-permute-start.5) | collective-permute-done | bytes 1048608 | tf_op jit(solution)/shard_map/ppermute | solution.py:289
  71.0 3.8 %collective-permute-start.7 = (bf16[2,256,1024]{2,1,0:T(8,128)(2,1)}, bf16[2,256,1024]{2,1,0:T(8,128)(2,1)}, u32[]{:S(2)}, u32[]{:S(2)}) collective-permute-start(bf16[2,256,1024]{2,1,0:T(8,128)(2,1)} %collective-permute-done.5.refs_3_), channel_id=1, source_target_pairs={{0,3},{1,0},{2,1},{3,2},{4,7},{5,4},{6,5},{7,6},{8,11},{9,8},{10,9... | collective-permute-start | bytes 3145736 | tf_op jit(solution)/shard_map/ppermute | solution.py:289
  74.9 6.6 %gains.1 = f32[16,8,128]{2,1,0:T(8,128)} custom-call(bf16[2,256,1024]{2,1,0:T(8,128)(2,1)S(1)} %get-tuple-element.25.real_ref.refs_4_, bf16[2,256,1024]{2,1,0:T(8,128)(2,1)S(1)} %get-tuple-element.24.imag_ref.refs_5_, s32[1,1024]{1,0:T(1,128)S(1)} %bitcast.10), custom_call_target="tpu_custom_call" | custom-call | flops 33554432 | bytes 2097152 | tf_op jit(solution)/shard_map/gains/pallas_call | solution.py:373
  81.5 4.6 %collective-permute-done.2.refs_1_ = bf16[2,256,1024]{2,1,0:T(8,128)(2,1)} collective-permute-done((bf16[2,256,1024]{2,1,0:T(8,128)(2,1)S(1)}, bf16[2,256,1024]{2,1,0:T(8,128)(2,1)}, u32[]{:S(2)}, u32[]{:S(2)}) %collective-permute-start.2) | collective-permute-done | bytes 1048608 | tf_op jit(solution)/shard_map/ppermute | solution.py:289
  86.1 7.4 %main_sums.1 = (bf16[2,3,2,64,1024]{4,3,2,1,0:T(8,128)(2,1)S(1)}, bf16[2,3,2,64,1024]{4,3,2,1,0:T(8,128)(2,1)}, bf16[2,3,2,64,1024]{4,3,2,1,0:T(8,128)(2,1)}, bf16[2,3,2,64,1024]{4,3,2,1,0:T(8,128)(2,1)S(1)}) custom-call(s32[2]{0:T(128)S(1)} %pad_add_fusion.position_ref, bf16[2,256,1024]{2,1,0:T(8,128)(2,1)} %collective-permute-done.4.refs_0_, ...), custom_call_target="tpu_custom_call" | custom-call | flops 3221225472 | bytes 12582912 | tf_op jit(solution)/shard_map/main_sums/pallas_call | solution.py:385
  93.5 0.1 collective-permute-done.7.refs_1_
  93.6 3.7 %collective-permute-done.6.refs_0_ = bf16[2,256,1024]{2,1,0:T(8,128)(2,1)} collective-permute-done((bf16[2,256,1024]{2,1,0:T(8,128)(2,1)}, bf16[2,256,1024]{2,1,0:T(8,128)(2,1)}, u32[]{:S(2)}, u32[]{:S(2)}) %collective-permute-start.6) | collective-permute-done | bytes 1048608 | tf_op jit(solution)/shard_map/ppermute | solution.py:289
  97.3 1.3 collective-permute-start.8
  98.6 0.7 collective-permute-start.9
  99.3 1.6 %collective-permute-start.10 = (bf16[2,3,2,64,1024]{4,3,2,1,0:T(8,128)(2,1)}, bf16[2,3,2,64,1024]{4,3,2,1,0:T(8,128)(2,1)}, u32[]{:S(2)}, u32[]{:S(2)}) collective-permute-start(bf16[2,3,2,64,1024]{4,3,2,1,0:T(8,128)(2,1)} %get-tuple-element.40), channel_id=1, source_target_pairs={{0,8},{1,9},{2,10},{3,11},{4,12},{5,13},{6,14},{7,15},{8,0},{9,1},... | collective-permute-start | bytes 4718600 | tf_op jit(solution)/shard_map/ppermute | solution.py:289
  101.0 4.0 %far_sums.1 = (bf16[2,1,2,64,1024]{4,3,2,1,0:T(8,128)(2,1)}, bf16[2,1,2,64,1024]{4,3,2,1,0:T(8,128)(2,1)}, bf16[2,1,2,64,1024]{4,3,2,1,0:T(8,128)(2,1)}, bf16[2,1,2,64,1024]{4,3,2,1,0:T(8,128)(2,1)S(1)}) custom-call(s32[2]{0:T(128)S(1)} %pad_add_fusion.position_ref, bf16[2,256,1024]{2,1,0:T(8,128)(2,1)} %collective-permute-done.6.refs_0_, ...), custom_call_target="tpu_custom_call" | custom-call | flops 1073741824 | bytes 4194304 | tf_op jit(solution)/shard_map/far_sums/pallas_call | solution.py:395
  105.0 1.0 collective-permute-start.11
  106.0 1.0 collective-permute-start.12
  107.0 10.7 %collective-permute-done.8.refs_0_ = bf16[2,3,2,64,1024]{4,3,2,1,0:T(8,128)(2,1)S(1)} collective-permute-done((bf16[2,3,2,64,1024]{4,3,2,1,0:T(8,128)(2,1)S(1)}, bf16[2,3,2,64,1024]{4,3,2,1,0:T(8,128)(2,1)S(1)}, u32[]{:S(2)}, u32[]{:S(2)}) %collective-permute-start.8) | collective-permute-done | bytes 1572896 | tf_op jit(solution)/shard_map/ppermute | solution.py:289
  117.7 1.6 %collective-permute-start.13 = (bf16[2,1,2,64,1024]{4,3,2,1,0:T(8,128)(2,1)}, bf16[2,1,2,64,1024]{4,3,2,1,0:T(8,128)(2,1)}, u32[]{:S(2)}, u32[]{:S(2)}) collective-permute-start(bf16[2,1,2,64,1024]{4,3,2,1,0:T(8,128)(2,1)} %get-tuple-element.43), channel_id=1, source_target_pairs={{0,8},{1,9},{2,10},{3,11},{4,12},{5,13},{6,14},{7,15},{8,0},{9,1},... | collective-permute-start | bytes 1572872 | tf_op jit(solution)/shard_map/ppermute | solution.py:289
  119.4 2.0 %place.2.refs_6_ = bf16[2,32,64,1024]{3,2,1,0:T(8,128)(2,1)} custom-call(s32[2]{0:T(128)S(1)} %pad_add_fusion.position_ref, bf16[2,3,2,64,1024]{4,3,2,1,0:T(8,128)(2,1)S(1)} %get-tuple-element.34.refs_0_, bf16[2,1,2,64,1024]{4,3,2,1,0:T(8,128)(2,1)S(1)} %get-tuple-element.37.refs_1_), custom_call_target="tpu_custom_call" | custom-call | bytes 8388608 | tf_op jit(solution)/shard_map/place/pallas_call | solution.py:295
  121.4 22.6 %all-to-all-start.1 = ((f32[16,8,128]{2,1,0:T(8,128)}), f32[16,8,128]{2,1,0:T(8,128)S(1)}, u32[]{:S(2)}, u32[]{:S(2)}) async-start(f32[16,8,128]{2,1,0:T(8,128)} %gains.1), calls=%async_computation.1 | async-start | bytes 131072 | tf_op jit(solution)/shard_map/all_to_all | solution.py:412
  144.0 5.2 %collective-permute-done.12.refs_4_ = bf16[2,1,2,64,1024]{4,3,2,1,0:T(8,128)(2,1)} collective-permute-done((bf16[2,1,2,64,1024]{4,3,2,1,0:T(8,128)(2,1)}, bf16[2,1,2,64,1024]{4,3,2,1,0:T(8,128)(2,1)}, u32[]{:S(2)}, u32[]{:S(2)}) %collective-permute-start.12) | collective-permute-done | bytes 524320 | tf_op jit(solution)/shard_map/ppermute | solution.py:289
  149.1 4.9 %place.3 = bf16[2,32,64,1024]{3,2,1,0:T(8,128)(2,1)} custom-call(s32[2]{0:T(128)S(1)} %pad_add_fusion.position_ref, bf16[2,3,2,64,1024]{4,3,2,1,0:T(8,128)(2,1)S(1)} %collective-permute-done.8.refs_0_, bf16[2,3,2,64,1024]{4,3,2,1,0:T(8,128)(2,1)S(1)} %collective-permute-done.9.refs_1_, ...), custom_call_target="tpu_custom_call", output_to_operand_aliasing={{}: (7, {})} | custom-call | bytes 25165824 | tf_op jit(solution)/shard_map/place/pallas_call | solution.py:295
  154.1 0.6 copy.7
  (20 shorter events, 0.1 us)
Async XLA Ops:
  0.6 7.0 %copy-start.1 = (bf16[512,512]{1,0:T(8,128)(2,1)S(1)}, bf16[512,512]{1,0:T(8,128)(2,1)}, u32[]{:S(2)}) copy-start(bf16[512,512]{1,0:T(8,128)(2,1)} %constant.29.clone.table_ref) | copy-start | bytes 1572868
  0.6 7.0 %copy-start.2 = (f32[16,256]{1,0:T(8,128)S(1)}, f32[16,256]{1,0:T(8,128)}, u32[]{:S(2)}) copy-start(f32[16,256]{1,0:T(8,128)} %constant.28.clone.taps_ref) | copy-start | bytes 49156
  1.8 11.3 %collective-permute-start.1 = (bf16[2,64,2048]{2,1,0:T(8,128)(2,1)S(1)}, bf16[2,64,2048]{2,1,0:T(8,128)(2,1)S(1)}, u32[]{:S(2)}, u32[]{:S(2)}) collective-permute-start(bf16[2,64,2048]{2,1,0:T(8,128)(2,1)S(1)} %slice.10), channel_id=1, source_target_pairs={{0,112},{16,0},{32,16},{48,32},{64,48},{80,64},{96,80},{112,96},{1... | collective-permute-start | bytes 1572872 | tf_op jit(solution)/shard_map/ppermute | solution.py:332
  6.3 6.7 %collective-permute-start = (bf16[2,64,1792]{2,1,0:T(8,128)(2,1)S(1)}, bf16[2,64,1792]{2,1,0:T(8,128)(2,1)S(1)}, u32[]{:S(2)}, u32[]{:S(2)}) collective-permute-start(bf16[2,64,1792]{2,1,0:T(8,128)(2,1)S(1)} %slice.9), channel_id=1, source_target_pairs={{0,16},{16,32},{32,48},{48,64},{64,80},{80,96},{96,112},{1,17},{17... | collective-permute-start | bytes 1376264 | tf_op jit(solution)/shard_map/ppermute | solution.py:329
  7.7 1.6 %copy-start = (bf16[2,64,8192]{2,1,0:T(8,128)(2,1)S(1)}, bf16[2,64,8192]{2,1,0:T(8,128)(2,1)}, u32[]{:S(2)}) copy-start(bf16[2,64,8192]{2,1,0:T(8,128)(2,1)} %v_ref.3) | copy-start | bytes 6291460
  55.2 19.7 %copy-start.3 = (s32[1024]{0:T(1024)S(1)}, s32[1024]{0:T(1024)}, u32[]{:S(2)}) copy-start(s32[1024]{0:T(1024)} %param.5) | copy-start | bytes 12292
  55.9 15.1 %collective-permute-start.5 = (bf16[2,256,1024]{2,1,0:T(8,128)(2,1)S(1)}, bf16[2,256,1024]{2,1,0:T(8,128)(2,1)}, u32[]{:S(2)}, u32[]{:S(2)}) collective-permute-start(bf16[2,256,1024]{2,1,0:T(8,128)(2,1)S(1)} %get-tuple-element.24.imag_ref.refs_5_), channel_id=1, source_target_pairs={{0,3},{1,0},{2,1},{3,2},{4,7},{5,4},{6,5},{7,6},{8,11},{9,8},{10,9... | collective-permute-start | bytes 3145736 | tf_op jit(solution)/shard_map/ppermute | solution.py:289
  58.7 16.1 %collective-permute-start.4 = (bf16[2,256,1024]{2,1,0:T(8,128)(2,1)S(1)}, bf16[2,256,1024]{2,1,0:T(8,128)(2,1)}, u32[]{:S(2)}, u32[]{:S(2)}) collective-permute-start(bf16[2,256,1024]{2,1,0:T(8,128)(2,1)S(1)} %get-tuple-element.25.real_ref.refs_4_), channel_id=1, source_target_pairs={{0,1},{1,2},{2,3},{3,0},{4,5},{5,6},{6,7},{7,4},{8,9},{9,10},{10,1... | collective-permute-start | bytes 3145736 | tf_op jit(solution)/shard_map/ppermute | solution.py:289
  58.7 27.3 %collective-permute-start.2 = (bf16[2,256,1024]{2,1,0:T(8,128)(2,1)S(1)}, bf16[2,256,1024]{2,1,0:T(8,128)(2,1)}, u32[]{:S(2)}, u32[]{:S(2)}) collective-permute-start(bf16[2,256,1024]{2,1,0:T(8,128)(2,1)S(1)} %get-tuple-element.24.imag_ref.refs_5_), channel_id=1, source_target_pairs={{0,1},{1,2},{2,3},{3,0},{4,5},{5,6},{6,7},{7,4},{8,9},{9,10},{10,1... | collective-permute-start | bytes 3145736 | tf_op jit(solution)/shard_map/ppermute | solution.py:289
  58.9 27.1 %collective-permute-start.3 = (bf16[2,256,1024]{2,1,0:T(8,128)(2,1)S(1)}, bf16[2,256,1024]{2,1,0:T(8,128)(2,1)}, u32[]{:S(2)}, u32[]{:S(2)}) collective-permute-start(bf16[2,256,1024]{2,1,0:T(8,128)(2,1)S(1)} %get-tuple-element.25.real_ref.refs_4_), channel_id=1, source_target_pairs={{0,3},{1,0},{2,1},{3,2},{4,7},{5,4},{6,5},{7,6},{8,11},{9,8},{10,9... | collective-permute-start | bytes 3145736 | tf_op jit(solution)/shard_map/ppermute | solution.py:289
  71.0 22.6 %collective-permute-start.7 = (bf16[2,256,1024]{2,1,0:T(8,128)(2,1)}, bf16[2,256,1024]{2,1,0:T(8,128)(2,1)}, u32[]{:S(2)}, u32[]{:S(2)}) collective-permute-start(bf16[2,256,1024]{2,1,0:T(8,128)(2,1)} %collective-permute-done.5.refs_3_), channel_id=1, source_target_pairs={{0,3},{1,0},{2,1},{3,2},{4,7},{5,4},{6,5},{7,6},{8,11},{9,8},{10,9... | collective-permute-start | bytes 3145736 | tf_op jit(solution)/shard_map/ppermute | solution.py:289
  74.8 22.5 %collective-permute-start.6 = (bf16[2,256,1024]{2,1,0:T(8,128)(2,1)}, bf16[2,256,1024]{2,1,0:T(8,128)(2,1)}, u32[]{:S(2)}, u32[]{:S(2)}) collective-permute-start(bf16[2,256,1024]{2,1,0:T(8,128)(2,1)} %collective-permute-done.4.refs_0_), channel_id=1, source_target_pairs={{0,1},{1,2},{2,3},{3,0},{4,5},{5,6},{6,7},{7,4},{8,9},{9,10},{10,1... | collective-permute-start | bytes 3145736 | tf_op jit(solution)/shard_map/ppermute | solution.py:289
  97.3 20.4 %collective-permute-start.8 = (bf16[2,3,2,64,1024]{4,3,2,1,0:T(8,128)(2,1)S(1)}, bf16[2,3,2,64,1024]{4,3,2,1,0:T(8,128)(2,1)S(1)}, u32[]{:S(2)}, u32[]{:S(2)}) collective-permute-start(bf16[2,3,2,64,1024]{4,3,2,1,0:T(8,128)(2,1)S(1)} %get-tuple-element.33), channel_id=1, source_target_pairs={{0,4},{1,5},{2,6},{3,7},{4,8},{5,9},{6,10},{7,11},{8,12},{9,13},{1... | collective-permute-start | bytes 4718600 | tf_op jit(solution)/shard_map/ppermute | solution.py:289
  98.6 50.6 %collective-permute-start.9 = (bf16[2,3,2,64,1024]{4,3,2,1,0:T(8,128)(2,1)}, bf16[2,3,2,64,1024]{4,3,2,1,0:T(8,128)(2,1)S(1)}, u32[]{:S(2)}, u32[]{:S(2)}) collective-permute-start(bf16[2,3,2,64,1024]{4,3,2,1,0:T(8,128)(2,1)} %get-tuple-element.39), channel_id=1, source_target_pairs={{0,12},{1,13},{2,14},{3,15},{4,0},{5,1},{6,2},{7,3},{8,4},{9,5},{1... | collective-permute-start | bytes 4718600 | tf_op jit(solution)/shard_map/ppermute | solution.py:289
  99.3 49.8 %collective-permute-start.10 = (bf16[2,3,2,64,1024]{4,3,2,1,0:T(8,128)(2,1)}, bf16[2,3,2,64,1024]{4,3,2,1,0:T(8,128)(2,1)}, u32[]{:S(2)}, u32[]{:S(2)}) collective-permute-start(bf16[2,3,2,64,1024]{4,3,2,1,0:T(8,128)(2,1)} %get-tuple-element.40), channel_id=1, source_target_pairs={{0,8},{1,9},{2,10},{3,11},{4,12},{5,13},{6,14},{7,15},{8,0},{9,1},... | collective-permute-start | bytes 4718600 | tf_op jit(solution)/shard_map/ppermute | solution.py:289
  105.0 38.9 %collective-permute-start.11 = (bf16[2,1,2,64,1024]{4,3,2,1,0:T(8,128)(2,1)}, bf16[2,1,2,64,1024]{4,3,2,1,0:T(8,128)(2,1)}, u32[]{:S(2)}, u32[]{:S(2)}) collective-permute-start(bf16[2,1,2,64,1024]{4,3,2,1,0:T(8,128)(2,1)} %get-tuple-element.41), channel_id=1, source_target_pairs={{0,4},{1,5},{2,6},{3,7},{4,8},{5,9},{6,10},{7,11},{8,12},{9,13},{1... | collective-permute-start | bytes 1572872 | tf_op jit(solution)/shard_map/ppermute | solution.py:289
  106.0 43.1 %collective-permute-start.12 = (bf16[2,1,2,64,1024]{4,3,2,1,0:T(8,128)(2,1)}, bf16[2,1,2,64,1024]{4,3,2,1,0:T(8,128)(2,1)}, u32[]{:S(2)}, u32[]{:S(2)}) collective-permute-start(bf16[2,1,2,64,1024]{4,3,2,1,0:T(8,128)(2,1)} %get-tuple-element.42), channel_id=1, source_target_pairs={{0,12},{1,13},{2,14},{3,15},{4,0},{5,1},{6,2},{7,3},{8,4},{9,5},{1... | collective-permute-start | bytes 1572872 | tf_op jit(solution)/shard_map/ppermute | solution.py:289
  117.7 31.4 %collective-permute-start.13 = (bf16[2,1,2,64,1024]{4,3,2,1,0:T(8,128)(2,1)}, bf16[2,1,2,64,1024]{4,3,2,1,0:T(8,128)(2,1)}, u32[]{:S(2)}, u32[]{:S(2)}) collective-permute-start(bf16[2,1,2,64,1024]{4,3,2,1,0:T(8,128)(2,1)} %get-tuple-element.43), channel_id=1, source_target_pairs={{0,8},{1,9},{2,10},{3,11},{4,12},{5,13},{6,14},{7,15},{8,0},{9,1},... | collective-permute-start | bytes 1572872 | tf_op jit(solution)/shard_map/ppermute | solution.py:289
  121.4 32.7 %all-to-all-start.1 = ((f32[16,8,128]{2,1,0:T(8,128)}), f32[16,8,128]{2,1,0:T(8,128)S(1)}, u32[]{:S(2)}, u32[]{:S(2)}) async-start(f32[16,8,128]{2,1,0:T(8,128)} %gains.1), calls=%async_computation.1 | async-start | bytes 131072 | tf_op jit(solution)/shard_map/all_to_all | solution.py:412

commit v6 on v5

--- a/solution.py
+++ b/solution.py
@@ -408,7 +408,7 @@
     sent_far = [turn(far_blocks[SHIFTS.index(shift)], 1, shift) for shift in order]
     out_shape = jax.ShapeDtypeStruct((2, tile_count * own, row_count, inputs), jnp.bfloat16)
     visibilities = place(position, [blocks[3], far_blocks[3]], [(0, near), (0, far)], out_shape)
-    gains, sent[0], visibilities = lax.optimization_barrier((gains, sent[0], visibilities))
+    gains, sent[1], visibilities = lax.optimization_barrier((gains, sent[1], visibilities))
     gains = lax.all_to_all(gains, "tile", split_axis=0, concat_axis=0, tiled=True)
     moves = [(shift, steps) for steps in (near, far) for shift in order]
     visibilities = place(position, sent + sent_far, moves, out_shape, visibilities)

time: 155 us -> 154 us (level); the launches traced: 155 us -> 151 us
  waiting for transfers between devices: 33.3 us -> 29.8 us
    ppermute x12, waiting for transfers between devices: 33.3 us -> 29.7 us  [turn(): return lax.ppermute(value, ('chan', 'tile'), pairs)]
where the time goes in v6:
time: 154 us; the launch traced here: 151 us
  starting transfers between devices  44.9 us (29%)
  blocking collectives  37.8 us (25%)
  Pallas kernels  33.6 us (22%)
  waiting for transfers between devices  29.8 us (19%)
  local copies, waits for them, and re-layouts  4.42 us (3%)
    all_to_all x1, blocking collectives, body(): lax.all_to_all(spectra, ('chan', 'tile'), split_axis=0, concat_axis=0, ti...  37.8 us
    ppermute x12, waiting for transfers between devices, turn(): return lax.ppermute(value, ('chan', 'tile'), pairs)  29.7 us
    all_to_all x1, starting transfers between devices, body(): lax.all_to_all(gains, 'tile', split_axis=0, concat_axis=0, tiled=True)  23.1 us
    ppermute x12, starting transfers between devices, turn(): return lax.ppermute(value, ('chan', 'tile'), pairs)  17 us
    pallas_call x1, Pallas kernels, body(): pl.pallas_call(main_kernel, in_specs=[smem] + [vmem] * 6, out_specs=[vmem...  7.38 us
    pallas_call x2, Pallas kernels, place(): pl.pallas_call(functools.partial(place_kernel, moves), in_specs=[pl.Block...  6.88 us
    pallas_call x1, Pallas kernels, body(): pl.pallas_call(gains_kernel, in_specs=[vmem] * 3, out_specs=vmem, out_sha...  6.55 us
    pallas_call x1, Pallas kernels, body(): pl.pallas_call(early_kernel, in_specs=[pl.BlockSpec(memory_space=pltpu.SM...  4.28 us
  transfers between devices with their start and end apart: 15, of which 6 were waited for; matrix products, arithmetic and copies ran while one was open for 1% of the time, Pallas kernels for 19%

profile of v6, /device:TPU:6, one launch (start us, length us, event | category | flops | bytes accessed | tf_op | source)
XLA Modules:
  0.0 151.4 jit_solution(16827722474295889584)
XLA Ops:
  0.7 1.1 slice.10
  1.8 3.5 %collective-permute-start.1 = (bf16[2,64,2048]{2,1,0:T(8,128)(2,1)S(1)}, bf16[2,64,2048]{2,1,0:T(8,128)(2,1)S(1)}, u32[]{:S(2)}, u32[]{:S(2)}) collective-permute-start(bf16[2,64,2048]{2,1,0:T(8,128)(2,1)S(1)} %slice.10), channel_id=1, source_target_pairs={{0,112},{16,0},{32,16},{48,32},{64,48},{80,64},{96,80},{112,96},{1... | collective-permute-start | bytes 1572872 | tf_op jit(solution)/shard_map/ppermute | solution.py:332
  5.3 1.0 slice.9
  6.3 1.3 collective-permute-start
  7.7 1.6 %copy-done = bf16[2,64,8192]{2,1,0:T(8,128)(2,1)S(1)} copy-done((bf16[2,64,8192]{2,1,0:T(8,128)(2,1)S(1)}, bf16[2,64,8192]{2,1,0:T(8,128)(2,1)}, u32[]{:S(2)}) %copy-start) | copy-done | bytes 2097176
  9.3 3.8 %late_spectra.1.late_ref = bf16[128,2,16,128]{3,2,1,0:T(8,128)(2,1)S(1)} custom-call(bf16[2,64,8192]{2,1,0:T(8,128)(2,1)S(1)} %copy-done, f32[16,256]{1,0:T(8,128)S(1)} %copy-done.2, bf16[512,512]{1,0:T(8,128)(2,1)S(1)} %copy-done.1), custom_call_target="tpu_custom_call" | custom-call | flops 1500000000 | bytes 4194304 | tf_op jit(solution)/shard_map/late_spectra/pallas_call | solution.py:336
  13.1 4.3 %early_spectra.1 = bf16[128,2,2,16,128]{4,3,2,1,0:T(8,128)(2,1)S(1)} custom-call(s32[1]{0:T(128)} %bitcast.2.last_ref, bf16[2,64,8192]{2,1,0:T(8,128)(2,1)S(1)} %copy-done, bf16[2,64,1792]{2,1,0:T(8,128)(2,1)S(1)} %collective-permute-done.before_ref, bf16[2,64,2048]{2,1,0:T(8,128)(2,1)S(1)} %collective-permute-done.1.after_ref, ...), custom_call_target="tpu_custom_call" | custom-call | flops 1500000000 | bytes 6291456 | tf_op jit(solution)/shard_map/early_spectra/pallas_call | solution.py:344
  17.4 37.8 %all_to_all.10 = bf16[128,2,2,16,128]{4,3,2,1,0:T(8,128)(2,1)S(1)} all-to-all(bf16[128,2,2,16,128]{4,3,2,1,0:T(8,128)(2,1)S(1)} %early_spectra.1), channel_id=1, replica_groups=mesh['chan'=8,'tile'=16] {'chan','tile'}, dimensions={0} | all-to-all | bytes 4194304 | tf_op jit(solution)/shard_map/all_to_all | solution.py:354
  55.2 0.7 order.1
  55.9 1.0 collective-permute-start.2
  56.9 2.3 %collective-permute-start.5 = (bf16[2,256,1024]{2,1,0:T(8,128)(2,1)S(1)}, bf16[2,256,1024]{2,1,0:T(8,128)(2,1)}, u32[]{:S(2)}, u32[]{:S(2)}) collective-permute-start(bf16[2,256,1024]{2,1,0:T(8,128)(2,1)S(1)} %get-tuple-element.25.imag_ref.refs_5_), channel_id=1, source_target_pairs={{0,3},{1,0},{2,1},{3,2},{4,7},{5,4},{6,5},{7,6},{8,11},{9,8},{10,9... | collective-permute-start | bytes 3145736 | tf_op jit(solution)/shard_map/ppermute | solution.py:289
  59.2 1.5 collective-permute-start.4
  60.7 0.5 collective-permute-start.3
  61.3 10.9 %collective-permute-done.2.refs_0_ = bf16[2,256,1024]{2,1,0:T(8,128)(2,1)} collective-permute-done((bf16[2,256,1024]{2,1,0:T(8,128)(2,1)S(1)}, bf16[2,256,1024]{2,1,0:T(8,128)(2,1)}, u32[]{:S(2)}, u32[]{:S(2)}) %collective-permute-start.2) | collective-permute-done | bytes 1048608 | tf_op jit(solution)/shard_map/ppermute | solution.py:289
  72.1 3.2 %collective-permute-start.7 = (bf16[2,256,1024]{2,1,0:T(8,128)(2,1)}, bf16[2,256,1024]{2,1,0:T(8,128)(2,1)}, u32[]{:S(2)}, u32[]{:S(2)}) collective-permute-start(bf16[2,256,1024]{2,1,0:T(8,128)(2,1)} %collective-permute-done.5.refs_3_), channel_id=1, source_target_pairs={{0,3},{1,0},{2,1},{3,2},{4,7},{5,4},{6,5},{7,6},{8,11},{9,8},{10,9... | collective-permute-start | bytes 3145736 | tf_op jit(solution)/shard_map/ppermute | solution.py:289
  75.4 6.6 %gains.1 = f32[16,8,128]{2,1,0:T(8,128)} custom-call(bf16[2,256,1024]{2,1,0:T(8,128)(2,1)S(1)} %get-tuple-element.24.real_ref.refs_4_, bf16[2,256,1024]{2,1,0:T(8,128)(2,1)S(1)} %get-tuple-element.25.imag_ref.refs_5_, s32[1,1024]{1,0:T(1,128)S(1)} %bitcast.10), custom_call_target="tpu_custom_call" | custom-call | flops 33554432 | bytes 2097152 | tf_op jit(solution)/shard_map/gains/pallas_call | solution.py:373
  82.0 1.1 collective-permute-done.4.refs_2_
  83.3 7.4 %main_sums.1 = (bf16[2,3,2,64,1024]{4,3,2,1,0:T(8,128)(2,1)}, bf16[2,3,2,64,1024]{4,3,2,1,0:T(8,128)(2,1)S(1)}, bf16[2,3,2,64,1024]{4,3,2,1,0:T(8,128)(2,1)}, bf16[2,3,2,64,1024]{4,3,2,1,0:T(8,128)(2,1)S(1)}) custom-call(s32[2]{0:T(128)S(1)} %pad_add_fusion.position_ref, bf16[2,256,1024]{2,1,0:T(8,128)(2,1)} %collective-permute-done.2.refs_0_, ...), custom_call_target="tpu_custom_call" | custom-call | flops 3221225472 | bytes 12582912 | tf_op jit(solution)/shard_map/main_sums/pallas_call | solution.py:385
  90.7 3.9 %collective-permute-done.6.refs_0_ = bf16[2,256,1024]{2,1,0:T(8,128)(2,1)} collective-permute-done((bf16[2,256,1024]{2,1,0:T(8,128)(2,1)}, bf16[2,256,1024]{2,1,0:T(8,128)(2,1)}, u32[]{:S(2)}, u32[]{:S(2)}) %collective-permute-start.6) | collective-permute-done | bytes 1048608 | tf_op jit(solution)/shard_map/ppermute | solution.py:289
  94.6 1.8 %collective-permute-start.9 = (bf16[2,3,2,64,1024]{4,3,2,1,0:T(8,128)(2,1)S(1)}, bf16[2,3,2,64,1024]{4,3,2,1,0:T(8,128)(2,1)S(1)}, u32[]{:S(2)}, u32[]{:S(2)}) collective-permute-start(bf16[2,3,2,64,1024]{4,3,2,1,0:T(8,128)(2,1)S(1)} %get-tuple-element.34), channel_id=1, source_target_pairs={{0,12},{1,13},{2,14},{3,15},{4,0},{5,1},{6,2},{7,3},{8,4},{9,5},{1... | collective-permute-start | bytes 4718600 | tf_op jit(solution)/shard_map/ppermute | solution.py:289
  96.3 1.5 collective-permute-start.8
  97.8 1.6 %collective-permute-start.10 = (bf16[2,3,2,64,1024]{4,3,2,1,0:T(8,128)(2,1)}, bf16[2,3,2,64,1024]{4,3,2,1,0:T(8,128)(2,1)}, u32[]{:S(2)}, u32[]{:S(2)}) collective-permute-start(bf16[2,3,2,64,1024]{4,3,2,1,0:T(8,128)(2,1)} %get-tuple-element.40), channel_id=1, source_target_pairs={{0,8},{1,9},{2,10},{3,11},{4,12},{5,13},{6,14},{7,15},{8,0},{9,1},... | collective-permute-start | bytes 4718600 | tf_op jit(solution)/shard_map/ppermute | solution.py:289
  99.4 4.0 %far_sums.1 = (bf16[2,1,2,64,1024]{4,3,2,1,0:T(8,128)(2,1)}, bf16[2,1,2,64,1024]{4,3,2,1,0:T(8,128)(2,1)}, bf16[2,1,2,64,1024]{4,3,2,1,0:T(8,128)(2,1)}, bf16[2,1,2,64,1024]{4,3,2,1,0:T(8,128)(2,1)S(1)}) custom-call(s32[2]{0:T(128)S(1)} %pad_add_fusion.position_ref, bf16[2,256,1024]{2,1,0:T(8,128)(2,1)} %collective-permute-done.6.refs_0_, ...), custom_call_target="tpu_custom_call" | custom-call | flops 1073741824 | bytes 4194304 | tf_op jit(solution)/shard_map/far_sums/pallas_call | solution.py:395
  103.5 1.6 %collective-permute-start.11 = (bf16[2,1,2,64,1024]{4,3,2,1,0:T(8,128)(2,1)}, bf16[2,1,2,64,1024]{4,3,2,1,0:T(8,128)(2,1)}, u32[]{:S(2)}, u32[]{:S(2)}) collective-permute-start(bf16[2,1,2,64,1024]{4,3,2,1,0:T(8,128)(2,1)} %get-tuple-element.41), channel_id=1, source_target_pairs={{0,4},{1,5},{2,6},{3,7},{4,8},{5,9},{6,10},{7,11},{8,12},{9,13},{1... | collective-permute-start | bytes 1572872 | tf_op jit(solution)/shard_map/ppermute | solution.py:289
  105.1 0.4 collective-permute-start.12
  105.5 10.7 %collective-permute-done.9.refs_1_ = bf16[2,3,2,64,1024]{4,3,2,1,0:T(8,128)(2,1)S(1)} collective-permute-done((bf16[2,3,2,64,1024]{4,3,2,1,0:T(8,128)(2,1)S(1)}, bf16[2,3,2,64,1024]{4,3,2,1,0:T(8,128)(2,1)S(1)}, u32[]{:S(2)}, u32[]{:S(2)}) %collective-permute-start.9) | collective-permute-done | bytes 1572896 | tf_op jit(solution)/shard_map/ppermute | solution.py:289
  116.2 1.6 %collective-permute-start.13 = (bf16[2,1,2,64,1024]{4,3,2,1,0:T(8,128)(2,1)}, bf16[2,1,2,64,1024]{4,3,2,1,0:T(8,128)(2,1)}, u32[]{:S(2)}, u32[]{:S(2)}) collective-permute-start(bf16[2,1,2,64,1024]{4,3,2,1,0:T(8,128)(2,1)} %get-tuple-element.43), channel_id=1, source_target_pairs={{0,8},{1,9},{2,10},{3,11},{4,12},{5,13},{6,14},{7,15},{8,0},{9,1},... | collective-permute-start | bytes 1572872 | tf_op jit(solution)/shard_map/ppermute | solution.py:289
  117.8 2.0 %place.2.refs_6_ = bf16[2,32,64,1024]{3,2,1,0:T(8,128)(2,1)} custom-call(s32[2]{0:T(128)S(1)} %pad_add_fusion.position_ref, bf16[2,3,2,64,1024]{4,3,2,1,0:T(8,128)(2,1)S(1)} %get-tuple-element.35.refs_0_, bf16[2,1,2,64,1024]{4,3,2,1,0:T(8,128)(2,1)S(1)} %get-tuple-element.38.refs_1_), custom_call_target="tpu_custom_call" | custom-call | bytes 8388608 | tf_op jit(solution)/shard_map/place/pallas_call | solution.py:295
  119.8 23.1 %all-to-all-start.1 = ((f32[16,8,128]{2,1,0:T(8,128)}), f32[16,8,128]{2,1,0:T(8,128)S(1)}, u32[]{:S(2)}, u32[]{:S(2)}) async-start(f32[16,8,128]{2,1,0:T(8,128)} %gains.1), calls=%async_computation.1 | async-start | bytes 131072 | tf_op jit(solution)/shard_map/all_to_all | solution.py:412
  142.9 2.9 %collective-permute-done.13.refs_5_ = bf16[2,1,2,64,1024]{4,3,2,1,0:T(8,128)(2,1)} collective-permute-done((bf16[2,1,2,64,1024]{4,3,2,1,0:T(8,128)(2,1)}, bf16[2,1,2,64,1024]{4,3,2,1,0:T(8,128)(2,1)}, u32[]{:S(2)}, u32[]{:S(2)}) %collective-permute-start.13) | collective-permute-done | bytes 524320 | tf_op jit(solution)/shard_map/ppermute | solution.py:289
  145.8 4.9 %place.3 = bf16[2,32,64,1024]{3,2,1,0:T(8,128)(2,1)} custom-call(s32[2]{0:T(128)S(1)} %pad_add_fusion.position_ref, bf16[2,3,2,64,1024]{4,3,2,1,0:T(8,128)(2,1)S(1)} %collective-permute-done.8.refs_0_, bf16[2,3,2,64,1024]{4,3,2,1,0:T(8,128)(2,1)S(1)} %collective-permute-done.9.refs_1_, ...), custom_call_target="tpu_custom_call", output_to_operand_aliasing={{}: (7, {})} | custom-call | bytes 25165824 | tf_op jit(solution)/shard_map/place/pallas_call | solution.py:295
  150.7 0.6 copy.7
  (20 shorter events, 0.4 us)
Async XLA Ops:
  0.6 7.0 %copy-start.1 = (bf16[512,512]{1,0:T(8,128)(2,1)S(1)}, bf16[512,512]{1,0:T(8,128)(2,1)}, u32[]{:S(2)}) copy-start(bf16[512,512]{1,0:T(8,128)(2,1)} %constant.29.clone.table_ref) | copy-start | bytes 1572868
  0.6 7.0 %copy-start.2 = (f32[16,256]{1,0:T(8,128)S(1)}, f32[16,256]{1,0:T(8,128)}, u32[]{:S(2)}) copy-start(f32[16,256]{1,0:T(8,128)} %constant.28.clone.taps_ref) | copy-start | bytes 49156
  1.8 11.3 %collective-permute-start.1 = (bf16[2,64,2048]{2,1,0:T(8,128)(2,1)S(1)}, bf16[2,64,2048]{2,1,0:T(8,128)(2,1)S(1)}, u32[]{:S(2)}, u32[]{:S(2)}) collective-permute-start(bf16[2,64,2048]{2,1,0:T(8,128)(2,1)S(1)} %slice.10), channel_id=1, source_target_pairs={{0,112},{16,0},{32,16},{48,32},{64,48},{80,64},{96,80},{112,96},{1... | collective-permute-start | bytes 1572872 | tf_op jit(solution)/shard_map/ppermute | solution.py:332
  6.3 6.7 %collective-permute-start = (bf16[2,64,1792]{2,1,0:T(8,128)(2,1)S(1)}, bf16[2,64,1792]{2,1,0:T(8,128)(2,1)S(1)}, u32[]{:S(2)}, u32[]{:S(2)}) collective-permute-start(bf16[2,64,1792]{2,1,0:T(8,128)(2,1)S(1)} %slice.9), channel_id=1, source_target_pairs={{0,16},{16,32},{32,48},{48,64},{64,80},{80,96},{96,112},{1,17},{17... | collective-permute-start | bytes 1376264 | tf_op jit(solution)/shard_map/ppermute | solution.py:329
  7.7 1.6 %copy-start = (bf16[2,64,8192]{2,1,0:T(8,128)(2,1)S(1)}, bf16[2,64,8192]{2,1,0:T(8,128)(2,1)}, u32[]{:S(2)}) copy-start(bf16[2,64,8192]{2,1,0:T(8,128)(2,1)} %v_ref.3) | copy-start | bytes 6291460
  55.2 20.2 %copy-start.3 = (s32[1024]{0:T(1024)S(1)}, s32[1024]{0:T(1024)}, u32[]{:S(2)}) copy-start(s32[1024]{0:T(1024)} %param.5) | copy-start | bytes 12292
  55.9 16.2 %collective-permute-start.2 = (bf16[2,256,1024]{2,1,0:T(8,128)(2,1)S(1)}, bf16[2,256,1024]{2,1,0:T(8,128)(2,1)}, u32[]{:S(2)}, u32[]{:S(2)}) collective-permute-start(bf16[2,256,1024]{2,1,0:T(8,128)(2,1)S(1)} %get-tuple-element.24.real_ref.refs_4_), channel_id=1, source_target_pairs={{0,1},{1,2},{2,3},{3,0},{4,5},{5,6},{6,7},{7,4},{8,9},{9,10},{10,1... | collective-permute-start | bytes 3145736 | tf_op jit(solution)/shard_map/ppermute | solution.py:289
  56.9 15.2 %collective-permute-start.5 = (bf16[2,256,1024]{2,1,0:T(8,128)(2,1)S(1)}, bf16[2,256,1024]{2,1,0:T(8,128)(2,1)}, u32[]{:S(2)}, u32[]{:S(2)}) collective-permute-start(bf16[2,256,1024]{2,1,0:T(8,128)(2,1)S(1)} %get-tuple-element.25.imag_ref.refs_5_), channel_id=1, source_target_pairs={{0,3},{1,0},{2,1},{3,2},{4,7},{5,4},{6,5},{7,6},{8,11},{9,8},{10,9... | collective-permute-start | bytes 3145736 | tf_op jit(solution)/shard_map/ppermute | solution.py:289
  59.2 23.8 %collective-permute-start.4 = (bf16[2,256,1024]{2,1,0:T(8,128)(2,1)S(1)}, bf16[2,256,1024]{2,1,0:T(8,128)(2,1)}, u32[]{:S(2)}, u32[]{:S(2)}) collective-permute-start(bf16[2,256,1024]{2,1,0:T(8,128)(2,1)S(1)} %get-tuple-element.24.real_ref.refs_4_), channel_id=1, source_target_pairs={{0,3},{1,0},{2,1},{3,2},{4,7},{5,4},{6,5},{7,6},{8,11},{9,8},{10,9... | collective-permute-start | bytes 3145736 | tf_op jit(solution)/shard_map/ppermute | solution.py:289
  60.7 22.6 %collective-permute-start.3 = (bf16[2,256,1024]{2,1,0:T(8,128)(2,1)S(1)}, bf16[2,256,1024]{2,1,0:T(8,128)(2,1)}, u32[]{:S(2)}, u32[]{:S(2)}) collective-permute-start(bf16[2,256,1024]{2,1,0:T(8,128)(2,1)S(1)} %get-tuple-element.25.imag_ref.refs_5_), channel_id=1, source_target_pairs={{0,1},{1,2},{2,3},{3,0},{4,5},{5,6},{6,7},{7,4},{8,9},{9,10},{10,1... | collective-permute-start | bytes 3145736 | tf_op jit(solution)/shard_map/ppermute | solution.py:289
  72.1 22.5 %collective-permute-start.6 = (bf16[2,256,1024]{2,1,0:T(8,128)(2,1)}, bf16[2,256,1024]{2,1,0:T(8,128)(2,1)}, u32[]{:S(2)}, u32[]{:S(2)}) collective-permute-start(bf16[2,256,1024]{2,1,0:T(8,128)(2,1)} %collective-permute-done.2.refs_0_), channel_id=1, source_target_pairs={{0,1},{1,2},{2,3},{3,0},{4,5},{5,6},{6,7},{7,4},{8,9},{9,10},{10,1... | collective-permute-start | bytes 3145736 | tf_op jit(solution)/shard_map/ppermute | solution.py:289
  72.1 22.5 %collective-permute-start.7 = (bf16[2,256,1024]{2,1,0:T(8,128)(2,1)}, bf16[2,256,1024]{2,1,0:T(8,128)(2,1)}, u32[]{:S(2)}, u32[]{:S(2)}) collective-permute-start(bf16[2,256,1024]{2,1,0:T(8,128)(2,1)} %collective-permute-done.5.refs_3_), channel_id=1, source_target_pairs={{0,3},{1,0},{2,1},{3,2},{4,7},{5,4},{6,5},{7,6},{8,11},{9,8},{10,9... | collective-permute-start | bytes 3145736 | tf_op jit(solution)/shard_map/ppermute | solution.py:289
  94.6 21.6 %collective-permute-start.9 = (bf16[2,3,2,64,1024]{4,3,2,1,0:T(8,128)(2,1)S(1)}, bf16[2,3,2,64,1024]{4,3,2,1,0:T(8,128)(2,1)S(1)}, u32[]{:S(2)}, u32[]{:S(2)}) collective-permute-start(bf16[2,3,2,64,1024]{4,3,2,1,0:T(8,128)(2,1)S(1)} %get-tuple-element.34), channel_id=1, source_target_pairs={{0,12},{1,13},{2,14},{3,15},{4,0},{5,1},{6,2},{7,3},{8,4},{9,5},{1... | collective-permute-start | bytes 4718600 | tf_op jit(solution)/shard_map/ppermute | solution.py:289
  96.3 49.5 %collective-permute-start.8 = (bf16[2,3,2,64,1024]{4,3,2,1,0:T(8,128)(2,1)}, bf16[2,3,2,64,1024]{4,3,2,1,0:T(8,128)(2,1)S(1)}, u32[]{:S(2)}, u32[]{:S(2)}) collective-permute-start(bf16[2,3,2,64,1024]{4,3,2,1,0:T(8,128)(2,1)} %get-tuple-element.32), channel_id=1, source_target_pairs={{0,4},{1,5},{2,6},{3,7},{4,8},{5,9},{6,10},{7,11},{8,12},{9,13},{1... | collective-permute-start | bytes 4718600 | tf_op jit(solution)/shard_map/ppermute | solution.py:289
  97.8 48.0 %collective-permute-start.10 = (bf16[2,3,2,64,1024]{4,3,2,1,0:T(8,128)(2,1)}, bf16[2,3,2,64,1024]{4,3,2,1,0:T(8,128)(2,1)}, u32[]{:S(2)}, u32[]{:S(2)}) collective-permute-start(bf16[2,3,2,64,1024]{4,3,2,1,0:T(8,128)(2,1)} %get-tuple-element.40), channel_id=1, source_target_pairs={{0,8},{1,9},{2,10},{3,11},{4,12},{5,13},{6,14},{7,15},{8,0},{9,1},... | collective-permute-start | bytes 4718600 | tf_op jit(solution)/shard_map/ppermute | solution.py:289
  103.5 39.4 %collective-permute-start.11 = (bf16[2,1,2,64,1024]{4,3,2,1,0:T(8,128)(2,1)}, bf16[2,1,2,64,1024]{4,3,2,1,0:T(8,128)(2,1)}, u32[]{:S(2)}, u32[]{:S(2)}) collective-permute-start(bf16[2,1,2,64,1024]{4,3,2,1,0:T(8,128)(2,1)} %get-tuple-element.41), channel_id=1, source_target_pairs={{0,4},{1,5},{2,6},{3,7},{4,8},{5,9},{6,10},{7,11},{8,12},{9,13},{1... | collective-permute-start | bytes 1572872 | tf_op jit(solution)/shard_map/ppermute | solution.py:289
  105.1 37.8 %collective-permute-start.12 = (bf16[2,1,2,64,1024]{4,3,2,1,0:T(8,128)(2,1)}, bf16[2,1,2,64,1024]{4,3,2,1,0:T(8,128)(2,1)}, u32[]{:S(2)}, u32[]{:S(2)}) collective-permute-start(bf16[2,1,2,64,1024]{4,3,2,1,0:T(8,128)(2,1)} %get-tuple-element.42), channel_id=1, source_target_pairs={{0,12},{1,13},{2,14},{3,15},{4,0},{5,1},{6,2},{7,3},{8,4},{9,5},{1... | collective-permute-start | bytes 1572872 | tf_op jit(solution)/shard_map/ppermute | solution.py:289
  116.2 29.6 %collective-permute-start.13 = (bf16[2,1,2,64,1024]{4,3,2,1,0:T(8,128)(2,1)}, bf16[2,1,2,64,1024]{4,3,2,1,0:T(8,128)(2,1)}, u32[]{:S(2)}, u32[]{:S(2)}) collective-permute-start(bf16[2,1,2,64,1024]{4,3,2,1,0:T(8,128)(2,1)} %get-tuple-element.43), channel_id=1, source_target_pairs={{0,8},{1,9},{2,10},{3,11},{4,12},{5,13},{6,14},{7,15},{8,0},{9,1},... | collective-permute-start | bytes 1572872 | tf_op jit(solution)/shard_map/ppermute | solution.py:289
  119.8 30.9 %all-to-all-start.1 = ((f32[16,8,128]{2,1,0:T(8,128)}), f32[16,8,128]{2,1,0:T(8,128)S(1)}, u32[]{:S(2)}, u32[]{:S(2)}) async-start(f32[16,8,128]{2,1,0:T(8,128)} %gains.1), calls=%async_computation.1 | async-start | bytes 131072 | tf_op jit(solution)/shard_map/all_to_all | solution.py:412

commit v7 on v6

--- a/solution.py
+++ b/solution.py
@@ -375,7 +375,7 @@
         in_specs=[vmem] * 3,
         out_specs=vmem,
         out_shape=jax.ShapeDtypeStruct((tile_count, 8, 128), jnp.float32),
-        compiler_params=params(),
+        compiler_params=params(12),
         cost_estimate=cost(own * inputs * samples * 64, 2 << 20),
         name="gains",
     )(real, imag, flags.reshape(1, inputs))
@@ -397,7 +397,7 @@
         in_specs=[smem] + [vmem] * 2,
         out_specs=[vmem] * 4,
         out_shape=[jax.ShapeDtypeStruct((own, 1, 2, row_count, inputs), jnp.bfloat16)] * 4,
-        compiler_params=params(),
+        compiler_params=params(14),
         cost_estimate=cost(2 * flops, 4 << 20),
         name="far_sums",
     )(position, far_real, far_imag)

time: 154 us -> 154 us (level)
  no operation moved by 1% of the time
where the time goes in v7:
time: 154 us; the launch traced here: 151 us
  starting transfers between devices  44.9 us (29%)
  blocking collectives  37.8 us (25%)
  Pallas kernels  33.6 us (22%)
  waiting for transfers between devices  29.8 us (19%)
  local copies, waits for them, and re-layouts  4.42 us (3%)
    all_to_all x1, blocking collectives, body(): lax.all_to_all(spectra, ('chan', 'tile'), split_axis=0, concat_axis=0, ti...  37.8 us
    ppermute x12, waiting for transfers between devices, turn(): return lax.ppermute(value, ('chan', 'tile'), pairs)  29.7 us
    all_to_all x1, starting transfers between devices, body(): lax.all_to_all(gains, 'tile', split_axis=0, concat_axis=0, tiled=True)  23.1 us
    ppermute x12, starting transfers between devices, turn(): return lax.ppermute(value, ('chan', 'tile'), pairs)  17 us
    pallas_call x1, Pallas kernels, body(): pl.pallas_call(main_kernel, in_specs=[smem] + [vmem] * 6, out_specs=[vmem...  7.38 us
    pallas_call x2, Pallas kernels, place(): pl.pallas_call(functools.partial(place_kernel, moves), in_specs=[pl.Block...  6.88 us
    pallas_call x1, Pallas kernels, body(): pl.pallas_call(gains_kernel, in_specs=[vmem] * 3, out_specs=vmem, out_sha...  6.55 us
    pallas_call x1, Pallas kernels, body(): pl.pallas_call(early_kernel, in_specs=[pl.BlockSpec(memory_space=pltpu.SM...  4.28 us
  transfers between devices with their start and end apart: 15, of which 6 were waited for; matrix products, arithmetic and copies ran while one was open for 1% of the time, Pallas kernels for 19%

profile of v7, /device:TPU:6, one launch (start us, length us, event | category | flops | bytes accessed | tf_op | source)
XLA Modules:
  0.0 151.4 jit_solution(5601582579745458777)
XLA Ops:
  0.7 1.1 slice.10
  1.8 3.5 %collective-permute-start.1 = (bf16[2,64,2048]{2,1,0:T(8,128)(2,1)S(1)}, bf16[2,64,2048]{2,1,0:T(8,128)(2,1)S(1)}, u32[]{:S(2)}, u32[]{:S(2)}) collective-permute-start(bf16[2,64,2048]{2,1,0:T(8,128)(2,1)S(1)} %slice.10), channel_id=1, source_target_pairs={{0,112},{16,0},{32,16},{48,32},{64,48},{80,64},{96,80},{112,96},{1... | collective-permute-start | bytes 1572872 | tf_op jit(solution)/shard_map/ppermute | solution.py:332
  5.3 1.0 slice.9
  6.3 1.3 collective-permute-start
  7.7 1.6 %copy-done = bf16[2,64,8192]{2,1,0:T(8,128)(2,1)S(1)} copy-done((bf16[2,64,8192]{2,1,0:T(8,128)(2,1)S(1)}, bf16[2,64,8192]{2,1,0:T(8,128)(2,1)}, u32[]{:S(2)}) %copy-start) | copy-done | bytes 2097176
  9.3 3.8 %late_spectra.1.late_ref = bf16[128,2,16,128]{3,2,1,0:T(8,128)(2,1)S(1)} custom-call(bf16[2,64,8192]{2,1,0:T(8,128)(2,1)S(1)} %copy-done, f32[16,256]{1,0:T(8,128)S(1)} %copy-done.2, bf16[512,512]{1,0:T(8,128)(2,1)S(1)} %copy-done.1), custom_call_target="tpu_custom_call" | custom-call | flops 1500000000 | bytes 4194304 | tf_op jit(solution)/shard_map/late_spectra/pallas_call | solution.py:336
  13.1 4.3 %early_spectra.1 = bf16[128,2,2,16,128]{4,3,2,1,0:T(8,128)(2,1)S(1)} custom-call(s32[1]{0:T(128)} %bitcast.2.last_ref, bf16[2,64,8192]{2,1,0:T(8,128)(2,1)S(1)} %copy-done, bf16[2,64,1792]{2,1,0:T(8,128)(2,1)S(1)} %collective-permute-done.before_ref, bf16[2,64,2048]{2,1,0:T(8,128)(2,1)S(1)} %collective-permute-done.1.after_ref, ...), custom_call_target="tpu_custom_call" | custom-call | flops 1500000000 | bytes 6291456 | tf_op jit(solution)/shard_map/early_spectra/pallas_call | solution.py:344
  17.4 37.8 %all_to_all.10 = bf16[128,2,2,16,128]{4,3,2,1,0:T(8,128)(2,1)S(1)} all-to-all(bf16[128,2,2,16,128]{4,3,2,1,0:T(8,128)(2,1)S(1)} %early_spectra.1), channel_id=1, replica_groups=mesh['chan'=8,'tile'=16] {'chan','tile'}, dimensions={0} | all-to-all | bytes 4194304 | tf_op jit(solution)/shard_map/all_to_all | solution.py:354
  55.2 0.7 order.1
  55.9 1.0 collective-permute-start.2
  56.9 2.3 %collective-permute-start.5 = (bf16[2,256,1024]{2,1,0:T(8,128)(2,1)S(1)}, bf16[2,256,1024]{2,1,0:T(8,128)(2,1)}, u32[]{:S(2)}, u32[]{:S(2)}) collective-permute-start(bf16[2,256,1024]{2,1,0:T(8,128)(2,1)S(1)} %get-tuple-element.25.imag_ref.refs_5_), channel_id=1, source_target_pairs={{0,3},{1,0},{2,1},{3,2},{4,7},{5,4},{6,5},{7,6},{8,11},{9,8},{10,9... | collective-permute-start | bytes 3145736 | tf_op jit(solution)/shard_map/ppermute | solution.py:289
  59.2 1.5 collective-permute-start.4
  60.7 0.5 collective-permute-start.3
  61.3 10.9 %collective-permute-done.2.refs_0_ = bf16[2,256,1024]{2,1,0:T(8,128)(2,1)} collective-permute-done((bf16[2,256,1024]{2,1,0:T(8,128)(2,1)S(1)}, bf16[2,256,1024]{2,1,0:T(8,128)(2,1)}, u32[]{:S(2)}, u32[]{:S(2)}) %collective-permute-start.2) | collective-permute-done | bytes 1048608 | tf_op jit(solution)/shard_map/ppermute | solution.py:289
  72.1 3.2 %collective-permute-start.7 = (bf16[2,256,1024]{2,1,0:T(8,128)(2,1)}, bf16[2,256,1024]{2,1,0:T(8,128)(2,1)}, u32[]{:S(2)}, u32[]{:S(2)}) collective-permute-start(bf16[2,256,1024]{2,1,0:T(8,128)(2,1)} %collective-permute-done.5.refs_3_), channel_id=1, source_target_pairs={{0,3},{1,0},{2,1},{3,2},{4,7},{5,4},{6,5},{7,6},{8,11},{9,8},{10,9... | collective-permute-start | bytes 3145736 | tf_op jit(solution)/shard_map/ppermute | solution.py:289
  75.4 6.6 %gains.1 = f32[16,8,128]{2,1,0:T(8,128)} custom-call(bf16[2,256,1024]{2,1,0:T(8,128)(2,1)S(1)} %get-tuple-element.24.real_ref.refs_4_, bf16[2,256,1024]{2,1,0:T(8,128)(2,1)S(1)} %get-tuple-element.25.imag_ref.refs_5_, s32[1,1024]{1,0:T(1,128)S(1)} %bitcast.10), custom_call_target="tpu_custom_call" | custom-call | flops 33554432 | bytes 2097152 | tf_op jit(solution)/shard_map/gains/pallas_call | solution.py:373
  82.0 1.1 collective-permute-done.4.refs_2_
  83.3 7.4 %main_sums.1 = (bf16[2,3,2,64,1024]{4,3,2,1,0:T(8,128)(2,1)}, bf16[2,3,2,64,1024]{4,3,2,1,0:T(8,128)(2,1)S(1)}, bf16[2,3,2,64,1024]{4,3,2,1,0:T(8,128)(2,1)}, bf16[2,3,2,64,1024]{4,3,2,1,0:T(8,128)(2,1)S(1)}) custom-call(s32[2]{0:T(128)S(1)} %pad_add_fusion.position_ref, bf16[2,256,1024]{2,1,0:T(8,128)(2,1)} %collective-permute-done.2.refs_0_, ...), custom_call_target="tpu_custom_call" | custom-call | flops 3221225472 | bytes 12582912 | tf_op jit(solution)/shard_map/main_sums/pallas_call | solution.py:385
  90.7 3.9 %collective-permute-done.6.refs_0_ = bf16[2,256,1024]{2,1,0:T(8,128)(2,1)} collective-permute-done((bf16[2,256,1024]{2,1,0:T(8,128)(2,1)}, bf16[2,256,1024]{2,1,0:T(8,128)(2,1)}, u32[]{:S(2)}, u32[]{:S(2)}) %collective-permute-start.6) | collective-permute-done | bytes 1048608 | tf_op jit(solution)/shard_map/ppermute | solution.py:289
  94.6 1.8 %collective-permute-start.9 = (bf16[2,3,2,64,1024]{4,3,2,1,0:T(8,128)(2,1)S(1)}, bf16[2,3,2,64,1024]{4,3,2,1,0:T(8,128)(2,1)S(1)}, u32[]{:S(2)}, u32[]{:S(2)}) collective-permute-start(bf16[2,3,2,64,1024]{4,3,2,1,0:T(8,128)(2,1)S(1)} %get-tuple-element.34), channel_id=1, source_target_pairs={{0,12},{1,13},{2,14},{3,15},{4,0},{5,1},{6,2},{7,3},{8,4},{9,5},{1... | collective-permute-start | bytes 4718600 | tf_op jit(solution)/shard_map/ppermute | solution.py:289
  96.3 1.5 collective-permute-start.8
  97.8 1.6 %collective-permute-start.10 = (bf16[2,3,2,64,1024]{4,3,2,1,0:T(8,128)(2,1)}, bf16[2,3,2,64,1024]{4,3,2,1,0:T(8,128)(2,1)}, u32[]{:S(2)}, u32[]{:S(2)}) collective-permute-start(bf16[2,3,2,64,1024]{4,3,2,1,0:T(8,128)(2,1)} %get-tuple-element.40), channel_id=1, source_target_pairs={{0,8},{1,9},{2,10},{3,11},{4,12},{5,13},{6,14},{7,15},{8,0},{9,1},... | collective-permute-start | bytes 4718600 | tf_op jit(solution)/shard_map/ppermute | solution.py:289
  99.4 4.0 %far_sums.1 = (bf16[2,1,2,64,1024]{4,3,2,1,0:T(8,128)(2,1)}, bf16[2,1,2,64,1024]{4,3,2,1,0:T(8,128)(2,1)}, bf16[2,1,2,64,1024]{4,3,2,1,0:T(8,128)(2,1)}, bf16[2,1,2,64,1024]{4,3,2,1,0:T(8,128)(2,1)S(1)}) custom-call(s32[2]{0:T(128)S(1)} %pad_add_fusion.position_ref, bf16[2,256,1024]{2,1,0:T(8,128)(2,1)} %collective-permute-done.6.refs_0_, ...), custom_call_target="tpu_custom_call" | custom-call | flops 1073741824 | bytes 4194304 | tf_op jit(solution)/shard_map/far_sums/pallas_call | solution.py:395
  103.5 1.6 %collective-permute-start.11 = (bf16[2,1,2,64,1024]{4,3,2,1,0:T(8,128)(2,1)}, bf16[2,1,2,64,1024]{4,3,2,1,0:T(8,128)(2,1)}, u32[]{:S(2)}, u32[]{:S(2)}) collective-permute-start(bf16[2,1,2,64,1024]{4,3,2,1,0:T(8,128)(2,1)} %get-tuple-element.41), channel_id=1, source_target_pairs={{0,4},{1,5},{2,6},{3,7},{4,8},{5,9},{6,10},{7,11},{8,12},{9,13},{1... | collective-permute-start | bytes 1572872 | tf_op jit(solution)/shard_map/ppermute | solution.py:289
  105.1 0.4 collective-permute-start.12
  105.5 10.7 %collective-permute-done.9.refs_1_ = bf16[2,3,2,64,1024]{4,3,2,1,0:T(8,128)(2,1)S(1)} collective-permute-done((bf16[2,3,2,64,1024]{4,3,2,1,0:T(8,128)(2,1)S(1)}, bf16[2,3,2,64,1024]{4,3,2,1,0:T(8,128)(2,1)S(1)}, u32[]{:S(2)}, u32[]{:S(2)}) %collective-permute-start.9) | collective-permute-done | bytes 1572896 | tf_op jit(solution)/shard_map/ppermute | solution.py:289
  116.2 1.6 %collective-permute-start.13 = (bf16[2,1,2,64,1024]{4,3,2,1,0:T(8,128)(2,1)}, bf16[2,1,2,64,1024]{4,3,2,1,0:T(8,128)(2,1)}, u32[]{:S(2)}, u32[]{:S(2)}) collective-permute-start(bf16[2,1,2,64,1024]{4,3,2,1,0:T(8,128)(2,1)} %get-tuple-element.43), channel_id=1, source_target_pairs={{0,8},{1,9},{2,10},{3,11},{4,12},{5,13},{6,14},{7,15},{8,0},{9,1},... | collective-permute-start | bytes 1572872 | tf_op jit(solution)/shard_map/ppermute | solution.py:289
  117.8 2.0 %place.2.refs_6_ = bf16[2,32,64,1024]{3,2,1,0:T(8,128)(2,1)} custom-call(s32[2]{0:T(128)S(1)} %pad_add_fusion.position_ref, bf16[2,3,2,64,1024]{4,3,2,1,0:T(8,128)(2,1)S(1)} %get-tuple-element.35.refs_0_, bf16[2,1,2,64,1024]{4,3,2,1,0:T(8,128)(2,1)S(1)} %get-tuple-element.38.refs_1_), custom_call_target="tpu_custom_call" | custom-call | bytes 8388608 | tf_op jit(solution)/shard_map/place/pallas_call | solution.py:295
  119.8 23.1 %all-to-all-start.1 = ((f32[16,8,128]{2,1,0:T(8,128)}), f32[16,8,128]{2,1,0:T(8,128)S(1)}, u32[]{:S(2)}, u32[]{:S(2)}) async-start(f32[16,8,128]{2,1,0:T(8,128)} %gains.1), calls=%async_computation.1 | async-start | bytes 131072 | tf_op jit(solution)/shard_map/all_to_all | solution.py:412
  142.9 2.9 %collective-permute-done.13.refs_5_ = bf16[2,1,2,64,1024]{4,3,2,1,0:T(8,128)(2,1)} collective-permute-done((bf16[2,1,2,64,1024]{4,3,2,1,0:T(8,128)(2,1)}, bf16[2,1,2,64,1024]{4,3,2,1,0:T(8,128)(2,1)}, u32[]{:S(2)}, u32[]{:S(2)}) %collective-permute-start.13) | collective-permute-done | bytes 524320 | tf_op jit(solution)/shard_map/ppermute | solution.py:289
  145.8 4.9 %place.3 = bf16[2,32,64,1024]{3,2,1,0:T(8,128)(2,1)} custom-call(s32[2]{0:T(128)S(1)} %pad_add_fusion.position_ref, bf16[2,3,2,64,1024]{4,3,2,1,0:T(8,128)(2,1)S(1)} %collective-permute-done.8.refs_0_, bf16[2,3,2,64,1024]{4,3,2,1,0:T(8,128)(2,1)S(1)} %collective-permute-done.9.refs_1_, ...), custom_call_target="tpu_custom_call", output_to_operand_aliasing={{}: (7, {})} | custom-call | bytes 25165824 | tf_op jit(solution)/shard_map/place/pallas_call | solution.py:295
  150.7 0.6 copy.7
  (20 shorter events, 0.4 us)
Async XLA Ops:
  0.6 7.0 %copy-start.1 = (bf16[512,512]{1,0:T(8,128)(2,1)S(1)}, bf16[512,512]{1,0:T(8,128)(2,1)}, u32[]{:S(2)}) copy-start(bf16[512,512]{1,0:T(8,128)(2,1)} %constant.29.clone.table_ref) | copy-start | bytes 1572868
  0.6 7.0 %copy-start.2 = (f32[16,256]{1,0:T(8,128)S(1)}, f32[16,256]{1,0:T(8,128)}, u32[]{:S(2)}) copy-start(f32[16,256]{1,0:T(8,128)} %constant.28.clone.taps_ref) | copy-start | bytes 49156
  1.8 11.3 %collective-permute-start.1 = (bf16[2,64,2048]{2,1,0:T(8,128)(2,1)S(1)}, bf16[2,64,2048]{2,1,0:T(8,128)(2,1)S(1)}, u32[]{:S(2)}, u32[]{:S(2)}) collective-permute-start(bf16[2,64,2048]{2,1,0:T(8,128)(2,1)S(1)} %slice.10), channel_id=1, source_target_pairs={{0,112},{16,0},{32,16},{48,32},{64,48},{80,64},{96,80},{112,96},{1... | collective-permute-start | bytes 1572872 | tf_op jit(solution)/shard_map/ppermute | solution.py:332
  6.3 6.7 %collective-permute-start = (bf16[2,64,1792]{2,1,0:T(8,128)(2,1)S(1)}, bf16[2,64,1792]{2,1,0:T(8,128)(2,1)S(1)}, u32[]{:S(2)}, u32[]{:S(2)}) collective-permute-start(bf16[2,64,1792]{2,1,0:T(8,128)(2,1)S(1)} %slice.9), channel_id=1, source_target_pairs={{0,16},{16,32},{32,48},{48,64},{64,80},{80,96},{96,112},{1,17},{17... | collective-permute-start | bytes 1376264 | tf_op jit(solution)/shard_map/ppermute | solution.py:329
  7.7 1.6 %copy-start = (bf16[2,64,8192]{2,1,0:T(8,128)(2,1)S(1)}, bf16[2,64,8192]{2,1,0:T(8,128)(2,1)}, u32[]{:S(2)}) copy-start(bf16[2,64,8192]{2,1,0:T(8,128)(2,1)} %v_ref.3) | copy-start | bytes 6291460
  55.2 20.2 %copy-start.3 = (s32[1024]{0:T(1024)S(1)}, s32[1024]{0:T(1024)}, u32[]{:S(2)}) copy-start(s32[1024]{0:T(1024)} %param.5) | copy-start | bytes 12292
  55.9 16.2 %collective-permute-start.2 = (bf16[2,256,1024]{2,1,0:T(8,128)(2,1)S(1)}, bf16[2,256,1024]{2,1,0:T(8,128)(2,1)}, u32[]{:S(2)}, u32[]{:S(2)}) collective-permute-start(bf16[2,256,1024]{2,1,0:T(8,128)(2,1)S(1)} %get-tuple-element.24.real_ref.refs_4_), channel_id=1, source_target_pairs={{0,1},{1,2},{2,3},{3,0},{4,5},{5,6},{6,7},{7,4},{8,9},{9,10},{10,1... | collective-permute-start | bytes 3145736 | tf_op jit(solution)/shard_map/ppermute | solution.py:289
  56.9 15.2 %collective-permute-start.5 = (bf16[2,256,1024]{2,1,0:T(8,128)(2,1)S(1)}, bf16[2,256,1024]{2,1,0:T(8,128)(2,1)}, u32[]{:S(2)}, u32[]{:S(2)}) collective-permute-start(bf16[2,256,1024]{2,1,0:T(8,128)(2,1)S(1)} %get-tuple-element.25.imag_ref.refs_5_), channel_id=1, source_target_pairs={{0,3},{1,0},{2,1},{3,2},{4,7},{5,4},{6,5},{7,6},{8,11},{9,8},{10,9... | collective-permute-start | bytes 3145736 | tf_op jit(solution)/shard_map/ppermute | solution.py:289
  59.2 23.8 %collective-permute-start.4 = (bf16[2,256,1024]{2,1,0:T(8,128)(2,1)S(1)}, bf16[2,256,1024]{2,1,0:T(8,128)(2,1)}, u32[]{:S(2)}, u32[]{:S(2)}) collective-permute-start(bf16[2,256,1024]{2,1,0:T(8,128)(2,1)S(1)} %get-tuple-element.24.real_ref.refs_4_), channel_id=1, source_target_pairs={{0,3},{1,0},{2,1},{3,2},{4,7},{5,4},{6,5},{7,6},{8,11},{9,8},{10,9... | collective-permute-start | bytes 3145736 | tf_op jit(solution)/shard_map/ppermute | solution.py:289
  60.7 22.6 %collective-permute-start.3 = (bf16[2,256,1024]{2,1,0:T(8,128)(2,1)S(1)}, bf16[2,256,1024]{2,1,0:T(8,128)(2,1)}, u32[]{:S(2)}, u32[]{:S(2)}) collective-permute-start(bf16[2,256,1024]{2,1,0:T(8,128)(2,1)S(1)} %get-tuple-element.25.imag_ref.refs_5_), channel_id=1, source_target_pairs={{0,1},{1,2},{2,3},{3,0},{4,5},{5,6},{6,7},{7,4},{8,9},{9,10},{10,1... | collective-permute-start | bytes 3145736 | tf_op jit(solution)/shard_map/ppermute | solution.py:289
  72.1 22.5 %collective-permute-start.6 = (bf16[2,256,1024]{2,1,0:T(8,128)(2,1)}, bf16[2,256,1024]{2,1,0:T(8,128)(2,1)}, u32[]{:S(2)}, u32[]{:S(2)}) collective-permute-start(bf16[2,256,1024]{2,1,0:T(8,128)(2,1)} %collective-permute-done.2.refs_0_), channel_id=1, source_target_pairs={{0,1},{1,2},{2,3},{3,0},{4,5},{5,6},{6,7},{7,4},{8,9},{9,10},{10,1... | collective-permute-start | bytes 3145736 | tf_op jit(solution)/shard_map/ppermute | solution.py:289
  72.1 22.5 %collective-permute-start.7 = (bf16[2,256,1024]{2,1,0:T(8,128)(2,1)}, bf16[2,256,1024]{2,1,0:T(8,128)(2,1)}, u32[]{:S(2)}, u32[]{:S(2)}) collective-permute-start(bf16[2,256,1024]{2,1,0:T(8,128)(2,1)} %collective-permute-done.5.refs_3_), channel_id=1, source_target_pairs={{0,3},{1,0},{2,1},{3,2},{4,7},{5,4},{6,5},{7,6},{8,11},{9,8},{10,9... | collective-permute-start | bytes 3145736 | tf_op jit(solution)/shard_map/ppermute | solution.py:289
  94.6 21.6 %collective-permute-start.9 = (bf16[2,3,2,64,1024]{4,3,2,1,0:T(8,128)(2,1)S(1)}, bf16[2,3,2,64,1024]{4,3,2,1,0:T(8,128)(2,1)S(1)}, u32[]{:S(2)}, u32[]{:S(2)}) collective-permute-start(bf16[2,3,2,64,1024]{4,3,2,1,0:T(8,128)(2,1)S(1)} %get-tuple-element.34), channel_id=1, source_target_pairs={{0,12},{1,13},{2,14},{3,15},{4,0},{5,1},{6,2},{7,3},{8,4},{9,5},{1... | collective-permute-start | bytes 4718600 | tf_op jit(solution)/shard_map/ppermute | solution.py:289
  96.3 49.5 %collective-permute-start.8 = (bf16[2,3,2,64,1024]{4,3,2,1,0:T(8,128)(2,1)}, bf16[2,3,2,64,1024]{4,3,2,1,0:T(8,128)(2,1)S(1)}, u32[]{:S(2)}, u32[]{:S(2)}) collective-permute-start(bf16[2,3,2,64,1024]{4,3,2,1,0:T(8,128)(2,1)} %get-tuple-element.32), channel_id=1, source_target_pairs={{0,4},{1,5},{2,6},{3,7},{4,8},{5,9},{6,10},{7,11},{8,12},{9,13},{1... | collective-permute-start | bytes 4718600 | tf_op jit(solution)/shard_map/ppermute | solution.py:289
  97.8 48.0 %collective-permute-start.10 = (bf16[2,3,2,64,1024]{4,3,2,1,0:T(8,128)(2,1)}, bf16[2,3,2,64,1024]{4,3,2,1,0:T(8,128)(2,1)}, u32[]{:S(2)}, u32[]{:S(2)}) collective-permute-start(bf16[2,3,2,64,1024]{4,3,2,1,0:T(8,128)(2,1)} %get-tuple-element.40), channel_id=1, source_target_pairs={{0,8},{1,9},{2,10},{3,11},{4,12},{5,13},{6,14},{7,15},{8,0},{9,1},... | collective-permute-start | bytes 4718600 | tf_op jit(solution)/shard_map/ppermute | solution.py:289
  103.5 39.4 %collective-permute-start.11 = (bf16[2,1,2,64,1024]{4,3,2,1,0:T(8,128)(2,1)}, bf16[2,1,2,64,1024]{4,3,2,1,0:T(8,128)(2,1)}, u32[]{:S(2)}, u32[]{:S(2)}) collective-permute-start(bf16[2,1,2,64,1024]{4,3,2,1,0:T(8,128)(2,1)} %get-tuple-element.41), channel_id=1, source_target_pairs={{0,4},{1,5},{2,6},{3,7},{4,8},{5,9},{6,10},{7,11},{8,12},{9,13},{1... | collective-permute-start | bytes 1572872 | tf_op jit(solution)/shard_map/ppermute | solution.py:289
  105.1 37.8 %collective-permute-start.12 = (bf16[2,1,2,64,1024]{4,3,2,1,0:T(8,128)(2,1)}, bf16[2,1,2,64,1024]{4,3,2,1,0:T(8,128)(2,1)}, u32[]{:S(2)}, u32[]{:S(2)}) collective-permute-start(bf16[2,1,2,64,1024]{4,3,2,1,0:T(8,128)(2,1)} %get-tuple-element.42), channel_id=1, source_target_pairs={{0,12},{1,13},{2,14},{3,15},{4,0},{5,1},{6,2},{7,3},{8,4},{9,5},{1... | collective-permute-start | bytes 1572872 | tf_op jit(solution)/shard_map/ppermute | solution.py:289
  116.2 29.6 %collective-permute-start.13 = (bf16[2,1,2,64,1024]{4,3,2,1,0:T(8,128)(2,1)}, bf16[2,1,2,64,1024]{4,3,2,1,0:T(8,128)(2,1)}, u32[]{:S(2)}, u32[]{:S(2)}) collective-permute-start(bf16[2,1,2,64,1024]{4,3,2,1,0:T(8,128)(2,1)} %get-tuple-element.43), channel_id=1, source_target_pairs={{0,8},{1,9},{2,10},{3,11},{4,12},{5,13},{6,14},{7,15},{8,0},{9,1},... | collective-permute-start | bytes 1572872 | tf_op jit(solution)/shard_map/ppermute | solution.py:289
  119.8 30.9 %all-to-all-start.1 = ((f32[16,8,128]{2,1,0:T(8,128)}), f32[16,8,128]{2,1,0:T(8,128)S(1)}, u32[]{:S(2)}, u32[]{:S(2)}) async-start(f32[16,8,128]{2,1,0:T(8,128)} %gains.1), calls=%async_computation.1 | async-start | bytes 131072 | tf_op jit(solution)/shard_map/all_to_all | solution.py:412
